TPU v7x, 1024 devices: a whole 4x4x32 slice. The times are simulated.
1024 devices in a mesh: blk: 16 (over y_hi, x, core), bal: 64 (over z, y_lo).
Axes of the slice: x: 4, y: 4 (y_hi: 2, y_lo: 2; y = y_hi * 2 + y_lo), z: 32, core: 2. Of those that a mesh axis runs over, the one named last changes fastest.
Arguments:
- patch_keys: bfloat16 [393216, 1536], P(('blk', 'bal')), may hold values from -128 to 128
- patch_values: bfloat16 [393216, 1536], P(('blk', 'bal')), may hold values from -6 to 6
- lengths: int32 [1024, 3], P(('blk', 'bal')), may hold values from 1 to 256, 384 in all within a row
- probe_query: bfloat16 [1536], replicated, may hold values from -3 to 3
- projection: bfloat16 [1536, 1152], replicated, may hold values from -0.15625 to 0.15625
- text_embeds: bfloat16 [3072, 1152], P(('blk', 'bal')), may hold values from -2 to 2
- pair_group: int32 [3072], replicated, may hold values from 0 to 3071
- logit_scale: float32 [1], replicated, may hold values from 10 to 30
- logit_bias: float32 [1], replicated, may hold values from -2 to 0
Outputs:
- pooled_grad: float32 [3072, 1536], P(('blk', 'bal'))
- text_grad: float32 [3072, 1152], P(('blk', 'bal'))
Inputs may be any that keep to these rules, and one draw needn't show every extreme that they name: `lengths`: the 3 counts of a device fill its 384 rows; some image has 256 patches. `pair_group`: pairs with equal groups are positive.
All inputs are finite; a program needn't handle non-finite values.
Results may differ from a plain program's by a relative error of at most 0.0065.
Values may be sent and summed in bfloat16 or wider, within the bound.
No kernel may reach another device: no remote copies, remote signals or barrier semaphores. Data moves between devices by JAX's collectives and lax.ppermute only.
A program may use at most 32 MiB of HBM per device.

v0:
```python
import math

import jax
import jax.numpy as jnp
from jax import lax
from jax.sharding import PartitionSpec as P

H = 16
HD = 96


epsilon = 1e-06


def pool_device(key_rows, value_rows, img_lengths, probe_query):
    total_rows = key_rows.shape[0]
    scores = jnp.einsum(
        "rhc,hc->rh",
        key_rows.reshape(total_rows, H, HD),
        probe_query.reshape(H, HD),
        preferred_element_type=jnp.float32,
    ) / math.sqrt(HD)
    ending = jnp.cumsum(img_lengths)
    starts = ending - img_lengths
    row_index = jnp.arange(total_rows, dtype=jnp.int32)
    member = (row_index[None, :] >= starts[:, None]) & (row_index[None, :] < ending[:, None])
    masked = jnp.where(member[:, :, None], scores[None, :, :], -jnp.inf)
    peak_score = jnp.max(masked, axis=1, keepdims=True)
    exp_terms = jnp.where(member[:, :, None], jnp.exp(masked - peak_score), 0.0)
    weights = (exp_terms / jnp.sum(exp_terms, axis=1, keepdims=True)).astype(jnp.bfloat16)
    pooled = jnp.einsum(
        "krh,rhc->khc",
        weights,
        value_rows.reshape(total_rows, H, HD),
        preferred_element_type=jnp.float32,
    )
    return pooled.reshape(img_lengths.shape[0], H * HD).astype(jnp.bfloat16)


def tile_grads(all_img, all_txt, img_ids, txt_ids, logit_mult, shift_val):
    logits = (
        jnp.einsum("ie,te->it", all_img, all_txt, preferred_element_type=jnp.float32) * logit_mult
        + shift_val
    )
    labels = jnp.where(img_ids[:, None] == txt_ids[None, :], jnp.float32(1.0), jnp.float32(-1.0))
    coeffs = (-labels * jax.nn.sigmoid(-labels * logits) * logit_mult).astype(jnp.bfloat16)
    img_part = jnp.einsum("it,te->ie", coeffs, all_txt, preferred_element_type=jnp.float32)
    txt_part = jnp.einsum("it,ie->te", coeffs, all_img, preferred_element_type=jnp.float32)
    return (img_part, txt_part)


def shards(
    patch_keys,
    patch_values,
    lengths,
    probe_query,
    projection,
    text_embeds,
    pair_group,
    logit_scale,
    logit_bias,
):
    pooled = pool_device(patch_keys, patch_values, lengths[0], probe_query)
    projected = jnp.dot(pooled, projection, preferred_element_type=jnp.float32)
    proj_norm = jnp.sqrt(jnp.sum(projected * projected, axis=1, keepdims=True) + epsilon)
    img_unit = (projected / proj_norm).astype(jnp.bfloat16)
    text_wide = text_embeds.astype(jnp.float32)
    text_norm = jnp.sqrt(jnp.sum(text_wide * text_wide, axis=1, keepdims=True) + epsilon)
    txt_unit = (text_wide / text_norm).astype(jnp.bfloat16)
    logit_mult = logit_scale[0]
    shift_val = logit_bias[0]
    blk_pos = lax.axis_index("blk")
    bal_pos = lax.axis_index("bal")
    blk_count = lax.axis_size("blk")
    bal_count = lax.axis_size("bal")
    img_count = img_unit.shape[0]
    row_ids = lax.dynamic_slice_in_dim(
        pair_group, blk_pos * bal_count * img_count, bal_count * img_count
    )
    grid_ids = pair_group.reshape(blk_count, bal_count, img_count)
    column_ids = lax.dynamic_index_in_dim(grid_ids, bal_pos, 1, keepdims=False).reshape(-1)
    all_img = lax.all_gather(img_unit, "bal", axis=0, tiled=True)
    all_txt = lax.all_gather(txt_unit, "blk", axis=0, tiled=True)
    img_part, txt_part = tile_grads(all_img, all_txt, row_ids, column_ids, logit_mult, shift_val)
    d_img = lax.psum_scatter(img_part, "bal", scatter_dimension=0, tiled=True)
    d_txt = lax.psum_scatter(txt_part, "blk", scatter_dimension=0, tiled=True)
    proj_dir = projected / proj_norm
    d_proj = (
        (d_img - jnp.sum(d_img * proj_dir, axis=1, keepdims=True) * proj_dir) / proj_norm
    ).astype(jnp.bfloat16)
    pooled_grad = jnp.dot(d_proj, projection.T, preferred_element_type=jnp.float32)
    text_dir = text_wide / text_norm
    text_grad = (d_txt - jnp.sum(d_txt * text_dir, axis=1, keepdims=True) * text_dir) / text_norm
    return (pooled_grad, text_grad)


def solution(mesh):
    in_specs = (
        P(("blk", "bal"), None),
        P(("blk", "bal"), None),
        P(("blk", "bal"), None),
        P(),
        P(),
        P(("blk", "bal"), None),
        P(),
        P(),
        P(),
    )
    out_specs = (P(("blk", "bal"), None), P(("blk", "bal"), None))
    return jax.shard_map(shards, mesh=mesh, in_specs=in_specs, out_specs=out_specs, check_vma=False)
```

profile of v0, /device:TPU:2, one launch (start us, length us, event | category | flops | bytes accessed | tf_op | source)
XLA Modules:
  0.0 898.2 jit_solution(15750972849094624281)
XLA Ops:
  7.2 0.0 copy-start
  7.2 0.0 all-reduce.7.cloned.1.call-start
  8.9 0.8 reduce-window.7
  9.7 0.0 copy-start.7
  9.7 1.2 bitcast_subtract_fusion
  10.9 1.8 reshape.108
  12.7 1.3 dynamic_slice.7
  14.1 0.8 fusion.20
  14.9 0.0 copy-done.7
  14.9 0.0 copy-start.4
  14.9 0.8 reshape.122
  15.7 0.8 convert_bitcast_fusion
  16.5 33.9 %all-gather.1 = bf16[16,3,1152]{2,1,0:T(4,128)(2,1)} all-gather(bf16[1,3,1152]{2,1,0:T(4,128)(2,1)S(1)} %convert_bitcast_fusion), channel_id=1, replica_groups=mesh['blk'=16,'bal'=64] {'blk'}, dimensions={0}, use_global_device_ids=true | all-gather | bytes 117504 | tf_op jit(solution)/shard_map/all_gather | solution.py:83
  50.4 1.6 reshape.118
  52.0 0.0 copy-done.4
  52.0 0.9 dynamic-slice_reduce_fusion
  52.9 0.6 eq.16
  53.5 2.4 copy.15
  55.9 1.6 fusion.37
  57.4 0.6 fusion.19
  58.1 0.0 copy-start.8
  58.1 0.0 copy-start.9
  58.1 2.4 copy.16
  60.5 0.0 copy-done.8
  60.5 0.0 copy-done.9
  60.5 0.1 fusion.30
  60.5 1.0 fusion.36
  61.6 2.5 fusion.13
  64.1 0.7 copy.17
  64.8 0.7 convert_element_type.30
  65.5 0.0 copy-done
  65.5 1.4 multiply_reduce_fusion.2
  66.9 0.0 copy-start.1
  66.9 0.0 copy-start.5
  66.9 0.0 copy-start.6
  67.0 0.6 copy-done.1
  67.5 0.1 convert_bitcast_fusion.1
  67.6 134.3 %all-gather = bf16[64,3,1152]{2,1,0:T(4,128)(2,1)} all-gather(bf16[1,3,1152]{2,1,0:T(4,128)(2,1)S(1)} %convert_bitcast_fusion.1), channel_id=1, replica_groups=mesh['blk'=16,'bal'=64] {'bal'}, dimensions={0}, use_global_device_ids=true | all-gather | bytes 449280 | tf_op jit(solution)/shard_map/all_gather | solution.py:82
  201.9 2.1 reshape.116
  204.0 0.0 copy-done.5
  204.0 0.0 copy-done.6
  204.0 1.3 fusion.12
  205.3 0.0 copy-start.3
  205.3 0.6 copy-done.3
  205.9 1.9 fusion.39
  207.9 0.0 copy-start.2
  207.9 0.0 all-reduce.7.cloned.1.call-update
  207.9 0.0 all-reduce.5.cloned.1.call-start
  207.9 2.2 fusion.38
  210.1 0.0 all-reduce.5.cloned.1.call-update
  210.1 1.3 dynamic-slice.2
  211.4 1.3 dynamic-slice
  214.0 155.2 %all-reduce.7.cloned.1.call-done = f32[48,1152]{1,0:T(8,128)} async-done(((f32[48,1152]{1,0:T(8,128)}), f32[48,1152]{1,0:T(8,128)}) %all-reduce.7.cloned.1.call-update) | async-done | bytes 221200
  369.1 0.0 copy-done.2
  369.1 1.1 multiply_reduce_fusion
  370.2 1.6 subtract_divide_fusion
  371.8 516.0 %all-reduce.5.cloned.1.call-done = f32[192,1152]{1,0:T(8,128)} async-done(((f32[192,1152]{1,0:T(8,128)}), f32[192,1152]{1,0:T(8,128)}) %all-reduce.5.cloned.1.call-update) | async-done | bytes 884752
  887.8 1.1 multiply_reduce_fusion.1
  888.8 2.5 fusion.22
  (2 shorter events, 0.0 us)
Async XLA Ops:
  7.2 58.4 %copy-start = (bf16[1536,1152]{1,0:T(8,128)(2,1)S(1)}, bf16[1536,1152]{1,0:T(8,128)(2,1)}, u32[]{:S(2)}) copy-start(bf16[1536,1152]{1,0:T(8,128)(2,1)} %param.13) | copy-start | bytes 10616836
  7.2 362.0 %all-reduce.7.cloned.1.call-start = ((), (), s32[]{:S(2)}) async-start(), calls=%async_computation.1 | async-start | bytes 442368
  9.7 5.2 copy-start.7
  14.9 37.1 %copy-start.4 = (f32[3]{0:T(128)}, f32[3]{0:T(128)S(1)}, u32[]{:S(2)}) copy-start(f32[3]{0:T(128)S(1)} %add_sqrt_fusion) | copy-start | bytes 40
  58.1 2.4 copy-start.8
  58.1 2.4 copy-start.9
  66.9 0.6 copy-start.1
  66.9 137.1 %copy-start.5 = (s32[192]{0:T(256)S(1)}, s32[192]{0:T(256)}, u32[]{:S(2)}) copy-start(s32[192]{0:T(256)} %dynamic_slice.7) | copy-start | bytes 2308
  66.9 137.1 %copy-start.6 = (s32[48]{0:T(128)S(1)}, s32[48]{0:T(128)}, u32[]{:S(2)}) copy-start(s32[48]{0:T(128)} %eq.16) | copy-start | bytes 580
  205.3 0.6 copy-start.3
  207.9 161.3 %copy-start.2 = (bf16[3,1152]{1,0:T(4,128)(2,1)S(1)}, bf16[3,1152]{1,0:T(4,128)(2,1)}, u32[]{:S(2)}) copy-start(bf16[3,1152]{1,0:T(4,128)(2,1)} %param.14) | copy-start | bytes 20740
  207.9 679.9 %all-reduce.5.cloned.1.call-start = ((), (), s32[]{:S(2)}) async-start(), calls=%async_computation | async-start | bytes 1769472
Sparse Core Ops, SparseCore 0:
  208.0 161.0 all-reduce.6
  373.0 514.6 all-reduce.4
where the time goes:
time: 899 us; the launch traced here: 898 us
  waiting for transfers between devices  671 us (75%)
  blocking collectives  168 us (19%)
  local copies, waits for them, and re-layouts  19.1 us (2%)
  between operations  17.1 us (2%)
  matrix products  13.4 us (1%)
  other arithmetic  9.19 us (1%)
    unnamed x4, waiting for transfers between devices  671 us
    all_gather x1, blocking collectives, shards(): all_img = lax.all_gather(img_unit, 'bal', axis=0, tiled=True)  134 us
    all_gather x1, blocking collectives, shards(): all_txt = lax.all_gather(txt_unit, 'blk', axis=0, tiled=True)  33.9 us
  transfers between devices with their start and end apart: 2, of which 2 were waited for; matrix products, arithmetic and copies ran while one was open for 1% of the time, Pallas kernels for 0%

commit v1 on v0

v1 whole, which is shorter than its diff:
```python
import math

import jax
import jax.numpy as jnp
from jax import lax
from jax.sharding import Mesh, PartitionSpec as P

H = 16
HD = 96

AXES = ("y_hi", "x", "core", "z", "y_lo")
SIZES = (2, 4, 2, 32, 2)
PLANE = ("core", "y_hi", "y_lo", "x")
AXES_PLANE = ("y_hi", "x", "core", "y_lo")

epsilon = 1e-06


def pool_device(key_rows, value_rows, img_lengths, probe_query):
    total_rows = key_rows.shape[0]
    scores = jnp.einsum(
        "rhc,hc->rh",
        key_rows.reshape(total_rows, H, HD),
        probe_query.reshape(H, HD),
        preferred_element_type=jnp.float32,
    ) / math.sqrt(HD)
    ending = jnp.cumsum(img_lengths)
    starts = ending - img_lengths
    row_index = jnp.arange(total_rows, dtype=jnp.int32)
    member = (row_index[None, :] >= starts[:, None]) & (row_index[None, :] < ending[:, None])
    masked = jnp.where(member[:, :, None], scores[None, :, :], -jnp.inf)
    peak_score = jnp.max(masked, axis=1, keepdims=True)
    exp_terms = jnp.where(member[:, :, None], jnp.exp(masked - peak_score), 0.0)
    weights = (exp_terms / jnp.sum(exp_terms, axis=1, keepdims=True)).astype(jnp.bfloat16)
    pooled = jnp.einsum(
        "krh,rhc->khc",
        weights,
        value_rows.reshape(total_rows, H, HD),
        preferred_element_type=jnp.float32,
    )
    return pooled.reshape(img_lengths.shape[0], H * HD).astype(jnp.bfloat16)


def shards(
    patch_keys,
    patch_values,
    lengths,
    probe_query,
    projection,
    text_embeds,
    pair_group,
    logit_scale,
    logit_bias,
):
    count, width = text_embeds.shape
    sizes = tuple(lax.axis_size(axis) for axis in AXES)
    n_z = lax.axis_size("z")
    n_plane = lax.axis_size(PLANE)
    lanes = 128
    packed = (2 * count * width // lanes, lanes)
    text_wide = text_embeds.astype(jnp.float32)
    text_norm = jnp.sqrt(jnp.sum(text_wide * text_wide, axis=1, keepdims=True) + epsilon)
    txt_unit = (text_wide / text_norm).astype(jnp.bfloat16)

    pooled = pool_device(patch_keys, patch_values, lengths[0], probe_query)
    projected = jnp.dot(pooled, projection, preferred_element_type=jnp.float32)
    proj_norm = jnp.sqrt(jnp.sum(projected * projected, axis=1, keepdims=True) + epsilon)
    img_unit = (projected / proj_norm).astype(jnp.bfloat16)

    block = jnp.concatenate([img_unit, txt_unit]).reshape(packed)
    line = lax.all_to_all(jnp.broadcast_to(block, (n_z,) + packed), "z", 0, 0, tiled=True)
    plane = block[None]
    for axis in PLANE[::-1]:
        plane = lax.all_gather(plane, axis, axis=0, tiled=True)
    line = line.reshape(-1, width)
    plane = plane.reshape(-1, width)

    place = dict((axis, lax.axis_index(axis)) for axis in AXES)
    ids = pair_group.reshape(sizes + (count,))
    at_z = lax.dynamic_index_in_dim(ids, place["z"], 3, keepdims=False)
    plane_ids = jnp.transpose(at_z, [AXES_PLANE.index(axis) for axis in PLANE] + [4]).reshape(n_plane, 1, count)
    line_ids = lax.dynamic_slice(
        ids,
        [0 if axis == "z" else place[axis] for axis in AXES] + [0],
        [n_z if axis == "z" else 1 for axis in AXES] + [count],
    ).reshape(n_z, 1, count)
    plane_ids = jnp.broadcast_to(plane_ids, (n_plane, 2, count)).reshape(-1)
    line_ids = jnp.broadcast_to(line_ids, (n_z, 2, count)).reshape(-1)
    plane_kind = jnp.arange(n_plane * 2 * count, dtype=jnp.int32) // count % 2
    line_kind = jnp.arange(n_z * 2 * count, dtype=jnp.int32) // count % 2

    logits = (
        jnp.einsum("pe,le->pl", plane, line, preferred_element_type=jnp.float32) * logit_scale[0]
        + logit_bias[0]
    )
    labels = jnp.where(plane_ids[:, None] == line_ids[None, :], jnp.float32(1.0), jnp.float32(-1.0))
    coeffs = -labels * jax.nn.sigmoid(-labels * logits) * logit_scale[0]
    coeffs = jnp.where(plane_kind[:, None] != line_kind[None, :], coeffs, 0.0).astype(jnp.bfloat16)
    parts = jnp.einsum("pl,le->pe", coeffs, line, preferred_element_type=jnp.float32)
    parts = parts.astype(jnp.bfloat16).reshape((n_plane,) + packed)
    parts = lax.all_to_all(parts, PLANE, 0, 0, tiled=True)
    d_units = jnp.sum(parts.astype(jnp.float32), axis=0).reshape(2 * count, width)
    d_img, d_txt = d_units[:count], d_units[count:]

    proj_dir = projected / proj_norm
    d_proj = (
        (d_img - jnp.sum(d_img * proj_dir, axis=1, keepdims=True) * proj_dir) / proj_norm
    ).astype(jnp.bfloat16)
    pooled_grad = jnp.dot(d_proj, projection.T, preferred_element_type=jnp.float32)
    text_dir = text_wide / text_norm
    text_grad = (d_txt - jnp.sum(d_txt * text_dir, axis=1, keepdims=True) * text_dir) / text_norm
    return (pooled_grad, text_grad)


def solution(mesh):
    fine = Mesh(mesh.devices.reshape(SIZES), AXES)
    rows = P(AXES, None)
    in_specs = (rows, rows, rows, P(), P(), rows, P(), P(), P())
    return jax.shard_map(
        shards, mesh=fine, in_specs=in_specs, out_specs=(rows, rows), check_vma=False
    )
```

time: 899 us -> 148 us (0.16)
  the two profiles are of different devices: /device:TPU:2 before, /device:TPU:1 now
where the time goes in v1:
time: 148 us; the launch traced here: 146 us
  blocking collectives  46.5 us (31%)
  local copies, waits for them, and re-layouts  32.2 us (22%)
  starting transfers between devices  29.4 us (20%)
  waiting for transfers between devices  15.5 us (10%)
  matrix products  10.8 us (7%)
  other arithmetic  9.43 us (6%)
  between operations  2.02 us (1%)
    all_to_all x1, starting transfers between devices, shards(): lax.all_to_all(jnp.broadcast_to(block, (n_z,) + packed), 'z', 0, 0, tiled...  29.4 us
    all_gather x4, blocking collectives, shards(): plane = lax.all_gather(plane, axis, axis=0, tiled=True)  26.9 us
    all_to_all x1, blocking collectives, shards(): parts = lax.all_to_all(parts, PLANE, 0, 0, tiled=True)  19.6 us
    all_to_all x1, waiting for transfers between devices, shards(): lax.all_to_all(jnp.broadcast_to(block, (n_z,) + packed), 'z', 0, 0, tiled...  15.5 us
    unnamed x12, local copies, waits for them, and re-layouts  5.34 us
    slice x3, local copies, waits for them, and re-layouts, shards(): d_img, d_txt = (d_units[:count], d_units[count:])  3.28 us
    eq x2, local copies, waits for them, and re-layouts, shards(): plane_ids[:, None] == line_ids[None, :]  2.98 us
  transfers between devices with their start and end apart: 1, of which 1 were waited for; matrix products, arithmetic and copies ran while one was open for 10% of the time, Pallas kernels for 0%

profile of v1, /device:TPU:1, one launch (start us, length us, event | category | flops | bytes accessed | tf_op | source)
XLA Modules:
  0.0 145.8 jit_solution(16221042836385014028)
XLA Ops:
  0.6 0.0 copy-start
  0.6 1.0 reduce-window.7
  1.6 1.3 bitcast_subtract_fusion
  2.9 0.8 fusion.34
  3.7 0.8 reshape.188
  4.5 2.4 %copy.29 = bf16[384,1536]{0,1:T(8,128)(2,1)} copy(bf16[384,1536]{1,0:T(8,128)(2,1)} %param.9) | data formatting | bytes 2359296 | tf_op args[0]
  6.9 1.6 %fusion.57 = f32[16,1,384]{2,1,0:T(1,128)S(1)} fusion(bf16[16,96,1]{1,2,0:T(2,128)(2,1)S(1)} %reshape.188, bf16[384,16,96]{0,2,1:T(8,128)(2,1)} %bitcast.34), kind=kOutput, calls=%fused_computation.81 | convolution fusion | flops 1179648 | bytes 1207296 | tf_op jit(solution)/shard_map/rhc,hc->rh/dot_general | solution.py:21
  8.4 0.6 fusion.33
  9.1 0.0 copy-start.4
  9.1 2.4 %copy.30 = bf16[384,1536]{0,1:T(8,128)(2,1)} copy(bf16[384,1536]{1,0:T(8,128)(2,1)} %param.10) | data formatting | bytes 2359296 | tf_op args[1]
  11.4 0.0 copy-done.4
  11.4 0.1 fusion.44
  11.5 1.0 fusion.56
  12.6 2.5 %fusion.14 = bf16[3,16,96]{2,0,1:T(4,128)(2,1)} fusion(bf16[384,16,96]{0,2,1:T(8,128)(2,1)} %bitcast.35, f32[3,16]{0,1:T(8,128)S(1)} %fusion.56, f32[384,16]{0,1:T(8,128)} %fusion.33, pred[3,384]{1,0:T(4,128)(4,1)S(1)} %fusion.44), kind=kOutput, calls=%fused_computation.17 | convolution fusion | flops 3636143 | bytes 1214784 | tf_op jit(solution)/shard_map/krh,rhc->khc/dot_general | solution.py:35
  15.1 0.7 copy.31
  15.8 0.7 convert_element_type.36
  16.5 0.0 copy-done
  16.5 0.0 copy-start.2
  16.5 1.4 multiply_reduce_fusion.2
  17.9 0.0 copy-start.1
  17.9 0.0 copy-start.3
  17.9 0.6 copy-done.1
  18.5 0.0 copy-done.2
  18.5 0.1 fusion.53
  18.6 0.0 copy-done.3
  18.6 0.6 pad_maximum_fusion
  19.2 1.4 reshape.182
  20.6 1.5 %broadcast_in_dim.84 = bf16[32,54,128]{2,1,0:T(8,128)(2,1)} broadcast(bf16[54,128]{1,0:T(8,128)(2,1)} %reshape.182), dimensions={1,2} | broadcast | bytes 456192 | tf_op jit(solution)/shard_map/broadcast_in_dim | solution.py:71
  22.1 29.4 %all-to-all-start = ((bf16[32,54,128]{2,1,0:T(8,128)(2,1)}), bf16[32,54,128]{2,1,0:T(8,128)(2,1)}, u32[]{:S(2)}, u32[]{:S(2)}) async-start(bf16[32,54,128]{2,1,0:T(8,128)(2,1)} %broadcast_in_dim.84), calls=%async_computation | async-start | bytes 917504 | tf_op jit(solution)/shard_map/all_to_all | solution.py:71
  51.5 1.4 broadcast_in_dim_reshape.2
  54.2 2.3 %reshape.174 = s32[2,4,2,32,2,3]{5,4,3,2,1,0:T(2,128)} reshape(s32[3072]{0:T(1024)} %param.15) | data formatting | bytes 24576 | tf_op jit(solution)/shard_map/reshape | solution.py:79
  56.5 0.7 dynamic-slice_bitcast_fusion
  57.2 0.6 copy.37
  57.8 0.8 constant_dynamic-slice_fusion
  58.6 0.6 broadcast_in_dim.77
  59.2 1.5 %eq.22 = s32[192]{0:T(256)} reshape(s32[32,2,3]{2,1,0:T(2,128)} %broadcast_in_dim.77) | data formatting | bytes 1536 | tf_op jit(solution)/shard_map/eq | solution.py:96
  60.7 1.3 broadcast_in_dim.75
  62.0 1.5 %eq.20 = s32[192]{0:T(256)} reshape(s32[32,2,3]{2,1,0:T(2,128)} %broadcast_in_dim.75) | data formatting | bytes 1536 | tf_op jit(solution)/shard_map/eq | solution.py:96
  63.5 10.8 %all_gather.12 = bf16[4,54,128]{2,1,0:T(8,128)(2,1)S(1)} all-gather(bf16[1,54,128]{2,1,0:T(8,128)(2,1)} %broadcast_in_dim_reshape.2), channel_id=1, replica_groups=mesh['y_hi'=2,'x'=4,'core'=2,'z'=32,'y_lo'=2] {'x'}, dimensions={0}, use_global_device_ids=true | all-gather | bytes 69120 | tf_op jit(solution)/shard_map/all_gather | solution.py:74
  74.3 4.1 %all_gather.13 = bf16[8,54,128]{2,1,0:T(8,128)(2,1)S(1)} all-gather(bf16[4,54,128]{2,1,0:T(8,128)(2,1)S(1)} %all_gather.12), channel_id=1, replica_groups=mesh['y_hi'=2,'x'=4,'core'=2,'z'=32,'y_lo'=2] {'y_lo'}, dimensions={0}, use_global_device_ids=true | all-gather | bytes 165888 | tf_op jit(solution)/shard_map/all_gather | solution.py:74
  78.4 6.7 %all_gather.14 = bf16[16,54,128]{2,0,1:T(8,128)(2,1)S(1)} all-gather(bf16[8,54,128]{2,0,1:T(8,128)(2,1)S(1)} %copy.32), channel_id=1, replica_groups=mesh['y_hi'=2,'x'=4,'core'=2,'z'=32,'y_lo'=2] {'y_hi'}, dimensions={0}, use_global_device_ids=true | all-gather | bytes 331776 | tf_op jit(solution)/shard_map/all_gather | solution.py:74
  85.1 5.3 %all_gather.15 = bf16[32,54,128]{2,0,1:T(8,128)(2,1)S(1)} all-gather(bf16[16,54,128]{2,0,1:T(8,128)(2,1)S(1)} %all_gather.14), channel_id=1, replica_groups=mesh['y_hi'=2,'x'=4,'core'=2,'z'=32,'y_lo'=2] {'core'}, dimensions={0}, use_global_device_ids=true | all-gather | bytes 663552 | tf_op jit(solution)/shard_map/all_gather | solution.py:74
  90.5 0.9 copy.33
  91.4 2.3 %reshape.181 = bf16[192,1152]{1,0:T(8,128)(2,1)} reshape(bf16[32,54,128]{2,1,0:T(8,128)(2,1)} %copy.33) | data formatting | bytes 884736 | tf_op jit(solution)/shard_map/reshape | solution.py:76
  93.7 0.6 and_select_fusion
  94.3 15.5 %all-to-all-done = bf16[32,54,128]{2,1,0:T(8,128)(2,1)} async-done(((bf16[32,54,128]{2,1,0:T(8,128)(2,1)}), bf16[32,54,128]{2,1,0:T(8,128)(2,1)}, u32[]{:S(2)}, u32[]{:S(2)}) %all-to-all-start) | async-done | bytes 442400 | tf_op jit(solution)/shard_map/all_to_all | solution.py:71
  109.8 2.3 %reshape.183 = bf16[192,1152]{1,0:T(8,128)(2,1)} reshape(bf16[32,54,128]{2,1,0:T(8,128)(2,1)} %all-to-all-done) | data formatting | bytes 884736 | tf_op jit(solution)/shard_map/reshape | solution.py:75
  112.1 2.9 %convolution_convert_fusion = bf16[192,1152]{1,0:T(8,128)(2,1)} fusion(bf16[192,1152]{1,0:T(8,128)(2,1)} %reshape.183, bf16[192,1152]{1,0:T(8,128)(2,1)} %reshape.181, f32[]{:T(128)} %bitcast.33, f32[]{:T(128)} %bitcast.32, s32[192]{0:T(256)} %eq.22, s32[192]{0:T(256)} %and_select_fusion, s32[192]{0:T(256)} %eq.20), kind=kOutput, calls=%fused_computation.1 | convolution fusion | flops 170606592 | bytes 1329416 | tf_op jit(solution)/shard_map/pl,le->pe/dot_general | solution.py:99
  115.0 2.3 %reshape.184 = bf16[32,54,128]{2,1,0:T(8,128)(2,1)} reshape(bf16[192,1152]{1,0:T(8,128)(2,1)} %convolution_convert_fusion) | data formatting | bytes 884736 | tf_op jit(solution)/shard_map/reshape | solution.py:100
  117.2 19.6 %all_to_all.10 = bf16[32,54,128]{2,1,0:T(8,128)(2,1)S(1)} all-to-all(bf16[32,54,128]{2,1,0:T(8,128)(2,1)} %reshape.184), channel_id=1, replica_groups=mesh['y_hi'=2,'x'=4,'core'=2,'z'=32,'y_lo'=2] {'core','y_hi','y_lo','x'}, dimensions={0} | all-to-all | bytes 884736 | tf_op jit(solution)/shard_map/all_to_all | solution.py:101
  136.8 0.1 convert_reduce_fusion
  136.9 0.6 fusion.55
  137.5 1.3 slice.15
  138.9 0.9 multiply_reduce_fusion
  139.8 1.4 subtract_divide_fusion
  141.2 1.3 slice.13
  142.5 0.9 multiply_reduce_fusion.1
  143.4 2.4 %fusion.36 = f32[3,1536]{1,0:T(4,128)} fusion(bf16[1536,1152]{1,0:T(8,128)(2,1)S(1)} %copy-done, f32[3,1152]{1,0:T(4,128)} %slice.13, f32[3]{0:T(128)S(1)} %multiply_reduce_fusion.1, f32[3]{0:T(128)} %copy-done.3, f32[3,1152]{1,0:T(4,128)} %copy-done.1), kind=kOutput, calls=%fused_computation.52 | convolution fusion | flops 10634112 | bytes 3585048 | tf_op jit(solution)/shard_map/dot_general | solution.py:109
  (3 shorter events, 0.0 us)
Async XLA Ops:
  0.6 15.9 %copy-start = (bf16[1536,1152]{1,0:T(8,128)(2,1)S(1)}, bf16[1536,1152]{1,0:T(8,128)(2,1)}, u32[]{:S(2)}) copy-start(bf16[1536,1152]{1,0:T(8,128)(2,1)} %param.13) | copy-start | bytes 10616836
  9.1 2.4 %copy-start.4 = (s32[3]{0:T(128)S(1)}, s32[3]{0:T(128)}, u32[]{:S(2)}) copy-start(s32[3]{0:T(128)} %bitcast_subtract_fusion) | copy-start | bytes 40
  16.5 2.0 %copy-start.2 = (bf16[3,1152]{1,0:T(4,128)(2,1)S(1)}, bf16[3,1152]{1,0:T(4,128)(2,1)}, u32[]{:S(2)}) copy-start(bf16[3,1152]{1,0:T(4,128)(2,1)} %param.14) | copy-start | bytes 20740
  17.9 0.6 copy-start.1
  17.9 0.7 copy-start.3
  22.1 87.6 %all-to-all-start = ((bf16[32,54,128]{2,1,0:T(8,128)(2,1)}), bf16[32,54,128]{2,1,0:T(8,128)(2,1)}, u32[]{:S(2)}, u32[]{:S(2)}) async-start(bf16[32,54,128]{2,1,0:T(8,128)(2,1)} %broadcast_in_dim.84), calls=%async_computation | async-start | bytes 917504 | tf_op jit(solution)/shard_map/all_to_all | solution.py:71

commit v2 on v1

v2 whole, which is shorter than its diff:
```python
import math

import jax
import jax.numpy as jnp
from jax import lax
from jax.experimental import pallas as pl
from jax.experimental.pallas import tpu as pltpu
from jax.sharding import Mesh, PartitionSpec as P

H = 16
HD = 96

AXES = ("y_hi", "x", "core", "z", "y_lo")
SIZES = (2, 4, 2, 32, 2)
PLANE = ("y_hi", "x", "core", "y_lo")

BLOCK = 8
HALF = 4

epsilon = 1e-06
VMEM = pl.BlockSpec(memory_space=pltpu.VMEM)
SMEM = pl.BlockSpec(memory_space=pltpu.SMEM)
PARAMS = pltpu.CompilerParams(vmem_limit_bytes=24 << 20)


def row_norm(rows):
    return jnp.sqrt(jnp.sum(rows * rows, axis=1, keepdims=True) + epsilon)


def units_kernel(
    lengths, keys, values, probe, projection, text, block, projected, pooled, units
):
    n_rows, width = keys.shape
    head = lax.broadcasted_iota(jnp.int32, (H, width), 0)
    own = lax.broadcasted_iota(jnp.int32, (H, width), 1) // HD == head
    query = jnp.where(own, probe[...].astype(jnp.float32), 0.0).astype(jnp.bfloat16)
    scores = lax.dot_general(
        query, keys[...], (((1,), (1,)), ((), ())), preferred_element_type=jnp.float32
    ) / math.sqrt(HD)
    row = lax.broadcasted_iota(jnp.int32, (H, n_rows), 1)
    start = jnp.int32(0)
    weights = []
    for image in range(lengths.shape[1]):
        end = start + lengths[0, image]
        member = (row >= start) & (row < end)
        masked = jnp.where(member, scores, -jnp.inf)
        terms = jnp.exp(masked - jnp.max(masked, axis=1, keepdims=True))
        weights.append((terms / jnp.sum(terms, axis=1, keepdims=True)).astype(jnp.bfloat16))
        start = end
    mixed = jnp.dot(
        jnp.concatenate(weights), values[...], preferred_element_type=jnp.float32
    )
    pooled[...] = jnp.zeros_like(pooled)
    for image in range(lengths.shape[1]):
        part = mixed[image * H : (image + 1) * H]
        pooled[image : image + 1, :] = jnp.sum(jnp.where(own, part, 0.0), axis=0, keepdims=True)
    proj = jnp.dot(
        pooled[...].astype(jnp.bfloat16), projection[...], preferred_element_type=jnp.float32
    )[:BLOCK]
    projected[...] = proj
    units[...] = proj / row_norm(proj)
    text_wide = text[...].astype(jnp.float32)
    count = text.shape[0]
    units[HALF : HALF + count, :] = text_wide / row_norm(text_wide)
    filled = lax.broadcasted_iota(jnp.int32, units.shape, 0) % HALF < count
    block[...] = jnp.where(filled, units[...], 0.0).astype(jnp.bfloat16)


def pick(groups, positions, axis):
    n_rows, lanes = groups.shape
    n = positions.shape[axis]
    high, low = groups // 64, groups % 64
    pieces = []
    for digit in (high, low):
        digit = digit.astype(jnp.float32).astype(jnp.bfloat16)
        if axis == 0:
            lane = lax.broadcasted_iota(jnp.int32, (n, lanes), 1)
            hot = jnp.where(lane == positions % lanes, 1.0, 0.0).astype(jnp.bfloat16)
            found = lax.dot_general(
                hot, digit, (((1,), (1,)), ((), ())), preferred_element_type=jnp.float32
            )
            line = lax.broadcasted_iota(jnp.int32, (n, n_rows), 1)
        else:
            lane = lax.broadcasted_iota(jnp.int32, (lanes, n), 0)
            hot = jnp.where(lane == positions % lanes, 1.0, 0.0).astype(jnp.bfloat16)
            found = jnp.dot(digit, hot, preferred_element_type=jnp.float32)
            line = lax.broadcasted_iota(jnp.int32, (n_rows, n), 0)
        kept = jnp.where(line == positions // lanes, found, 0.0)
        pieces.append(jnp.sum(kept, axis=1 - axis, keepdims=True))
    return pieces[0] * 64.0 + pieces[1]


def tile_kernel(count, plane, line, groups, scale, bias, parts):
    n_x, n_core, n_z, n_y = (lax.axis_size(axis) for axis in ("x", "core", "z", "y_lo"))
    blk = (lax.axis_index("y_hi") * n_x + lax.axis_index("x")) * n_core + lax.axis_index("core")
    per_blk = n_z * n_y * count
    at = lax.broadcasted_iota(jnp.int32, (plane.shape[0], 1), 0)
    member, slot = at // BLOCK, jnp.minimum(at % HALF, count - 1)
    plane_at = (
        member // n_y * per_blk
        + (lax.axis_index("z") * n_y + member % n_y) * count
        + slot
    )
    plane_kind = at % BLOCK // HALF
    at = lax.broadcasted_iota(jnp.int32, (1, line.shape[0]), 1)
    member, slot = at // BLOCK, jnp.minimum(at % HALF, count - 1)
    line_at = blk * per_blk + (member * n_y + lax.axis_index("y_lo")) * count + slot
    line_kind = at % BLOCK // HALF
    plane_ids = pick(groups[...], plane_at, 0)
    line_ids = pick(groups[...], line_at, 1)

    logits = (
        lax.dot_general(
            plane[...], line[...], (((1,), (1,)), ((), ())), preferred_element_type=jnp.float32
        )
        * scale[0]
        + bias[0]
    )
    labels = jnp.where(plane_ids == line_ids, 1.0, -1.0)
    coeffs = -labels * jax.nn.sigmoid(-labels * logits) * scale[0]
    coeffs = jnp.where(plane_kind != line_kind, coeffs, 0.0).astype(jnp.bfloat16)
    parts[...] = jnp.dot(coeffs, line[...], preferred_element_type=jnp.float32).astype(jnp.bfloat16)


def grads_kernel(parts, projected, projection, text, pooled_grad, text_grad, sums):
    count, width = text.shape
    total = parts[...].astype(jnp.float32).reshape(-1, BLOCK, width)
    total = jnp.sum(total, axis=0)
    sums[...] = total
    proj = projected[...]
    norm = row_norm(proj)
    u = proj / norm
    d_proj = (total - jnp.sum(total * u, axis=1, keepdims=True) * u) / norm
    d_proj = jnp.concatenate([d_proj, jnp.zeros_like(d_proj)]).astype(jnp.bfloat16)
    pooled_grad[...] = lax.dot_general(
        d_proj, projection[...], (((1,), (1,)), ((), ())), preferred_element_type=jnp.float32
    )[:count]
    text_wide = text[...].astype(jnp.float32)
    norm = row_norm(text_wide)
    v = text_wide / norm
    d_txt = sums[HALF : HALF + count, :]
    text_grad[...] = (d_txt - jnp.sum(d_txt * v, axis=1, keepdims=True) * v) / norm


def shards(
    patch_keys,
    patch_values,
    lengths,
    probe_query,
    projection,
    text_embeds,
    pair_group,
    logit_scale,
    logit_bias,
):
    count, width = text_embeds.shape
    depth = patch_keys.shape[1]
    n_z = lax.axis_size("z")
    n_plane = lax.axis_size(PLANE)
    block, projected = pl.pallas_call(
        units_kernel,
        out_shape=(
            jax.ShapeDtypeStruct((BLOCK, width), jnp.bfloat16),
            jax.ShapeDtypeStruct((BLOCK, width), jnp.float32),
        ),
        in_specs=[SMEM] + [VMEM] * 5,
        out_specs=(VMEM, VMEM),
        scratch_shapes=[
            pltpu.VMEM((2 * BLOCK, depth), jnp.float32),
            pltpu.VMEM((BLOCK, width), jnp.float32),
        ],
        compiler_params=PARAMS,
        name="units",
    )(lengths, patch_keys, patch_values, probe_query.reshape(1, depth), projection, text_embeds)

    plane = lax.all_to_all(
        jnp.broadcast_to(block, (n_plane, BLOCK, width)), PLANE, 0, 0, tiled=True
    )
    line = lax.all_gather(block[None], "z", axis=0, tiled=True)
    parts = pl.pallas_call(
        lambda *refs: tile_kernel(count, *refs),
        out_shape=jax.ShapeDtypeStruct((n_plane * BLOCK, width), jnp.bfloat16),
        in_specs=[VMEM] * 3 + [SMEM] * 2,
        out_specs=VMEM,
        compiler_params=PARAMS,
        name="tile",
    )(
        plane.reshape(-1, width),
        line.reshape(-1, width),
        pair_group.reshape(-1, 128),
        logit_scale,
        logit_bias,
    )
    parts = lax.all_to_all(parts.reshape(n_plane, BLOCK, width), PLANE, 0, 0, tiled=True)
    return pl.pallas_call(
        grads_kernel,
        out_shape=(
            jax.ShapeDtypeStruct((count, depth), jnp.float32),
            jax.ShapeDtypeStruct((count, width), jnp.float32),
        ),
        in_specs=[VMEM] * 4,
        out_specs=(VMEM, VMEM),
        scratch_shapes=[pltpu.VMEM((BLOCK, width), jnp.float32)],
        compiler_params=PARAMS,
        name="grads",
    )(parts.reshape(-1, width), projected, projection, text_embeds)


def solution(mesh):
    fine = Mesh(mesh.devices.reshape(SIZES), AXES)
    rows = P(AXES, None)
    in_specs = (rows, rows, rows, P(), P(), rows, P(), P(), P())
    return jax.shard_map(
        shards, mesh=fine, in_specs=in_specs, out_specs=(rows, rows), check_vma=False
    )
```

time: 148 us -> 123 us (0.83); the launches traced: 146 us -> 123 us
  blocking collectives: 46.5 us -> 85.5 us
  local copies, waits for them, and re-layouts: 32.2 us -> 10.5 us
  waiting for transfers between devices: 15.5 us -> 0.01 us
  starting transfers between devices: 29.4 us -> 18.5 us
  matrix products: 10.8 us -> 0 us
  other arithmetic: 9.43 us -> 0 us
  Pallas kernels: 0 us -> 6.16 us
    all_gather x4 -> x1, blocking collectives: 26.9 us -> 53.1 us  [shards(): line = lax.all_gather(block[None], 'z', axis=0, tiled=True)]
    all_to_all x1, waiting for transfers between devices: 15.5 us -> 0.01 us  [shards(): lax.all_to_all(jnp.broadcast_to(block, (n_plane, BLOCK, width)), PLANE, 0...]
    all_to_all x1, blocking collectives: 19.6 us -> 32.4 us  [shards(): lax.all_to_all(parts.reshape(n_plane, BLOCK, width), PLANE, 0, 0, tiled=T...]
    all_to_all x1, starting transfers between devices: 29.4 us -> 18.5 us  [shards(): lax.all_to_all(jnp.broadcast_to(block, (n_plane, BLOCK, width)), PLANE, 0...]
    dot_general x5 -> x0, matrix products: 10.8 us -> none  [the longest x1 2.87 us: shards(): jnp.einsum('pl,le->pe', coeffs, line, preferred_element_type=jnp.float32)]
    reshape x6 -> x1, local copies, waits for them, and re-layouts: 11.3 us -> 0.69 us  [shards(): probe_query.reshape(1, depth)]
    pallas_call x0 -> x3, Pallas kernels: none -> 6.16 us  [the longest x1 2.2 us: shards(): pl.pallas_call(units_kernel, out_shape=(jax.ShapeDtypeStruct((BLOCK, widt...]
    unnamed x12 -> x24, local copies, waits for them, and re-layouts: 5.34 us -> 8.89 us
  transfers between devices with their start and end apart: 1 -> 1, of which waited for: 1 -> 0; matrix products, arithmetic and copies ran while one was open for 10% -> 0% of each run, Pallas kernels for 0% -> 0%
where the time goes in v2:
time: 123 us
  blocking collectives  85.5 us (70%)
  starting transfers between devices  18.5 us (15%)
  local copies, waits for them, and re-layouts  10.5 us (9%)
  Pallas kernels  6.16 us (5%)
  between operations  1.98 us (2%)
    all_gather x1, blocking collectives, shards(): line = lax.all_gather(block[None], 'z', axis=0, tiled=True)  53.1 us
    all_to_all x1, blocking collectives, shards(): lax.all_to_all(parts.reshape(n_plane, BLOCK, width), PLANE, 0, 0, tiled=T...  32.4 us
    all_to_all x1, starting transfers between devices, shards(): lax.all_to_all(jnp.broadcast_to(block, (n_plane, BLOCK, width)), PLANE, 0...  18.5 us
    unnamed x24, local copies, waits for them, and re-layouts  8.89 us
  transfers between devices with their start and end apart: 1, of which 0 were waited for; matrix products, arithmetic and copies ran while one was open for 0% of the time, Pallas kernels for 0%

profile of v2, /device:TPU:1, one launch (start us, length us, event | category | flops | bytes accessed | tf_op | source)
XLA Modules:
  0.0 122.6 jit_solution(5237278742554906151)
XLA Ops:
  0.6 0.7 reshape.22.probe
  1.3 0.0 copy-start
  1.3 2.0 %copy-done = bf16[1536,1152]{1,0:T(8,128)(2,1)S(1)} copy-done((bf16[1536,1152]{1,0:T(8,128)(2,1)S(1)}, bf16[1536,1152]{1,0:T(8,128)(2,1)}, u32[]{:S(2)}) %copy-start) | copy-done | bytes 3538968
  3.3 0.0 copy-start.3
  3.3 1.3 %copy-done.3 = bf16[384,1536]{1,0:T(8,128)(2,1)S(1)} copy-done((bf16[384,1536]{1,0:T(8,128)(2,1)S(1)}, bf16[384,1536]{1,0:T(8,128)(2,1)}, u32[]{:S(2)}) %copy-start.3) | copy-done | bytes 1179672
  4.6 0.0 copy-start.4
  4.6 1.3 %copy-done.4 = bf16[384,1536]{1,0:T(8,128)(2,1)S(1)} copy-done((bf16[384,1536]{1,0:T(8,128)(2,1)S(1)}, bf16[384,1536]{1,0:T(8,128)(2,1)}, u32[]{:S(2)}) %copy-start.4) | copy-done | bytes 1179672
  5.9 0.0 copy-start.8
  5.9 0.7 copy-done.8
  6.6 0.0 copy-start.11
  6.6 0.7 copy-done.11
  7.2 2.2 %units.1 = (bf16[8,1152]{1,0:T(8,128)(2,1)S(1)}, f32[8,1152]{1,0:T(8,128)S(1)}) custom-call(s32[1,3]{1,0:T(1,128)S(1)} %copy-done.11, bf16[384,1536]{1,0:T(8,128)(2,1)S(1)} %copy-done.3, bf16[384,1536]{1,0:T(8,128)(2,1)S(1)} %copy-done.4, bf16[1,1536]{1,0:T(2,128)(2,1)S(1)} %reshape.22.probe, bf16[1536,1152]{1,0:T(8,128)(2,1)S(1)} %copy-done, ...), custom_call_target="tpu_custom_call" | custom-call | tf_op jit(solution)/shard_map/units/pallas_call | solution.py:160
  9.4 0.0 copy-start.6
  9.4 0.6 copy-done.6
  10.1 0.0 copy-start.5
  10.1 0.6 copy-done.5
  10.7 0.9 broadcast_in_dim.6
  11.5 0.0 copy-start.9
  11.5 18.5 %all-to-all-start = ((bf16[32,8,1152]{2,1,0:T(8,128)(2,1)}), bf16[32,8,1152]{2,1,0:T(8,128)(2,1)}, u32[]{:S(2)}, u32[]{:S(2)}) async-start(bf16[32,8,1152]{2,1,0:T(8,128)(2,1)} %broadcast_in_dim.6), calls=%async_computation | async-start | bytes 1179648 | tf_op jit(solution)/shard_map/all_to_all | solution.py:176
  31.3 0.0 copy-start.1
  31.3 53.1 %all-gather.refs_1_ = bf16[256,1152]{1,0:T(8,128)(2,1)} all-gather(bf16[8,1152]{1,0:T(8,128)(2,1)} %copy-done.5), channel_id=2, replica_groups=mesh['y_hi'=2,'x'=4,'core'=2,'z'=32,'y_lo'=2] {'z'}, dimensions={0}, use_global_device_ids=true | all-gather | bytes 608256 | tf_op jit(solution)/shard_map/all_gather | solution.py:179
  84.4 0.0 all-to-all-done
  84.4 0.0 copy-start.2
  84.4 1.1 copy-done.2
  85.5 0.0 copy-start.10
  85.5 0.7 copy-done.10
  86.2 0.0 copy-start.7
  86.2 2.2 %tile.1 = bf16[256,1152]{1,0:T(8,128)(2,1)S(1)} custom-call(bf16[256,1152]{1,0:T(8,128)(2,1)} %bitcast.refs_0_, bf16[256,1152]{1,0:T(8,128)(2,1)S(1)} %copy-done.2, s32[24,128]{1,0:T(8,128)S(1)} %bitcast.6, f32[1]{0:T(128)S(6)} %copy.11.refs_3_, f32[1]{0:T(128)S(6)} %copy.12.refs_4_), custom_call_target="tpu_custom_call" | custom-call | tf_op jit(solution)/shard_map/tile/pallas_call | solution.py:180
  88.4 32.4 %all_to_all.10 = bf16[32,8,1152]{2,1,0:T(8,128)(2,1)S(1)} all-to-all(bf16[32,8,1152]{2,1,0:T(8,128)(2,1)S(1)} %bitcast.4), channel_id=1, replica_groups=mesh['y_hi'=2,'x'=4,'core'=2,'z'=32,'y_lo'=2] {'y_hi','x','core','y_lo'}, dimensions={0} | all-to-all | bytes 1179648 | tf_op jit(solution)/shard_map/all_to_all | solution.py:194
  120.8 0.0 copy-done.9
  120.8 0.0 copy-done.1
  120.8 0.0 copy-done.7
  120.8 1.8 %grads.1 = (f32[3,1536]{1,0:T(4,128)}, f32[3,1152]{1,0:T(4,128)}) custom-call(bf16[256,1152]{1,0:T(8,128)(2,1)S(1)} %bitcast.5, f32[8,1152]{1,0:T(8,128)S(1)} %copy-done.7, bf16[1536,1152]{1,0:T(8,128)(2,1)S(1)} %copy-done.1, bf16[3,1152]{1,0:T(4,128)(2,1)S(1)} %copy-done.9), custom_call_target="tpu_custom_call" | custom-call | tf_op jit(solution)/shard_map/grads/pallas_call | solution.py:195
Async XLA Ops:
  1.3 2.0 %copy-start = (bf16[1536,1152]{1,0:T(8,128)(2,1)S(1)}, bf16[1536,1152]{1,0:T(8,128)(2,1)}, u32[]{:S(2)}) copy-start(bf16[1536,1152]{1,0:T(8,128)(2,1)} %projection.3) | copy-start | bytes 10616836
  3.3 1.3 %copy-start.3 = (bf16[384,1536]{1,0:T(8,128)(2,1)S(1)}, bf16[384,1536]{1,0:T(8,128)(2,1)}, u32[]{:S(2)}) copy-start(bf16[384,1536]{1,0:T(8,128)(2,1)} %keys.1) | copy-start | bytes 3538948
  4.6 1.3 %copy-start.4 = (bf16[384,1536]{1,0:T(8,128)(2,1)S(1)}, bf16[384,1536]{1,0:T(8,128)(2,1)}, u32[]{:S(2)}) copy-start(bf16[384,1536]{1,0:T(8,128)(2,1)} %values.1) | copy-start | bytes 3538948
  5.9 0.7 copy-start.8
  6.6 0.7 copy-start.11
  9.4 0.6 copy-start.6
  10.1 0.6 copy-start.5
  11.5 109.3 %copy-start.9 = (bf16[3,1152]{1,0:T(4,128)(2,1)S(1)}, bf16[3,1152]{1,0:T(4,128)(2,1)}, u32[]{:S(2)}) copy-start(bf16[3,1152]{1,0:T(4,128)(2,1)} %text.3) | copy-start | bytes 20740
  11.5 72.9 %all-to-all-start = ((bf16[32,8,1152]{2,1,0:T(8,128)(2,1)}), bf16[32,8,1152]{2,1,0:T(8,128)(2,1)}, u32[]{:S(2)}, u32[]{:S(2)}) async-start(bf16[32,8,1152]{2,1,0:T(8,128)(2,1)} %broadcast_in_dim.6), calls=%async_computation | async-start | bytes 1179648 | tf_op jit(solution)/shard_map/all_to_all | solution.py:176
  31.3 89.5 %copy-start.1 = (bf16[1536,1152]{1,0:T(8,128)(2,1)S(1)}, bf16[1536,1152]{1,0:T(8,128)(2,1)}, u32[]{:S(2)}) copy-start(bf16[1536,1152]{1,0:T(8,128)(2,1)} %projection.3) | copy-start | bytes 10616836
  84.4 1.1 copy-start.2
  85.5 0.7 copy-start.10
  86.2 34.6 %copy-start.7 = (f32[8,1152]{1,0:T(8,128)S(1)}, f32[8,1152]{1,0:T(8,128)}, u32[]{:S(2)}) copy-start(f32[8,1152]{1,0:T(8,128)} %copy-done.6) | copy-start | bytes 110596

commit v3 on v2

--- a/solution.py
+++ b/solution.py
@@ -10,8 +10,8 @@
 H = 16
 HD = 96
 
-AXES = ("y_hi", "x", "core", "z", "y_lo")
-SIZES = (2, 4, 2, 32, 2)
+AXES = ("y_hi", "x", "core", "z_hi", "z_lo", "y_lo")
+SIZES = (2, 4, 2, 8, 4, 2)
 PLANE = ("y_hi", "x", "core", "y_lo")
 
 BLOCK = 8
@@ -91,19 +91,21 @@
 
 
 def tile_kernel(count, plane, line, groups, scale, bias, parts):
-    n_x, n_core, n_z, n_y = (lax.axis_size(axis) for axis in ("x", "core", "z", "y_lo"))
+    n_x, n_core, n_far, n_near, n_y = (lax.axis_size(axis) for axis in AXES[1:])
     blk = (lax.axis_index("y_hi") * n_x + lax.axis_index("x")) * n_core + lax.axis_index("core")
-    per_blk = n_z * n_y * count
+    z = lax.axis_index("z_hi") * n_near + lax.axis_index("z_lo")
+    per_blk = n_far * n_near * n_y * count
     at = lax.broadcasted_iota(jnp.int32, (plane.shape[0], 1), 0)
     member, slot = at // BLOCK, jnp.minimum(at % HALF, count - 1)
     plane_at = (
         member // n_y * per_blk
-        + (lax.axis_index("z") * n_y + member % n_y) * count
+        + (z * n_y + member % n_y) * count
         + slot
     )
     plane_kind = at % BLOCK // HALF
     at = lax.broadcasted_iota(jnp.int32, (1, line.shape[0]), 1)
     member, slot = at // BLOCK, jnp.minimum(at % HALF, count - 1)
+    member = member % n_far * n_near + member // n_far
     line_at = blk * per_blk + (member * n_y + lax.axis_index("y_lo")) * count + slot
     line_kind = at % BLOCK // HALF
     plane_ids = pick(groups[...], plane_at, 0)
@@ -142,6 +144,12 @@
     text_grad[...] = (d_txt - jnp.sum(d_txt * v, axis=1, keepdims=True) * v) / norm
 
 
+def spread(rows, axis):
+    n = lax.axis_size(axis)
+    copies = jnp.broadcast_to(rows, (n,) + rows.shape)
+    return lax.all_to_all(copies, axis, 0, 0, tiled=True).reshape(-1, rows.shape[1])
+
+
 def shards(
     patch_keys,
     patch_values,
@@ -155,7 +163,6 @@
 ):
     count, width = text_embeds.shape
     depth = patch_keys.shape[1]
-    n_z = lax.axis_size("z")
     n_plane = lax.axis_size(PLANE)
     block, projected = pl.pallas_call(
         units_kernel,
@@ -173,10 +180,13 @@
         name="units",
     )(lengths, patch_keys, patch_values, probe_query.reshape(1, depth), projection, text_embeds)
 
-    plane = lax.all_to_all(
-        jnp.broadcast_to(block, (n_plane, BLOCK, width)), PLANE, 0, 0, tiled=True
-    )
-    line = lax.all_gather(block[None], "z", axis=0, tiled=True)
+    far = spread(block, "z_hi")
+    plane = block
+    for step, axis in enumerate(PLANE[::-1]):
+        if step == 2:
+            far, plane = lax.optimization_barrier((far, plane))
+        plane = lax.all_gather(plane, axis, axis=0, tiled=True)
+    line = spread(far, "z_lo")
     parts = pl.pallas_call(
         lambda *refs: tile_kernel(count, *refs),
         out_shape=jax.ShapeDtypeStruct((n_plane * BLOCK, width), jnp.bfloat16),
@@ -185,8 +195,8 @@
         compiler_params=PARAMS,
         name="tile",
     )(
-        plane.reshape(-1, width),
-        line.reshape(-1, width),
+        plane,
+        line,
         pair_group.reshape(-1, 128),
         logit_scale,
         logit_bias,

time: 123 us -> 123 us (level)
  blocking collectives: 85.5 us -> 48 us
  waiting for transfers between devices: 0.01 us -> 19.4 us
  starting transfers between devices: 18.5 us -> 36.2 us
    all_gather x1 -> x4, blocking collectives: 53.1 us -> 26.3 us  [shards(): plane = lax.all_gather(plane, axis, axis=0, tiled=True)]
    all_to_all x1 -> x2, waiting for transfers between devices: 0.01 us -> 19.4 us  [spread(): lax.all_to_all(copies, axis, 0, 0, tiled=True).reshape(-1, rows.shape[1])]
    all_to_all x1 -> x2, starting transfers between devices: 18.5 us -> 36.2 us  [spread(): lax.all_to_all(copies, axis, 0, 0, tiled=True).reshape(-1, rows.shape[1])]
    all_to_all x1, blocking collectives: 32.4 us -> 21.6 us  [shards(): lax.all_to_all(parts.reshape(n_plane, BLOCK, width), PLANE, 0, 0, tiled=T...]
    unnamed x24 -> x22, local copies, waits for them, and re-layouts: 8.89 us -> 7.58 us
  transfers between devices with their start and end apart: 1 -> 2, of which waited for: 0 -> 1; matrix products, arithmetic and copies ran while one was open for 0% -> 0% of each run, Pallas kernels for 0% -> 0%
where the time goes in v3:
time: 123 us; the launch traced here: 122 us
  blocking collectives  48 us (39%)
  starting transfers between devices  36.2 us (29%)
  waiting for transfers between devices  19.4 us (16%)
  local copies, waits for them, and re-layouts  9.8 us (8%)
  Pallas kernels  6.17 us (5%)
  between operations  1.97 us (2%)
    all_to_all x2, starting transfers between devices, spread(): lax.all_to_all(copies, axis, 0, 0, tiled=True).reshape(-1, rows.shape[1])  36.2 us
    all_gather x4, blocking collectives, shards(): plane = lax.all_gather(plane, axis, axis=0, tiled=True)  26.3 us
    all_to_all x1, blocking collectives, shards(): lax.all_to_all(parts.reshape(n_plane, BLOCK, width), PLANE, 0, 0, tiled=T...  21.6 us
    all_to_all x2, waiting for transfers between devices, spread(): lax.all_to_all(copies, axis, 0, 0, tiled=True).reshape(-1, rows.shape[1])  19.4 us
    unnamed x22, local copies, waits for them, and re-layouts  7.58 us
  transfers between devices with their start and end apart: 2, of which 1 were waited for; matrix products, arithmetic and copies ran while one was open for 0% of the time, Pallas kernels for 0%

profile of v3, /device:TPU:1, one launch (start us, length us, event | category | flops | bytes accessed | tf_op | source)
XLA Modules:
  0.0 121.6 jit_solution(15940565675917763678)
XLA Ops:
  0.6 0.7 reshape.22.probe
  1.3 0.0 copy-start
  1.3 2.0 %copy-done = bf16[1536,1152]{1,0:T(8,128)(2,1)S(1)} copy-done((bf16[1536,1152]{1,0:T(8,128)(2,1)S(1)}, bf16[1536,1152]{1,0:T(8,128)(2,1)}, u32[]{:S(2)}) %copy-start) | copy-done | bytes 3538968
  3.3 0.0 copy-start.3
  3.3 1.3 %copy-done.3 = bf16[384,1536]{1,0:T(8,128)(2,1)S(1)} copy-done((bf16[384,1536]{1,0:T(8,128)(2,1)S(1)}, bf16[384,1536]{1,0:T(8,128)(2,1)}, u32[]{:S(2)}) %copy-start.3) | copy-done | bytes 1179672
  4.6 0.0 copy-start.4
  4.6 1.3 %copy-done.4 = bf16[384,1536]{1,0:T(8,128)(2,1)S(1)} copy-done((bf16[384,1536]{1,0:T(8,128)(2,1)S(1)}, bf16[384,1536]{1,0:T(8,128)(2,1)}, u32[]{:S(2)}) %copy-start.4) | copy-done | bytes 1179672
  5.9 0.0 copy-start.7
  5.9 0.7 copy-done.7
  6.6 0.0 copy-start.10
  6.6 0.7 copy-done.10
  7.2 2.2 %units.1 = (bf16[8,1152]{1,0:T(8,128)(2,1)S(1)}, f32[8,1152]{1,0:T(8,128)S(1)}) custom-call(s32[1,3]{1,0:T(1,128)S(1)} %copy-done.10, bf16[384,1536]{1,0:T(8,128)(2,1)S(1)} %copy-done.3, bf16[384,1536]{1,0:T(8,128)(2,1)S(1)} %copy-done.4, bf16[1,1536]{1,0:T(2,128)(2,1)S(1)} %reshape.22.probe, bf16[1536,1152]{1,0:T(8,128)(2,1)S(1)} %copy-done, ...), custom_call_target="tpu_custom_call" | custom-call | tf_op jit(solution)/shard_map/units/pallas_call | solution.py:167
  9.4 0.0 copy-start.5
  9.4 0.6 copy-done.5
  10.1 0.7 broadcast_in_dim.6
  10.7 28.9 %all-to-all-start = ((bf16[8,8,1152]{2,1,0:T(8,128)(2,1)}), bf16[8,8,1152]{2,1,0:T(8,128)(2,1)S(1)}, u32[]{:S(2)}, u32[]{:S(2)}) async-start(bf16[8,8,1152]{2,1,0:T(8,128)(2,1)} %broadcast_in_dim.6), calls=%async_computation | async-start | bytes 294912 | tf_op jit(solution)/shard_map/all_to_all | solution.py:150
  39.6 3.3 %all_gather.12 = bf16[16,1152]{1,0:T(8,128)(2,1)S(1)} all-gather(bf16[8,1152]{1,0:T(8,128)(2,1)S(1)} %get-tuple-element.6), channel_id=1, replica_groups=mesh['y_hi'=2,'x'=4,'core'=2,'z_hi'=8,'z_lo'=4,'y_lo'=2] {'y_lo'}, dimensions={0}, use_global_device_ids=true | all-gather | bytes 55296 | tf_op jit(solution)/shard_map/all_gather | solution.py:188
  42.9 3.6 %all_gather.13 = bf16[32,1152]{1,0:T(8,128)(2,1)S(1)} all-gather(bf16[16,1152]{1,0:T(8,128)(2,1)S(1)} %all_gather.12), channel_id=1, replica_groups=mesh['y_hi'=2,'x'=4,'core'=2,'z_hi'=8,'z_lo'=4,'y_lo'=2] {'core'}, dimensions={0}, use_global_device_ids=true | all-gather | bytes 110592 | tf_op jit(solution)/shard_map/all_gather | solution.py:188
  46.5 19.4 %all-to-all-done = bf16[8,8,1152]{2,1,0:T(8,128)(2,1)S(1)} async-done(((bf16[8,8,1152]{2,1,0:T(8,128)(2,1)}), bf16[8,8,1152]{2,1,0:T(8,128)(2,1)S(1)}, u32[]{:S(2)}, u32[]{:S(2)}) %all-to-all-start) | async-done | bytes 147488 | tf_op jit(solution)/shard_map/all_to_all | solution.py:150
  65.9 0.9 broadcast_in_dim.7
  66.8 0.0 copy-start.9
  66.8 7.3 %all-to-all-start.1 = ((bf16[4,64,1152]{2,1,0:T(8,128)(2,1)}), bf16[4,64,1152]{2,1,0:T(8,128)(2,1)}, u32[]{:S(2)}, u32[]{:S(2)}) async-start(bf16[4,64,1152]{2,1,0:T(8,128)(2,1)} %broadcast_in_dim.7), calls=%async_computation.1 | async-start | bytes 1179648 | tf_op jit(solution)/shard_map/all_to_all | solution.py:150
  75.4 11.2 %all_gather.14 = bf16[128,1152]{1,0:T(8,128)(2,1)S(1)} all-gather(bf16[32,1152]{1,0:T(8,128)(2,1)S(1)} %all_gather.13), channel_id=1, replica_groups=mesh['y_hi'=2,'x'=4,'core'=2,'z_hi'=8,'z_lo'=4,'y_lo'=2] {'x'}, dimensions={0}, use_global_device_ids=true | all-gather | bytes 368640 | tf_op jit(solution)/shard_map/all_gather | solution.py:188
  86.6 0.0 copy-start.1
  86.6 8.3 %all_gather.15.refs_0_ = bf16[256,1152]{1,0:T(8,128)(2,1)} all-gather(bf16[128,1152]{1,0:T(8,128)(2,1)S(1)} %all_gather.14), channel_id=1, replica_groups=mesh['y_hi'=2,'x'=4,'core'=2,'z_hi'=8,'z_lo'=4,'y_lo'=2] {'y_hi'}, dimensions={0}, use_global_device_ids=true | all-gather | bytes 884736 | tf_op jit(solution)/shard_map/all_gather | solution.py:188
  94.9 0.0 all-to-all-done.1
  94.9 0.0 copy-done.9
  94.9 0.0 copy-start.2
  94.9 1.1 copy-done.2
  96.0 0.0 copy-start.6
  96.0 0.0 copy-start.8
  96.0 2.2 %tile.1 = bf16[256,1152]{1,0:T(8,128)(2,1)S(1)} custom-call(bf16[256,1152]{1,0:T(8,128)(2,1)S(1)} %copy-done.2, bf16[256,1152]{1,0:T(8,128)(2,1)} %bitcast.1.refs_1_, s32[24,128]{1,0:T(8,128)S(1)} %bitcast.7, f32[1]{0:T(128)S(6)} %copy.11.refs_3_, f32[1]{0:T(128)S(6)} %copy.12.refs_4_), custom_call_target="tpu_custom_call" | custom-call | tf_op jit(solution)/shard_map/tile/pallas_call | solution.py:190
  98.1 21.6 %all_to_all.15 = bf16[32,8,1152]{2,1,0:T(8,128)(2,1)S(1)} all-to-all(bf16[32,8,1152]{2,1,0:T(8,128)(2,1)S(1)} %bitcast.5), channel_id=1, replica_groups=mesh['y_hi'=2,'x'=4,'core'=2,'z_hi'=8,'z_lo'=4,'y_lo'=2] {'y_hi','x','co..., dimensions={0} | all-to-all | bytes 1179648 | tf_op jit(solution)/shard_map/all_to_all | solution.py:204
  119.8 0.0 copy-done.1
  119.8 0.0 copy-done.6
  119.8 0.0 copy-done.8
  119.8 1.8 %grads.1 = (f32[3,1536]{1,0:T(4,128)}, f32[3,1152]{1,0:T(4,128)}) custom-call(bf16[256,1152]{1,0:T(8,128)(2,1)S(1)} %bitcast.6, f32[8,1152]{1,0:T(8,128)S(1)} %copy-done.6, bf16[1536,1152]{1,0:T(8,128)(2,1)S(1)} %copy-done.1, bf16[3,1152]{1,0:T(4,128)(2,1)S(1)} %copy-done.8), custom_call_target="tpu_custom_call" | custom-call | tf_op jit(solution)/shard_map/grads/pallas_call | solution.py:205
Async XLA Ops:
  1.3 2.0 %copy-start = (bf16[1536,1152]{1,0:T(8,128)(2,1)S(1)}, bf16[1536,1152]{1,0:T(8,128)(2,1)}, u32[]{:S(2)}) copy-start(bf16[1536,1152]{1,0:T(8,128)(2,1)} %projection.3) | copy-start | bytes 10616836
  3.3 1.3 %copy-start.3 = (bf16[384,1536]{1,0:T(8,128)(2,1)S(1)}, bf16[384,1536]{1,0:T(8,128)(2,1)}, u32[]{:S(2)}) copy-start(bf16[384,1536]{1,0:T(8,128)(2,1)} %keys.1) | copy-start | bytes 3538948
  4.6 1.3 %copy-start.4 = (bf16[384,1536]{1,0:T(8,128)(2,1)S(1)}, bf16[384,1536]{1,0:T(8,128)(2,1)}, u32[]{:S(2)}) copy-start(bf16[384,1536]{1,0:T(8,128)(2,1)} %values.1) | copy-start | bytes 3538948
  5.9 0.7 copy-start.7
  6.6 0.7 copy-start.10
  9.4 0.6 copy-start.5
  10.7 55.2 %all-to-all-start = ((bf16[8,8,1152]{2,1,0:T(8,128)(2,1)}), bf16[8,8,1152]{2,1,0:T(8,128)(2,1)S(1)}, u32[]{:S(2)}, u32[]{:S(2)}) async-start(bf16[8,8,1152]{2,1,0:T(8,128)(2,1)} %broadcast_in_dim.6), calls=%async_computation | async-start | bytes 294912 | tf_op jit(solution)/shard_map/all_to_all | solution.py:150
  66.8 28.1 %copy-start.9 = (s32[3072]{0:T(1024)S(1)}, s32[3072]{0:T(1024)}, u32[]{:S(2)}) copy-start(s32[3072]{0:T(1024)} %param.15) | copy-start | bytes 36868
  66.8 28.1 %all-to-all-start.1 = ((bf16[4,64,1152]{2,1,0:T(8,128)(2,1)}), bf16[4,64,1152]{2,1,0:T(8,128)(2,1)}, u32[]{:S(2)}, u32[]{:S(2)}) async-start(bf16[4,64,1152]{2,1,0:T(8,128)(2,1)} %broadcast_in_dim.7), calls=%async_computation.1 | async-start | bytes 1179648 | tf_op jit(solution)/shard_map/all_to_all | solution.py:150
  86.6 33.2 %copy-start.1 = (bf16[1536,1152]{1,0:T(8,128)(2,1)S(1)}, bf16[1536,1152]{1,0:T(8,128)(2,1)}, u32[]{:S(2)}) copy-start(bf16[1536,1152]{1,0:T(8,128)(2,1)} %projection.3) | copy-start | bytes 10616836
  94.9 1.1 copy-start.2
  96.0 23.8 %copy-start.6 = (f32[8,1152]{1,0:T(8,128)S(1)}, f32[8,1152]{1,0:T(8,128)}, u32[]{:S(2)}) copy-start(f32[8,1152]{1,0:T(8,128)} %copy-done.5) | copy-start | bytes 110596
  96.0 23.8 %copy-start.8 = (bf16[3,1152]{1,0:T(4,128)(2,1)S(1)}, bf16[3,1152]{1,0:T(4,128)(2,1)}, u32[]{:S(2)}) copy-start(bf16[3,1152]{1,0:T(4,128)(2,1)} %text.3) | copy-start | bytes 20740

commit v4 on v2

--- a/solution.py
+++ b/solution.py
@@ -16,10 +16,14 @@
 
 BLOCK = 8
 HALF = 4
+LANES = 128
+SPARE = (3, 7)
+FILLED = (0, 1, 2, 4, 5, 6)
 
 epsilon = 1e-06
 VMEM = pl.BlockSpec(memory_space=pltpu.VMEM)
 SMEM = pl.BlockSpec(memory_space=pltpu.SMEM)
+HBM = pl.BlockSpec(memory_space=pltpu.HBM)
 PARAMS = pltpu.CompilerParams(vmem_limit_bytes=24 << 20)
 
 
@@ -27,13 +31,84 @@
     return jnp.sqrt(jnp.sum(rows * rows, axis=1, keepdims=True) + epsilon)
 
 
+def pack(rows):
+    main = rows.shape[2] - len(SPARE) * LANES
+    place = lax.broadcasted_iota(jnp.int32, (rows.shape[0], BLOCK, LANES), 1)
+    runs = []
+    for run in range(main // LANES):
+        here = rows[:, :, run * LANES : (run + 1) * LANES]
+        for step, spare in enumerate(SPARE):
+            if run < len(FILLED):
+                at = main + step * LANES
+                moved = rows[:, FILLED[run] : FILLED[run] + 1, at : at + LANES]
+                here = jnp.where(place == spare, moved, here)
+            else:
+                here = jnp.where(place == spare, 0.0, here)
+        runs.append(here)
+    return jnp.concatenate(runs, axis=2)
+
+
+def unpack(rows):
+    place = lax.broadcasted_iota(jnp.int32, (rows.shape[0], BLOCK, LANES), 1)
+    runs = []
+    for run in range(rows.shape[2] // LANES):
+        here = rows[:, :, run * LANES : (run + 1) * LANES]
+        for spare in SPARE:
+            here = jnp.where(place == spare, 0.0, here)
+        runs.append(here)
+    for spare in SPARE:
+        tail = jnp.zeros(place.shape, rows.dtype)
+        for run, filled in enumerate(FILLED):
+            moved = rows[:, spare : spare + 1, run * LANES : (run + 1) * LANES]
+            tail = jnp.where(place == filled, moved, tail)
+        runs.append(tail)
+    return jnp.concatenate(runs, axis=2)
+
+
+def unpack_rows(rows):
+    wide = unpack(rows.astype(jnp.float32).reshape(-1, BLOCK, rows.shape[1]))
+    return wide.reshape(-1, wide.shape[2]).astype(jnp.bfloat16)
+
+
 def units_kernel(
-    lengths, keys, values, probe, projection, text, block, projected, pooled, units
+    lengths_at,
+    keys_at,
+    values_at,
+    probe,
+    projection_at,
+    text_at,
+    block,
+    copies,
+    projected,
+    lengths,
+    keys,
+    values,
+    projection,
+    text,
+    pooled,
+    units,
+    arrived,
 ):
+    fetches = [
+        pltpu.make_async_copy(source, target, arrived.at[i])
+        for i, (source, target) in enumerate(
+            (
+                (lengths_at, lengths),
+                (keys_at, keys),
+                (values_at, values),
+                (text_at, text),
+                (projection_at, projection),
+            )
+        )
+    ]
+    for fetch in fetches:
+        fetch.start()
     n_rows, width = keys.shape
     head = lax.broadcasted_iota(jnp.int32, (H, width), 0)
     own = lax.broadcasted_iota(jnp.int32, (H, width), 1) // HD == head
     query = jnp.where(own, probe[...].astype(jnp.float32), 0.0).astype(jnp.bfloat16)
+    fetches[0].wait()
+    fetches[1].wait()
     scores = lax.dot_general(
         query, keys[...], (((1,), (1,)), ((), ())), preferred_element_type=jnp.float32
     ) / math.sqrt(HD)
@@ -47,6 +122,7 @@
         terms = jnp.exp(masked - jnp.max(masked, axis=1, keepdims=True))
         weights.append((terms / jnp.sum(terms, axis=1, keepdims=True)).astype(jnp.bfloat16))
         start = end
+    fetches[2].wait()
     mixed = jnp.dot(
         jnp.concatenate(weights), values[...], preferred_element_type=jnp.float32
     )
@@ -54,6 +130,8 @@
     for image in range(lengths.shape[1]):
         part = mixed[image * H : (image + 1) * H]
         pooled[image : image + 1, :] = jnp.sum(jnp.where(own, part, 0.0), axis=0, keepdims=True)
+    fetches[3].wait()
+    fetches[4].wait()
     proj = jnp.dot(
         pooled[...].astype(jnp.bfloat16), projection[...], preferred_element_type=jnp.float32
     )[:BLOCK]
@@ -62,8 +140,12 @@
     text_wide = text[...].astype(jnp.float32)
     count = text.shape[0]
     units[HALF : HALF + count, :] = text_wide / row_norm(text_wide)
-    filled = lax.broadcasted_iota(jnp.int32, units.shape, 0) % HALF < count
-    block[...] = jnp.where(filled, units[...], 0.0).astype(jnp.bfloat16)
+    packed = pack(units[...][None])
+    block[...] = packed[0].astype(jnp.bfloat16)
+    n = copies.shape[0] // BLOCK
+    copies[...] = (
+        jnp.broadcast_to(packed, (n,) + packed.shape[1:]).reshape(copies.shape).astype(jnp.bfloat16)
+    )
 
 
 def pick(groups, positions, axis):
@@ -109,9 +191,10 @@
     plane_ids = pick(groups[...], plane_at, 0)
     line_ids = pick(groups[...], line_at, 1)
 
+    plane_rows, line_rows = unpack_rows(plane[...]), unpack_rows(line[...])
     logits = (
         lax.dot_general(
-            plane[...], line[...], (((1,), (1,)), ((), ())), preferred_element_type=jnp.float32
+            plane_rows, line_rows, (((1,), (1,)), ((), ())), preferred_element_type=jnp.float32
         )
         * scale[0]
         + bias[0]
@@ -119,13 +202,15 @@
     labels = jnp.where(plane_ids == line_ids, 1.0, -1.0)
     coeffs = -labels * jax.nn.sigmoid(-labels * logits) * scale[0]
     coeffs = jnp.where(plane_kind != line_kind, coeffs, 0.0).astype(jnp.bfloat16)
-    parts[...] = jnp.dot(coeffs, line[...], preferred_element_type=jnp.float32).astype(jnp.bfloat16)
+    wide = jnp.dot(coeffs, line_rows, preferred_element_type=jnp.float32)
+    packed = pack(wide.reshape(-1, BLOCK, wide.shape[1]))
+    parts[...] = packed.reshape(parts.shape).astype(jnp.bfloat16)
 
 
 def grads_kernel(parts, projected, projection, text, pooled_grad, text_grad, sums):
     count, width = text.shape
-    total = parts[...].astype(jnp.float32).reshape(-1, BLOCK, width)
-    total = jnp.sum(total, axis=0)
+    total = parts[...].astype(jnp.float32).reshape(-1, BLOCK, parts.shape[1])
+    total = unpack(jnp.sum(total, axis=0, keepdims=True))[0]
     sums[...] = total
     proj = projected[...]
     norm = row_norm(proj)
@@ -157,41 +242,49 @@
     depth = patch_keys.shape[1]
     n_z = lax.axis_size("z")
     n_plane = lax.axis_size(PLANE)
-    block, projected = pl.pallas_call(
+    narrow = width - len(SPARE) * LANES
+    block, copies, projected = pl.pallas_call(
         units_kernel,
         out_shape=(
-            jax.ShapeDtypeStruct((BLOCK, width), jnp.bfloat16),
+            jax.ShapeDtypeStruct((BLOCK, narrow), jnp.bfloat16),
+            jax.ShapeDtypeStruct((n_z * BLOCK, narrow), jnp.bfloat16),
             jax.ShapeDtypeStruct((BLOCK, width), jnp.float32),
         ),
-        in_specs=[SMEM] + [VMEM] * 5,
-        out_specs=(VMEM, VMEM),
+        in_specs=[HBM] * 3 + [VMEM] + [HBM] * 2,
+        out_specs=(VMEM, VMEM, VMEM),
         scratch_shapes=[
+            pltpu.SMEM(lengths.shape, lengths.dtype),
+            pltpu.VMEM(patch_keys.shape, patch_keys.dtype),
+            pltpu.VMEM(patch_values.shape, patch_values.dtype),
+            pltpu.VMEM(projection.shape, projection.dtype),
+            pltpu.VMEM(text_embeds.shape, text_embeds.dtype),
             pltpu.VMEM((2 * BLOCK, depth), jnp.float32),
             pltpu.VMEM((BLOCK, width), jnp.float32),
+            pltpu.SemaphoreType.DMA((5,)),
         ],
-        compiler_params=PARAMS,
+        compiler_params=pltpu.CompilerParams(vmem_limit_bytes=60 << 20),
         name="units",
     )(lengths, patch_keys, patch_values, probe_query.reshape(1, depth), projection, text_embeds)
 
-    plane = lax.all_to_all(
-        jnp.broadcast_to(block, (n_plane, BLOCK, width)), PLANE, 0, 0, tiled=True
-    )
-    line = lax.all_gather(block[None], "z", axis=0, tiled=True)
+    line = lax.all_to_all(copies.reshape(n_z, BLOCK, narrow), "z", 0, 0, tiled=True)
+    plane = block
+    for axis in PLANE[::-1]:
+        plane = lax.all_gather(plane, axis, axis=0, tiled=True)
     parts = pl.pallas_call(
         lambda *refs: tile_kernel(count, *refs),
-        out_shape=jax.ShapeDtypeStruct((n_plane * BLOCK, width), jnp.bfloat16),
+        out_shape=jax.ShapeDtypeStruct((n_plane * BLOCK, narrow), jnp.bfloat16),
         in_specs=[VMEM] * 3 + [SMEM] * 2,
         out_specs=VMEM,
         compiler_params=PARAMS,
         name="tile",
     )(
-        plane.reshape(-1, width),
-        line.reshape(-1, width),
+        plane,
+        line.reshape(-1, narrow),
         pair_group.reshape(-1, 128),
         logit_scale,
         logit_bias,
     )
-    parts = lax.all_to_all(parts.reshape(n_plane, BLOCK, width), PLANE, 0, 0, tiled=True)
+    parts = lax.all_to_all(parts.reshape(n_plane, BLOCK, narrow), PLANE, 0, 0, tiled=True)
     return pl.pallas_call(
         grads_kernel,
         out_shape=(
@@ -203,7 +296,7 @@
         scratch_shapes=[pltpu.VMEM((BLOCK, width), jnp.float32)],
         compiler_params=PARAMS,
         name="grads",
-    )(parts.reshape(-1, width), projected, projection, text_embeds)
+    )(parts.reshape(-1, narrow), projected, projection, text_embeds)
 
 
 def solution(mesh):

time: 123 us -> 120 us (0.976)
  blocking collectives: 85.5 us -> 43.9 us
  waiting for transfers between devices: 0.01 us -> 32.2 us
  starting transfers between devices: 18.5 us -> 29.7 us
  local copies, waits for them, and re-layouts: 10.5 us -> 2.32 us
  Pallas kernels: 6.16 us -> 9.11 us
    all_to_all x1, waiting for transfers between devices: 0.01 us -> 32.2 us  [shards(): lax.all_to_all(copies.reshape(n_z, BLOCK, narrow), 'z', 0, 0, tiled=True)]
    all_gather x1 -> x4, blocking collectives: 53.1 us -> 24.8 us  [shards(): plane = lax.all_gather(plane, axis, axis=0, tiled=True)]
    all_to_all x1, blocking collectives: 32.4 us -> 19.1 us  [shards(): lax.all_to_all(parts.reshape(n_plane, BLOCK, narrow), PLANE, 0, 0, tiled=...]
    all_to_all x1, starting transfers between devices: 18.5 us -> 29.7 us  [shards(): lax.all_to_all(copies.reshape(n_z, BLOCK, narrow), 'z', 0, 0, tiled=True)]
    unnamed x24 -> x10, local copies, waits for them, and re-layouts: 8.89 us -> 1.04 us
    pallas_call x1, Pallas kernels: 2.2 us -> 4.98 us  [shards(): pl.pallas_call(units_kernel, out_shape=(jax.ShapeDtypeStruct((BLOCK, narr...]
  transfers between devices with their start and end apart: 1 -> 1, of which waited for: 0 -> 1; matrix products, arithmetic and copies ran while one was open for 0% -> 0% of each run, Pallas kernels for 0% -> 0%
where the time goes in v4:
time: 120 us; the launch traced here: 119 us
  blocking collectives  43.9 us (37%)
  waiting for transfers between devices  32.2 us (27%)
  starting transfers between devices  29.7 us (25%)
  Pallas kernels  9.11 us (8%)
  local copies, waits for them, and re-layouts  2.32 us (2%)
  between operations  1.97 us (2%)
    all_to_all x1, waiting for transfers between devices, shards(): lax.all_to_all(copies.reshape(n_z, BLOCK, narrow), 'z', 0, 0, tiled=True)  32.2 us
    all_to_all x1, starting transfers between devices, shards(): lax.all_to_all(copies.reshape(n_z, BLOCK, narrow), 'z', 0, 0, tiled=True)  29.7 us
    all_gather x4, blocking collectives, shards(): plane = lax.all_gather(plane, axis, axis=0, tiled=True)  24.8 us
    all_to_all x1, blocking collectives, shards(): lax.all_to_all(parts.reshape(n_plane, BLOCK, narrow), PLANE, 0, 0, tiled=...  19.1 us
    pallas_call x1, Pallas kernels, shards(): pl.pallas_call(units_kernel, out_shape=(jax.ShapeDtypeStruct((BLOCK, narr...  4.98 us
  transfers between devices with their start and end apart: 1, of which 1 were waited for; matrix products, arithmetic and copies ran while one was open for 0% of the time, Pallas kernels for 0%

profile of v4, /device:TPU:1, one launch (start us, length us, event | category | flops | bytes accessed | tf_op | source)
XLA Modules:
  0.0 119.2 jit_solution(14111351553899325933)
XLA Ops:
  0.6 1.3 %reshape.22.probe = bf16[1,1536]{1,0:T(2,128)(2,1)} reshape(bf16[1536]{0:T(1024)(128)(2,1)} %param.12) | data formatting | bytes 6144 | tf_op jit(solution)/shard_map/reshape | solution.py:267
  1.9 0.0 copy-start.4
  1.9 5.0 %units.1 = (bf16[8,896]{1,0:T(8,128)(2,1)}, bf16[256,896]{1,0:T(8,128)(2,1)}, f32[8,1152]{1,0:T(8,128)}) custom-call(s32[1,3]{1,0:T(1,128)} %lengths_at.1, bf16[384,1536]{1,0:T(8,128)(2,1)} %keys_at.1, bf16[384,1536]{1,0:T(8,128)(2,1)} %values_at.1, bf16[1,1536]{1,0:T(2,128)(2,1)} %reshape.22.probe, bf16[1536,1152]{1,0:T(8,128)(2,1)} %projection.1, ...), custom_call_target="tpu_custom_call" | custom-call | tf_op jit(solution)/shard_map/units/pallas_call | solution.py:246
  6.9 0.0 copy-start
  6.9 29.7 %all-to-all-start = ((bf16[32,8,896]{2,1,0:T(8,128)(2,1)}), bf16[32,8,896]{2,1,0:T(8,128)(2,1)}, u32[]{:S(2)}, u32[]{:S(2)}) async-start(bf16[32,8,896]{2,1,0:T(8,128)(2,1)} %bitcast.8), calls=%async_computation | async-start | bytes 917504 | tf_op jit(solution)/shard_map/all_to_all | solution.py:269
  37.9 3.5 %all_gather.12 = bf16[16,896]{1,0:T(8,128)(2,1)S(1)} all-gather(bf16[8,896]{1,0:T(8,128)(2,1)} %get-tuple-element.5), channel_id=1, replica_groups=mesh['y_hi'=2,'x'=4,'core'=2,'z'=32,'y_lo'=2] {'y_lo'}, dimensions={0}, use_global_device_ids=true | all-gather | bytes 43008 | tf_op jit(solution)/shard_map/all_gather | solution.py:272
  41.4 3.6 %all_gather.13 = bf16[32,896]{1,0:T(8,128)(2,1)S(1)} all-gather(bf16[16,896]{1,0:T(8,128)(2,1)S(1)} %all_gather.12), channel_id=1, replica_groups=mesh['y_hi'=2,'x'=4,'core'=2,'z'=32,'y_lo'=2] {'core'}, dimensions={0}, use_global_device_ids=true | all-gather | bytes 86016 | tf_op jit(solution)/shard_map/all_gather | solution.py:272
  45.0 10.2 %all_gather.14 = bf16[128,896]{1,0:T(8,128)(2,1)S(1)} all-gather(bf16[32,896]{1,0:T(8,128)(2,1)S(1)} %all_gather.13), channel_id=1, replica_groups=mesh['y_hi'=2,'x'=4,'core'=2,'z'=32,'y_lo'=2] {'x'}, dimensions={0}, use_global_device_ids=true | all-gather | bytes 286720 | tf_op jit(solution)/shard_map/all_gather | solution.py:272
  55.2 7.4 %all_gather.15.refs_0_ = bf16[256,896]{1,0:T(8,128)(2,1)} all-gather(bf16[128,896]{1,0:T(8,128)(2,1)S(1)} %all_gather.14), channel_id=1, replica_groups=mesh['y_hi'=2,'x'=4,'core'=2,'z'=32,'y_lo'=2] {'y_hi'}, dimensions={0}, use_global_device_ids=true | all-gather | bytes 688128 | tf_op jit(solution)/shard_map/all_gather | solution.py:272
  62.6 32.2 %all-to-all-done = bf16[32,8,896]{2,1,0:T(8,128)(2,1)} async-done(((bf16[32,8,896]{2,1,0:T(8,128)(2,1)}), bf16[32,8,896]{2,1,0:T(8,128)(2,1)}, u32[]{:S(2)}, u32[]{:S(2)}) %all-to-all-start) | async-done | bytes 458784 | tf_op jit(solution)/shard_map/all_to_all | solution.py:269
  94.8 0.0 copy-done.4
  94.8 0.0 copy-start.1
  94.8 1.0 copy-done.1
  95.9 0.0 copy-start.2
  95.9 0.0 copy-start.3
  95.9 2.4 %tile.1 = bf16[256,896]{1,0:T(8,128)(2,1)S(1)} custom-call(bf16[256,896]{1,0:T(8,128)(2,1)S(1)} %copy-done.1, bf16[256,896]{1,0:T(8,128)(2,1)} %bitcast.1.refs_1_, s32[24,128]{1,0:T(8,128)S(1)} %bitcast.7, f32[1]{0:T(128)S(6)} %copy.11.refs_3_, f32[1]{0:T(128)S(6)} %copy.12.refs_4_), custom_call_target="tpu_custom_call" | custom-call | tf_op jit(solution)/shard_map/tile/pallas_call | solution.py:273
  98.2 19.1 %all_to_all.10 = bf16[32,8,896]{2,1,0:T(8,128)(2,1)S(1)} all-to-all(bf16[32,8,896]{2,1,0:T(8,128)(2,1)S(1)} %bitcast.5), channel_id=1, replica_groups=mesh['y_hi'=2,'x'=4,'core'=2,'z'=32,'y_lo'=2] {'y_hi','x','core','y_lo'}, dimensions={0} | all-to-all | bytes 917504 | tf_op jit(solution)/shard_map/all_to_all | solution.py:287
  117.4 0.0 copy-done
  117.4 0.0 copy-done.2
  117.4 0.0 copy-done.3
  117.4 1.8 %grads.1 = (f32[3,1536]{1,0:T(4,128)}, f32[3,1152]{1,0:T(4,128)}) custom-call(bf16[256,896]{1,0:T(8,128)(2,1)S(1)} %bitcast.6, f32[8,1152]{1,0:T(8,128)S(1)} %copy-done.2, bf16[1536,1152]{1,0:T(8,128)(2,1)S(1)} %copy-done, bf16[3,1152]{1,0:T(4,128)(2,1)S(1)} %copy-done.3), custom_call_target="tpu_custom_call" | custom-call | tf_op jit(solution)/shard_map/grads/pallas_call | solution.py:288
Async XLA Ops:
  1.9 92.9 %copy-start.4 = (s32[3072]{0:T(1024)S(1)}, s32[3072]{0:T(1024)}, u32[]{:S(2)}) copy-start(s32[3072]{0:T(1024)} %param.15) | copy-start | bytes 36868
  6.9 110.5 %copy-start = (bf16[1536,1152]{1,0:T(8,128)(2,1)S(1)}, bf16[1536,1152]{1,0:T(8,128)(2,1)}, u32[]{:S(2)}) copy-start(bf16[1536,1152]{1,0:T(8,128)(2,1)} %projection.1) | copy-start | bytes 10616836
  6.9 87.9 %all-to-all-start = ((bf16[32,8,896]{2,1,0:T(8,128)(2,1)}), bf16[32,8,896]{2,1,0:T(8,128)(2,1)}, u32[]{:S(2)}, u32[]{:S(2)}) async-start(bf16[32,8,896]{2,1,0:T(8,128)(2,1)} %bitcast.8), calls=%async_computation | async-start | bytes 917504 | tf_op jit(solution)/shard_map/all_to_all | solution.py:269
  94.8 1.0 copy-start.1
  95.9 21.5 %copy-start.2 = (f32[8,1152]{1,0:T(8,128)S(1)}, f32[8,1152]{1,0:T(8,128)}, u32[]{:S(2)}) copy-start(f32[8,1152]{1,0:T(8,128)} %get-tuple-element.7.projected) | copy-start | bytes 110596
  95.9 21.5 %copy-start.3 = (bf16[3,1152]{1,0:T(4,128)(2,1)S(1)}, bf16[3,1152]{1,0:T(4,128)(2,1)}, u32[]{:S(2)}) copy-start(bf16[3,1152]{1,0:T(4,128)(2,1)} %text.1) | copy-start | bytes 20740

commit v5 on v4

--- a/solution.py
+++ b/solution.py
@@ -10,9 +10,9 @@
 H = 16
 HD = 96
 
-AXES = ("y_hi", "x", "core", "z", "y_lo")
-SIZES = (2, 4, 2, 32, 2)
-PLANE = ("y_hi", "x", "core", "y_lo")
+AXES = ("y_hi", "x", "core", "z_hi", "z_lo", "y_lo")
+SIZES = (2, 4, 2, 8, 4, 2)
+PLANE = ("core", "y_hi", "y_lo", "x")
 
 BLOCK = 8
 HALF = 4
@@ -106,7 +106,7 @@
     n_rows, width = keys.shape
     head = lax.broadcasted_iota(jnp.int32, (H, width), 0)
     own = lax.broadcasted_iota(jnp.int32, (H, width), 1) // HD == head
-    query = jnp.where(own, probe[...].astype(jnp.float32), 0.0).astype(jnp.bfloat16)
+    query = jnp.where(own, probe[...].astype(jnp.float32).reshape(1, width), 0.0).astype(jnp.bfloat16)
     fetches[0].wait()
     fetches[1].wait()
     scores = lax.dot_general(
@@ -172,21 +172,28 @@
     return pieces[0] * 64.0 + pieces[1]
 
 
+def device(place, sizes):
+    number = 0
+    for axis in AXES:
+        number = number * sizes[axis] + place[axis]
+    return number
+
+
 def tile_kernel(count, plane, line, groups, scale, bias, parts):
-    n_x, n_core, n_z, n_y = (lax.axis_size(axis) for axis in ("x", "core", "z", "y_lo"))
-    blk = (lax.axis_index("y_hi") * n_x + lax.axis_index("x")) * n_core + lax.axis_index("core")
-    per_blk = n_z * n_y * count
+    sizes = dict((axis, lax.axis_size(axis)) for axis in AXES)
+    place = dict((axis, lax.axis_index(axis)) for axis in AXES)
     at = lax.broadcasted_iota(jnp.int32, (plane.shape[0], 1), 0)
     member, slot = at // BLOCK, jnp.minimum(at % HALF, count - 1)
-    plane_at = (
-        member // n_y * per_blk
-        + (lax.axis_index("z") * n_y + member % n_y) * count
-        + slot
-    )
+    there = dict(place)
+    for axis in PLANE[::-1]:
+        there[axis] = member % sizes[axis]
+        member = member // sizes[axis]
+    plane_at = device(there, sizes) * count + slot
     plane_kind = at % BLOCK // HALF
     at = lax.broadcasted_iota(jnp.int32, (1, line.shape[0]), 1)
     member, slot = at // BLOCK, jnp.minimum(at % HALF, count - 1)
-    line_at = blk * per_blk + (member * n_y + lax.axis_index("y_lo")) * count + slot
+    there = dict(place, z_hi=member % sizes["z_hi"], z_lo=member // sizes["z_hi"])
+    line_at = device(there, sizes) * count + slot
     line_kind = at % BLOCK // HALF
     plane_ids = pick(groups[...], plane_at, 0)
     line_ids = pick(groups[...], line_at, 1)
@@ -227,6 +234,11 @@
     text_grad[...] = (d_txt - jnp.sum(d_txt * v, axis=1, keepdims=True) * v) / norm
 
 
+def exchange(rows, axis):
+    shape = (lax.axis_size(axis), -1, rows.shape[1])
+    return lax.all_to_all(rows.reshape(shape), axis, 0, 0, tiled=True).reshape(rows.shape)
+
+
 def shards(
     patch_keys,
     patch_values,
@@ -240,14 +252,14 @@
 ):
     count, width = text_embeds.shape
     depth = patch_keys.shape[1]
-    n_z = lax.axis_size("z")
+    n_far = lax.axis_size("z_hi")
     n_plane = lax.axis_size(PLANE)
     narrow = width - len(SPARE) * LANES
     block, copies, projected = pl.pallas_call(
         units_kernel,
         out_shape=(
             jax.ShapeDtypeStruct((BLOCK, narrow), jnp.bfloat16),
-            jax.ShapeDtypeStruct((n_z * BLOCK, narrow), jnp.bfloat16),
+            jax.ShapeDtypeStruct((n_far * BLOCK, narrow), jnp.bfloat16),
             jax.ShapeDtypeStruct((BLOCK, width), jnp.float32),
         ),
         in_specs=[HBM] * 3 + [VMEM] + [HBM] * 2,
@@ -264,27 +276,30 @@
         ],
         compiler_params=pltpu.CompilerParams(vmem_limit_bytes=60 << 20),
         name="units",
-    )(lengths, patch_keys, patch_values, probe_query.reshape(1, depth), projection, text_embeds)
-
-    line = lax.all_to_all(copies.reshape(n_z, BLOCK, narrow), "z", 0, 0, tiled=True)
+    )(lengths, patch_keys, patch_values, probe_query, projection, text_embeds)
+
+    far = exchange(copies, "z_hi")
     plane = block
-    for axis in PLANE[::-1]:
+    for step, axis in enumerate(PLANE[::-1]):
+        if step == 2:
+            far, plane = lax.optimization_barrier((far, plane))
         plane = lax.all_gather(plane, axis, axis=0, tiled=True)
+    line = exchange(jnp.tile(far, (lax.axis_size("z_lo"), 1)), "z_lo")
     parts = pl.pallas_call(
         lambda *refs: tile_kernel(count, *refs),
         out_shape=jax.ShapeDtypeStruct((n_plane * BLOCK, narrow), jnp.bfloat16),
         in_specs=[VMEM] * 3 + [SMEM] * 2,
         out_specs=VMEM,
-        compiler_params=PARAMS,
+        compiler_params=pltpu.CompilerParams(vmem_limit_bytes=60 << 20),
         name="tile",
     )(
         plane,
-        line.reshape(-1, narrow),
+        line,
         pair_group.reshape(-1, 128),
         logit_scale,
         logit_bias,
     )
-    parts = lax.all_to_all(parts.reshape(n_plane, BLOCK, narrow), PLANE, 0, 0, tiled=True)
+    parts = exchange(parts, PLANE)
     return pl.pallas_call(
         grads_kernel,
         out_shape=(
@@ -296,7 +311,7 @@
         scratch_shapes=[pltpu.VMEM((BLOCK, width), jnp.float32)],
         compiler_params=PARAMS,
         name="grads",
-    )(parts.reshape(-1, narrow), projected, projection, text_embeds)
+    )(parts, projected, projection, text_embeds)
 
 
 def solution(mesh):

time: 120 us -> 104 us (0.87)
  waiting for transfers between devices: 32.2 us -> 9.77 us
  starting transfers between devices: 29.7 us -> 35.7 us
  local copies, waits for them, and re-layouts: 2.32 us -> 0.83 us
    all_to_all x1 -> x2, waiting for transfers between devices: 32.2 us -> 9.77 us  [exchange(): lax.all_to_all(rows.reshape(shape), axis, 0, 0, tiled=True)]
    all_to_all x1 -> x2, starting transfers between devices: 29.7 us -> 35.7 us  [exchange(): lax.all_to_all(rows.reshape(shape), axis, 0, 0, tiled=True)]
    all_gather x4, blocking collectives: 24.8 us -> 26.2 us  [shards(): plane = lax.all_gather(plane, axis, axis=0, tiled=True)]
    reshape x1 -> x0, local copies, waits for them, and re-layouts: 1.28 us -> none  [shards(): probe_query.reshape(1, depth)]
  transfers between devices with their start and end apart: 1 -> 2, of which waited for: 1 -> 1; matrix products, arithmetic and copies ran while one was open for 0% -> 0% of each run, Pallas kernels for 0% -> 0%
where the time goes in v5:
time: 104 us; the launch traced here: 103 us
  blocking collectives  44.9 us (43%)
  starting transfers between devices  35.7 us (34%)
  Pallas kernels  10 us (10%)
  waiting for transfers between devices  9.77 us (9%)
  between operations  1.95 us (2%)
    all_to_all x2, starting transfers between devices, exchange(): lax.all_to_all(rows.reshape(shape), axis, 0, 0, tiled=True)  35.7 us
    all_gather x4, blocking collectives, shards(): plane = lax.all_gather(plane, axis, axis=0, tiled=True)  26.2 us
    all_to_all x1, blocking collectives, exchange(): lax.all_to_all(rows.reshape(shape), axis, 0, 0, tiled=True)  18.8 us
    all_to_all x2, waiting for transfers between devices, exchange(): lax.all_to_all(rows.reshape(shape), axis, 0, 0, tiled=True)  9.77 us
    pallas_call x1, Pallas kernels, shards(): pl.pallas_call(units_kernel, out_shape=(jax.ShapeDtypeStruct((BLOCK, narr...  4.81 us
    pallas_call x1, Pallas kernels, shards(): pl.pallas_call(lambda *refs: tile_kernel(count, *refs), out_shape=jax.Sha...  3.47 us
  transfers between devices with their start and end apart: 2, of which 1 were waited for; matrix products, arithmetic and copies ran while one was open for 0% of the time, Pallas kernels for 0%

profile of v5, /device:TPU:1, one launch (start us, length us, event | category | flops | bytes accessed | tf_op | source)
XLA Modules:
  0.0 103.3 jit_solution(11761136842171533531)
XLA Ops:
  0.6 4.8 %units.1 = (bf16[8,896]{1,0:T(8,128)(2,1)}, bf16[64,896]{1,0:T(8,128)(2,1)}, f32[8,1152]{1,0:T(8,128)}) custom-call(s32[1,3]{1,0:T(1,128)} %lengths_at.1, bf16[384,1536]{1,0:T(8,128)(2,1)} %keys_at.1, bf16[384,1536]{1,0:T(8,128)(2,1)} %values_at.1, bf16[1536]{0:T(1024)(128)(2,1)} %probe.1, bf16[1536,1152]{1,0:T(8,128)(2,1)} %projection.1, bf16[3,1152]{1,0:T(4,128)(2,1)} %text.1), custom_call_target="tpu_custom_call" | custom-call | tf_op jit(solution)/shard_map/units/pallas_call | solution.py:258
  5.4 28.9 %all-to-all-start = ((bf16[8,8,896]{2,1,0:T(8,128)(2,1)}), bf16[8,8,896]{2,1,0:T(8,128)(2,1)S(1)}, u32[]{:S(2)}, u32[]{:S(2)}) async-start(bf16[8,8,896]{2,1,0:T(8,128)(2,1)} %bitcast.9), calls=%async_computation | async-start | bytes 229376 | tf_op jit(solution)/shard_map/all_to_all | solution.py:239
  34.4 10.1 %all_gather.12 = bf16[32,896]{1,0:T(8,128)(2,1)S(1)} all-gather(bf16[8,896]{1,0:T(8,128)(2,1)} %get-tuple-element.8), channel_id=1, replica_groups=mesh['y_hi'=2,'x'=4,'core'=2,'z_hi'=8,'z_lo'=4,'y_lo'=2] {'x'}, dimensions={0}, use_global_device_ids=true | all-gather | bytes 71680 | tf_op jit(solution)/shard_map/all_gather | solution.py:286
  44.4 4.0 %all_gather.13 = bf16[64,896]{1,0:T(8,128)(2,1)} all-gather(bf16[32,896]{1,0:T(8,128)(2,1)S(1)} %all_gather.12), channel_id=1, replica_groups=mesh['y_hi'=2,'x'=4,'core'=2,'z_hi'=8,'z_lo'=4,'y_lo'=2] {'y_lo'}, dimensions={0}, use_global_device_ids=true | all-gather | bytes 172032 | tf_op jit(solution)/shard_map/all_gather | solution.py:286
  48.4 9.8 %all-to-all-done = bf16[8,8,896]{2,1,0:T(8,128)(2,1)S(1)} async-done(((bf16[8,8,896]{2,1,0:T(8,128)(2,1)}), bf16[8,8,896]{2,1,0:T(8,128)(2,1)S(1)}, u32[]{:S(2)}, u32[]{:S(2)}) %all-to-all-start) | async-done | bytes 114720 | tf_op jit(solution)/shard_map/all_to_all | solution.py:239
  58.2 0.8 reshape_tile.3
  59.0 0.0 copy-start
  59.0 6.8 %all-to-all-start.1 = ((bf16[4,64,896]{2,1,0:T(8,128)(2,1)}), bf16[4,64,896]{2,1,0:T(8,128)(2,1)}, u32[]{:S(2)}, u32[]{:S(2)}) async-start(bf16[4,64,896]{2,1,0:T(8,128)(2,1)} %reshape_tile.3), calls=%async_computation.1 | async-start | bytes 917504 | tf_op jit(solution)/shard_map/all_to_all | solution.py:239
  67.1 6.0 %all_gather.14 = bf16[128,896]{1,0:T(8,128)(2,1)S(1)} all-gather(bf16[64,896]{1,0:T(8,128)(2,1)} %all_gather.13), channel_id=1, replica_groups=mesh['y_hi'=2,'x'=4,'core'=2,'z_hi'=8,'z_lo'=4,'y_lo'=2] {'y_hi'}, dimensions={0}, use_global_device_ids=true | all-gather | bytes 344064 | tf_op jit(solution)/shard_map/all_gather | solution.py:286
  73.1 6.1 %all_gather.15.refs_0_ = bf16[256,896]{1,0:T(8,128)(2,1)} all-gather(bf16[128,896]{1,0:T(8,128)(2,1)S(1)} %all_gather.14), channel_id=1, replica_groups=mesh['y_hi'=2,'x'=4,'core'=2,'z_hi'=8,'z_lo'=4,'y_lo'=2] {'core'}, dimensions={0}, use_global_device_ids=true | all-gather | bytes 688128 | tf_op jit(solution)/shard_map/all_gather | solution.py:286
  79.2 0.0 copy-start.2
  79.3 0.0 all-to-all-done.1
  79.3 0.0 copy-start.1
  79.3 3.5 %tile.1 = bf16[256,896]{1,0:T(8,128)(2,1)} custom-call(bf16[256,896]{1,0:T(8,128)(2,1)} %all_gather.15.refs_0_, bf16[256,896]{1,0:T(8,128)(2,1)} %bitcast.2.refs_1_, s32[24,128]{1,0:T(8,128)} %bitcast.10, f32[1]{0:T(128)S(6)} %copy.11.refs_3_, f32[1]{0:T(128)S(6)} %copy.12.refs_4_), custom_call_target="tpu_custom_call" | custom-call | tf_op jit(solution)/shard_map/tile/pallas_call | solution.py:288
  82.7 18.8 %all_to_all.15 = bf16[32,8,896]{2,1,0:T(8,128)(2,1)S(1)} all-to-all(bf16[32,8,896]{2,1,0:T(8,128)(2,1)} %bitcast.7), channel_id=1, replica_groups=mesh['y_hi'=2,'x'=4,'core'=2,'z_hi'=8,'z_lo'=4,'y_lo'=2] {'core','y_hi',..., dimensions={0} | all-to-all | bytes 917504 | tf_op jit(solution)/shard_map/all_to_all | solution.py:239
  101.5 0.0 copy-done
  101.5 0.0 copy-done.2
  101.5 0.0 copy-done.1
  101.5 1.8 %grads.1 = (f32[3,1536]{1,0:T(4,128)}, f32[3,1152]{1,0:T(4,128)}) custom-call(bf16[256,896]{1,0:T(8,128)(2,1)S(1)} %bitcast.6, f32[8,1152]{1,0:T(8,128)S(1)} %copy-done.1, bf16[1536,1152]{1,0:T(8,128)(2,1)S(1)} %copy-done, bf16[3,1152]{1,0:T(4,128)(2,1)S(1)} %copy-done.2), custom_call_target="tpu_custom_call" | custom-call | tf_op jit(solution)/shard_map/grads/pallas_call | solution.py:303
Async XLA Ops:
  5.4 52.7 %all-to-all-start = ((bf16[8,8,896]{2,1,0:T(8,128)(2,1)}), bf16[8,8,896]{2,1,0:T(8,128)(2,1)S(1)}, u32[]{:S(2)}, u32[]{:S(2)}) async-start(bf16[8,8,896]{2,1,0:T(8,128)(2,1)} %bitcast.9), calls=%async_computation | async-start | bytes 229376 | tf_op jit(solution)/shard_map/all_to_all | solution.py:239
  59.0 42.5 %copy-start = (bf16[1536,1152]{1,0:T(8,128)(2,1)S(1)}, bf16[1536,1152]{1,0:T(8,128)(2,1)}, u32[]{:S(2)}) copy-start(bf16[1536,1152]{1,0:T(8,128)(2,1)} %projection.1) | copy-start | bytes 10616836
  59.0 20.3 %all-to-all-start.1 = ((bf16[4,64,896]{2,1,0:T(8,128)(2,1)}), bf16[4,64,896]{2,1,0:T(8,128)(2,1)}, u32[]{:S(2)}, u32[]{:S(2)}) async-start(bf16[4,64,896]{2,1,0:T(8,128)(2,1)} %reshape_tile.3), calls=%async_computation.1 | async-start | bytes 917504 | tf_op jit(solution)/shard_map/all_to_all | solution.py:239
  79.2 22.2 %copy-start.2 = (bf16[3,1152]{1,0:T(4,128)(2,1)S(1)}, bf16[3,1152]{1,0:T(4,128)(2,1)}, u32[]{:S(2)}) copy-start(bf16[3,1152]{1,0:T(4,128)(2,1)} %text.1) | copy-start | bytes 20740
  79.3 22.2 %copy-start.1 = (f32[8,1152]{1,0:T(8,128)S(1)}, f32[8,1152]{1,0:T(8,128)}, u32[]{:S(2)}) copy-start(f32[8,1152]{1,0:T(8,128)} %get-tuple-element.11.projected) | copy-start | bytes 110596

commit v6 on v5

--- a/solution.py
+++ b/solution.py
@@ -10,15 +10,16 @@
 H = 16
 HD = 96
 
-AXES = ("y_hi", "x", "core", "z_hi", "z_lo", "y_lo")
-SIZES = (2, 4, 2, 8, 4, 2)
-PLANE = ("core", "y_hi", "y_lo", "x")
+AXES = ("y_hi", "x_hi", "x_lo", "core", "z_hi", "z_lo", "y_lo")
+SIZES = (2, 2, 2, 2, 8, 4, 2)
+PLANE = ("core", "y_hi", "x_hi", "y_lo", "x_lo")
 
 BLOCK = 8
 HALF = 4
 LANES = 128
 SPARE = (3, 7)
 FILLED = (0, 1, 2, 4, 5, 6)
+PARTS = 4
 
 epsilon = 1e-06
 VMEM = pl.BlockSpec(memory_space=pltpu.VMEM)
@@ -89,16 +90,20 @@
     units,
     arrived,
 ):
+    deep = projection.shape[0] // PARTS
     fetches = [
         pltpu.make_async_copy(source, target, arrived.at[i])
         for i, (source, target) in enumerate(
-            (
+            [
                 (lengths_at, lengths),
                 (keys_at, keys),
                 (values_at, values),
                 (text_at, text),
-                (projection_at, projection),
-            )
+            ]
+            + [
+                (projection_at.at[pl.ds(part * deep, deep)], projection.at[pl.ds(part * deep, deep)])
+                for part in range(PARTS)
+            ]
         )
     ]
     for fetch in fetches:
@@ -130,11 +135,17 @@
     for image in range(lengths.shape[1]):
         part = mixed[image * H : (image + 1) * H]
         pooled[image : image + 1, :] = jnp.sum(jnp.where(own, part, 0.0), axis=0, keepdims=True)
+    proj = jnp.zeros((2 * BLOCK, projected.shape[1]), jnp.float32)
+    for part in range(PARTS):
+        fetches[4 + part].wait()
+        here = slice(part * deep, (part + 1) * deep)
+        proj += jnp.dot(
+            pooled[:, here].astype(jnp.bfloat16),
+            projection[here, :],
+            preferred_element_type=jnp.float32,
+        )
+    proj = proj[:BLOCK]
     fetches[3].wait()
-    fetches[4].wait()
-    proj = jnp.dot(
-        pooled[...].astype(jnp.bfloat16), projection[...], preferred_element_type=jnp.float32
-    )[:BLOCK]
     projected[...] = proj
     units[...] = proj / row_norm(proj)
     text_wide = text[...].astype(jnp.float32)
@@ -272,7 +283,7 @@
             pltpu.VMEM(text_embeds.shape, text_embeds.dtype),
             pltpu.VMEM((2 * BLOCK, depth), jnp.float32),
             pltpu.VMEM((BLOCK, width), jnp.float32),
-            pltpu.SemaphoreType.DMA((5,)),
+            pltpu.SemaphoreType.DMA((4 + PARTS,)),
         ],
         compiler_params=pltpu.CompilerParams(vmem_limit_bytes=60 << 20),
         name="units",
@@ -281,7 +292,7 @@
     far = exchange(copies, "z_hi")
     plane = block
     for step, axis in enumerate(PLANE[::-1]):
-        if step == 2:
+        if step == 3:
             far, plane = lax.optimization_barrier((far, plane))
         plane = lax.all_gather(plane, axis, axis=0, tiled=True)
     line = exchange(jnp.tile(far, (lax.axis_size("z_lo"), 1)), "z_lo")

time: 104 us -> 104 us (level)
  waiting for transfers between devices: 9.77 us -> 11.2 us
    all_to_all x2, waiting for transfers between devices: 9.77 us -> 11.2 us  [exchange(): lax.all_to_all(rows.reshape(shape), axis, 0, 0, tiled=True)]
    all_gather x4 -> x5, blocking collectives: 26.2 us -> 24.8 us  [shards(): plane = lax.all_gather(plane, axis, axis=0, tiled=True)]
where the time goes in v6:
time: 104 us
  blocking collectives  44 us (42%)
  starting transfers between devices  35.7 us (34%)
  waiting for transfers between devices  11.2 us (11%)
  Pallas kernels  10.1 us (10%)
  between operations  1.95 us (2%)
    all_to_all x2, starting transfers between devices, exchange(): lax.all_to_all(rows.reshape(shape), axis, 0, 0, tiled=True)  35.7 us
    all_gather x5, blocking collectives, shards(): plane = lax.all_gather(plane, axis, axis=0, tiled=True)  24.8 us
    all_to_all x1, blocking collectives, exchange(): lax.all_to_all(rows.reshape(shape), axis, 0, 0, tiled=True)  19.3 us
    all_to_all x2, waiting for transfers between devices, exchange(): lax.all_to_all(rows.reshape(shape), axis, 0, 0, tiled=True)  11.2 us
    pallas_call x1, Pallas kernels, shards(): pl.pallas_call(units_kernel, out_shape=(jax.ShapeDtypeStruct((BLOCK, narr...  4.79 us
    pallas_call x1, Pallas kernels, shards(): pl.pallas_call(lambda *refs: tile_kernel(count, *refs), out_shape=jax.Sha...  3.57 us
  transfers between devices with their start and end apart: 2, of which 1 were waited for; matrix products, arithmetic and copies ran while one was open for 0% of the time, Pallas kernels for 0%

profile of v6, /device:TPU:1, one launch (start us, length us, event | category | flops | bytes accessed | tf_op | source)
XLA Modules:
  0.0 103.8 jit_solution(9597711648886028525)
XLA Ops:
  0.6 4.8 %units.1 = (bf16[8,896]{1,0:T(8,128)(2,1)}, bf16[64,896]{1,0:T(8,128)(2,1)}, f32[8,1152]{1,0:T(8,128)}) custom-call(s32[1,3]{1,0:T(1,128)} %lengths_at.1, bf16[384,1536]{1,0:T(8,128)(2,1)} %keys_at.1, bf16[384,1536]{1,0:T(8,128)(2,1)} %values_at.1, bf16[1536]{0:T(1024)(128)(2,1)} %probe.1, bf16[1536,1152]{1,0:T(8,128)(2,1)} %projection.1, bf16[3,1152]{1,0:T(4,128)(2,1)} %text.1), custom_call_target="tpu_custom_call" | custom-call | tf_op jit(solution)/shard_map/units/pallas_call | solution.py:269
  5.4 28.9 %all-to-all-start = ((bf16[8,8,896]{2,1,0:T(8,128)(2,1)}), bf16[8,8,896]{2,1,0:T(8,128)(2,1)S(1)}, u32[]{:S(2)}, u32[]{:S(2)}) async-start(bf16[8,8,896]{2,1,0:T(8,128)(2,1)} %bitcast.9), calls=%async_computation | async-start | bytes 229376 | tf_op jit(solution)/shard_map/all_to_all | solution.py:250
  34.3 3.5 %all_gather.15 = bf16[16,896]{1,0:T(8,128)(2,1)S(1)} all-gather(bf16[8,896]{1,0:T(8,128)(2,1)} %get-tuple-element.8), channel_id=1, replica_groups=mesh['y_hi'=2,'x_hi'=2,'x_lo'=2,'core'=2,'z_hi'=8,'z_lo'=4,'y_lo'=2] {'x..., dimensions={0}, use_global_device_ids=true | all-gather | bytes 43008 | tf_op jit(solution)/shard_map/all_gather | solution.py:297
  37.8 3.7 %all_gather.16 = bf16[32,896]{1,0:T(8,128)(2,1)S(1)} all-gather(bf16[16,896]{1,0:T(8,128)(2,1)S(1)} %all_gather.15), channel_id=1, replica_groups=mesh['y_hi'=2,'x_hi'=2,'x_lo'=2,'core'=2,'z_hi'=8,'z_lo'=4,'y_lo'=2] {'y..., dimensions={0}, use_global_device_ids=true | all-gather | bytes 86016 | tf_op jit(solution)/shard_map/all_gather | solution.py:297
  41.5 5.5 %all_gather.17 = bf16[64,896]{1,0:T(8,128)(2,1)} all-gather(bf16[32,896]{1,0:T(8,128)(2,1)S(1)} %all_gather.16), channel_id=1, replica_groups=mesh['y_hi'=2,'x_hi'=2,'x_lo'=2,'core'=2,'z_hi'=8,'z_lo'=4,'y_lo'=2] {'x..., dimensions={0}, use_global_device_ids=true | all-gather | bytes 172032 | tf_op jit(solution)/shard_map/all_gather | solution.py:297
  47.0 11.2 %all-to-all-done = bf16[8,8,896]{2,1,0:T(8,128)(2,1)S(1)} async-done(((bf16[8,8,896]{2,1,0:T(8,128)(2,1)}), bf16[8,8,896]{2,1,0:T(8,128)(2,1)S(1)}, u32[]{:S(2)}, u32[]{:S(2)}) %all-to-all-start) | async-done | bytes 114720 | tf_op jit(solution)/shard_map/all_to_all | solution.py:250
  58.2 0.8 reshape_tile.3
  59.0 0.0 copy-start
  59.0 6.8 %all-to-all-start.1 = ((bf16[4,64,896]{2,1,0:T(8,128)(2,1)}), bf16[4,64,896]{2,1,0:T(8,128)(2,1)}, u32[]{:S(2)}, u32[]{:S(2)}) async-start(bf16[4,64,896]{2,1,0:T(8,128)(2,1)} %reshape_tile.3), calls=%async_computation.1 | async-start | bytes 917504 | tf_op jit(solution)/shard_map/all_to_all | solution.py:250
  67.1 6.0 %all_gather.18 = bf16[128,896]{1,0:T(8,128)(2,1)S(1)} all-gather(bf16[64,896]{1,0:T(8,128)(2,1)} %all_gather.17), channel_id=1, replica_groups=mesh['y_hi'=2,'x_hi'=2,'x_lo'=2,'core'=2,'z_hi'=8,'z_lo'=4,'y_lo'=2] {'y..., dimensions={0}, use_global_device_ids=true | all-gather | bytes 344064 | tf_op jit(solution)/shard_map/all_gather | solution.py:297
  73.1 6.1 %all_gather.19.refs_0_ = bf16[256,896]{1,0:T(8,128)(2,1)} all-gather(bf16[128,896]{1,0:T(8,128)(2,1)S(1)} %all_gather.18), channel_id=1, replica_groups=mesh['y_hi'=2,'x_hi'=2,'x_lo'=2,'core'=2,'z_hi'=8,'z_lo'=4,'y_lo'=2] {'c..., dimensions={0}, use_global_device_ids=true | all-gather | bytes 688128 | tf_op jit(solution)/shard_map/all_gather | solution.py:297
  79.2 0.0 copy-start.2
  79.2 0.0 all-to-all-done.1
  79.2 0.0 copy-start.1
  79.2 3.6 %tile.1 = bf16[256,896]{1,0:T(8,128)(2,1)} custom-call(bf16[256,896]{1,0:T(8,128)(2,1)} %all_gather.19.refs_0_, bf16[256,896]{1,0:T(8,128)(2,1)} %bitcast.2.refs_1_, s32[24,128]{1,0:T(8,128)} %bitcast.10, f32[1]{0:T(128)S(6)} %copy.11.refs_3_, f32[1]{0:T(128)S(6)} %copy.12.refs_4_), custom_call_target="tpu_custom_call" | custom-call | tf_op jit(solution)/shard_map/tile/pallas_call | solution.py:299
  82.8 19.3 %all_to_all.15 = bf16[32,8,896]{2,1,0:T(8,128)(2,1)S(1)} all-to-all(bf16[32,8,896]{2,1,0:T(8,128)(2,1)} %bitcast.7), channel_id=1, replica_groups=mesh['y_hi'=2,'x_hi'=2,'x_lo'=2,'core'=2,'z_hi'=8,'z_lo'=4,'y_lo'=2] {'c..., dimensions={0} | all-to-all | bytes 917504 | tf_op jit(solution)/shard_map/all_to_all | solution.py:250
  102.1 0.0 copy-done
  102.1 0.0 copy-done.2
  102.1 0.0 copy-done.1
  102.1 1.8 %grads.1 = (f32[3,1536]{1,0:T(4,128)}, f32[3,1152]{1,0:T(4,128)}) custom-call(bf16[256,896]{1,0:T(8,128)(2,1)S(1)} %bitcast.6, f32[8,1152]{1,0:T(8,128)S(1)} %copy-done.1, bf16[1536,1152]{1,0:T(8,128)(2,1)S(1)} %copy-done, bf16[3,1152]{1,0:T(4,128)(2,1)S(1)} %copy-done.2), custom_call_target="tpu_custom_call" | custom-call | tf_op jit(solution)/shard_map/grads/pallas_call | solution.py:314
Async XLA Ops:
  5.4 52.8 %all-to-all-start = ((bf16[8,8,896]{2,1,0:T(8,128)(2,1)}), bf16[8,8,896]{2,1,0:T(8,128)(2,1)S(1)}, u32[]{:S(2)}, u32[]{:S(2)}) async-start(bf16[8,8,896]{2,1,0:T(8,128)(2,1)} %bitcast.9), calls=%async_computation | async-start | bytes 229376 | tf_op jit(solution)/shard_map/all_to_all | solution.py:250
  59.0 43.1 %copy-start = (bf16[1536,1152]{1,0:T(8,128)(2,1)S(1)}, bf16[1536,1152]{1,0:T(8,128)(2,1)}, u32[]{:S(2)}) copy-start(bf16[1536,1152]{1,0:T(8,128)(2,1)} %projection.1) | copy-start | bytes 10616836
  59.0 20.2 %all-to-all-start.1 = ((bf16[4,64,896]{2,1,0:T(8,128)(2,1)}), bf16[4,64,896]{2,1,0:T(8,128)(2,1)}, u32[]{:S(2)}, u32[]{:S(2)}) async-start(bf16[4,64,896]{2,1,0:T(8,128)(2,1)} %reshape_tile.3), calls=%async_computation.1 | async-start | bytes 917504 | tf_op jit(solution)/shard_map/all_to_all | solution.py:250
  79.2 22.8 %copy-start.2 = (bf16[3,1152]{1,0:T(4,128)(2,1)S(1)}, bf16[3,1152]{1,0:T(4,128)(2,1)}, u32[]{:S(2)}) copy-start(bf16[3,1152]{1,0:T(4,128)(2,1)} %text.1) | copy-start | bytes 20740
  79.2 22.8 %copy-start.1 = (f32[8,1152]{1,0:T(8,128)S(1)}, f32[8,1152]{1,0:T(8,128)}, u32[]{:S(2)}) copy-start(f32[8,1152]{1,0:T(8,128)} %get-tuple-element.11.projected) | copy-start | bytes 110596

commit v7 on v6

--- a/solution.py
+++ b/solution.py
@@ -190,7 +190,9 @@
     return number
 
 
-def tile_kernel(count, plane, line, groups, scale, bias, parts):
+def tile_kernel(count, plane, *refs):
+    *lines, groups, scale, bias, parts = refs
+    line = jnp.concatenate([unpack_rows(rows[...]) for rows in lines])
     sizes = dict((axis, lax.axis_size(axis)) for axis in AXES)
     place = dict((axis, lax.axis_index(axis)) for axis in AXES)
     at = lax.broadcasted_iota(jnp.int32, (plane.shape[0], 1), 0)
@@ -203,16 +205,17 @@
     plane_kind = at % BLOCK // HALF
     at = lax.broadcasted_iota(jnp.int32, (1, line.shape[0]), 1)
     member, slot = at // BLOCK, jnp.minimum(at % HALF, count - 1)
-    there = dict(place, z_hi=member % sizes["z_hi"], z_lo=member // sizes["z_hi"])
+    behind = place["z_lo"] - member // sizes["z_hi"] + sizes["z_lo"]
+    there = dict(place, z_hi=member % sizes["z_hi"], z_lo=behind % sizes["z_lo"])
     line_at = device(there, sizes) * count + slot
     line_kind = at % BLOCK // HALF
     plane_ids = pick(groups[...], plane_at, 0)
     line_ids = pick(groups[...], line_at, 1)
 
-    plane_rows, line_rows = unpack_rows(plane[...]), unpack_rows(line[...])
+    plane_rows = unpack_rows(plane[...])
     logits = (
         lax.dot_general(
-            plane_rows, line_rows, (((1,), (1,)), ((), ())), preferred_element_type=jnp.float32
+            plane_rows, line, (((1,), (1,)), ((), ())), preferred_element_type=jnp.float32
         )
         * scale[0]
         + bias[0]
@@ -220,7 +223,7 @@
     labels = jnp.where(plane_ids == line_ids, 1.0, -1.0)
     coeffs = -labels * jax.nn.sigmoid(-labels * logits) * scale[0]
     coeffs = jnp.where(plane_kind != line_kind, coeffs, 0.0).astype(jnp.bfloat16)
-    wide = jnp.dot(coeffs, line_rows, preferred_element_type=jnp.float32)
+    wide = jnp.dot(coeffs, line, preferred_element_type=jnp.float32)
     packed = pack(wide.reshape(-1, BLOCK, wide.shape[1]))
     parts[...] = packed.reshape(parts.shape).astype(jnp.bfloat16)
 
@@ -291,21 +294,24 @@
 
     far = exchange(copies, "z_hi")
     plane = block
-    for step, axis in enumerate(PLANE[::-1]):
-        if step == 3:
-            far, plane = lax.optimization_barrier((far, plane))
+    for axis in PLANE[::-1]:
         plane = lax.all_gather(plane, axis, axis=0, tiled=True)
-    line = exchange(jnp.tile(far, (lax.axis_size("z_lo"), 1)), "z_lo")
+    far, plane = lax.optimization_barrier((far, plane))
+    n_near = lax.axis_size("z_lo")
+    lines = [far]
+    for ahead in range(1, n_near):
+        route = [(i, (i + ahead) % n_near) for i in range(n_near)]
+        lines.append(lax.ppermute(far, "z_lo", route))
     parts = pl.pallas_call(
         lambda *refs: tile_kernel(count, *refs),
         out_shape=jax.ShapeDtypeStruct((n_plane * BLOCK, narrow), jnp.bfloat16),
-        in_specs=[VMEM] * 3 + [SMEM] * 2,
+        in_specs=[VMEM] * (2 + n_near) + [SMEM] * 2,
         out_specs=VMEM,
-        compiler_params=pltpu.CompilerParams(vmem_limit_bytes=60 << 20),
+        compiler_params=PARAMS,
         name="tile",
     )(
         plane,
-        line,
+        *lines,
         pair_group.reshape(-1, 128),
         logit_scale,
         logit_bias,

time: 104 us -> 104 us (level)
  waiting for transfers between devices: 11.2 us -> 3.51 us
  starting transfers between devices: 35.7 us -> 39.8 us
  blocking collectives: 44 us -> 47 us
    all_to_all x2 -> x1, waiting for transfers between devices: 11.2 us -> 0.01 us  [exchange(): lax.all_to_all(rows.reshape(shape), axis, 0, 0, tiled=True)]
    ppermute x0 -> x3, starting transfers between devices: none -> 10.9 us  [shards(): lines.append(lax.ppermute(far, 'z_lo', route))]
    all_to_all x2 -> x1, starting transfers between devices: 35.7 us -> 28.9 us  [exchange(): lax.all_to_all(rows.reshape(shape), axis, 0, 0, tiled=True)]
    ppermute x0 -> x3, waiting for transfers between devices: none -> 3.51 us  [shards(): lines.append(lax.ppermute(far, 'z_lo', route))]
    all_to_all x1, blocking collectives: 19.3 us -> 21.5 us  [exchange(): lax.all_to_all(rows.reshape(shape), axis, 0, 0, tiled=True)]
    unnamed x6 -> x10, local copies, waits for them, and re-layouts: 0.01 us -> 1.74 us
    pallas_call x1, Pallas kernels: 3.57 us -> 2.53 us  [shards(): pl.pallas_call(lambda *refs: tile_kernel(count, *refs), out_shape=jax.Sha...]
  transfers between devices with their start and end apart: 2 -> 4, of which waited for: 1 -> 1; matrix products, arithmetic and copies ran while one was open for 0% -> 0% of each run, Pallas kernels for 0% -> 0%
where the time goes in v7:
time: 104 us; the launch traced here: 103 us
  blocking collectives  47 us (45%)
  starting transfers between devices  39.8 us (38%)
  Pallas kernels  9.09 us (9%)
  waiting for transfers between devices  3.51 us (3%)
  between operations  1.99 us (2%)
  local copies, waits for them, and re-layouts  1.74 us (2%)
    all_to_all x1, starting transfers between devices, exchange(): lax.all_to_all(rows.reshape(shape), axis, 0, 0, tiled=True)  28.9 us
    all_gather x5, blocking collectives, shards(): plane = lax.all_gather(plane, axis, axis=0, tiled=True)  25.4 us
    all_to_all x1, blocking collectives, exchange(): lax.all_to_all(rows.reshape(shape), axis, 0, 0, tiled=True)  21.5 us
    ppermute x3, starting transfers between devices, shards(): lines.append(lax.ppermute(far, 'z_lo', route))  10.9 us
    pallas_call x1, Pallas kernels, shards(): pl.pallas_call(units_kernel, out_shape=(jax.ShapeDtypeStruct((BLOCK, narr...  4.8 us
    ppermute x3, waiting for transfers between devices, shards(): lines.append(lax.ppermute(far, 'z_lo', route))  3.51 us
    pallas_call x1, Pallas kernels, shards(): pl.pallas_call(lambda *refs: tile_kernel(count, *refs), out_shape=jax.Sha...  2.53 us
  transfers between devices with their start and end apart: 4, of which 1 were waited for; matrix products, arithmetic and copies ran while one was open for 0% of the time, Pallas kernels for 0%

profile of v7, /device:TPU:1, one launch (start us, length us, event | category | flops | bytes accessed | tf_op | source)
XLA Modules:
  0.0 103.1 jit_solution(16760839170028465324)
XLA Ops:
  0.6 4.8 %units.1 = (bf16[8,896]{1,0:T(8,128)(2,1)}, bf16[64,896]{1,0:T(8,128)(2,1)}, f32[8,1152]{1,0:T(8,128)}) custom-call(s32[1,3]{1,0:T(1,128)} %lengths_at.1, bf16[384,1536]{1,0:T(8,128)(2,1)} %keys_at.1, bf16[384,1536]{1,0:T(8,128)(2,1)} %values_at.1, bf16[1536]{0:T(1024)(128)(2,1)} %probe.1, bf16[1536,1152]{1,0:T(8,128)(2,1)} %projection.1, bf16[3,1152]{1,0:T(4,128)(2,1)} %text.1), custom_call_target="tpu_custom_call" | custom-call | tf_op jit(solution)/shard_map/units/pallas_call | solution.py:272
  5.4 28.9 %all-to-all-start = ((bf16[8,8,896]{2,1,0:T(8,128)(2,1)}), bf16[8,8,896]{2,1,0:T(8,128)(2,1)}, u32[]{:S(2)}, u32[]{:S(2)}) async-start(bf16[8,8,896]{2,1,0:T(8,128)(2,1)} %bitcast.8), calls=%async_computation | async-start | bytes 229376 | tf_op jit(solution)/shard_map/all_to_all | solution.py:253
  34.3 0.0 copy-start.3
  34.3 3.5 %all_gather.15 = bf16[16,896]{1,0:T(8,128)(2,1)S(1)} all-gather(bf16[8,896]{1,0:T(8,128)(2,1)} %get-tuple-element.8), channel_id=1, replica_groups=mesh['y_hi'=2,'x_hi'=2,'x_lo'=2,'core'=2,'z_hi'=8,'z_lo'=4,'y_lo'=2] {'x..., dimensions={0}, use_global_device_ids=true | all-gather | bytes 43008 | tf_op jit(solution)/shard_map/all_gather | solution.py:298
  37.8 0.0 copy-start
  37.8 3.9 %all_gather.16 = bf16[32,896]{1,0:T(8,128)(2,1)S(1)} all-gather(bf16[16,896]{1,0:T(8,128)(2,1)S(1)} %all_gather.15), channel_id=1, replica_groups=mesh['y_hi'=2,'x_hi'=2,'x_lo'=2,'core'=2,'z_hi'=8,'z_lo'=4,'y_lo'=2] {'y..., dimensions={0}, use_global_device_ids=true | all-gather | bytes 86016 | tf_op jit(solution)/shard_map/all_gather | solution.py:298
  41.7 5.6 %all_gather.17 = bf16[64,896]{1,0:T(8,128)(2,1)S(1)} all-gather(bf16[32,896]{1,0:T(8,128)(2,1)S(1)} %all_gather.16), channel_id=1, replica_groups=mesh['y_hi'=2,'x_hi'=2,'x_lo'=2,'core'=2,'z_hi'=8,'z_lo'=4,'y_lo'=2] {'x..., dimensions={0}, use_global_device_ids=true | all-gather | bytes 172032 | tf_op jit(solution)/shard_map/all_gather | solution.py:298
  47.3 6.2 %all_gather.18 = bf16[128,896]{1,0:T(8,128)(2,1)S(1)} all-gather(bf16[64,896]{1,0:T(8,128)(2,1)S(1)} %all_gather.17), channel_id=1, replica_groups=mesh['y_hi'=2,'x_hi'=2,'x_lo'=2,'core'=2,'z_hi'=8,'z_lo'=4,'y_lo'=2] {'y..., dimensions={0}, use_global_device_ids=true | all-gather | bytes 344064 | tf_op jit(solution)/shard_map/all_gather | solution.py:298
  53.6 6.2 %all_gather.19.refs_0_ = bf16[256,896]{1,0:T(8,128)(2,1)} all-gather(bf16[128,896]{1,0:T(8,128)(2,1)S(1)} %all_gather.18), channel_id=1, replica_groups=mesh['y_hi'=2,'x_hi'=2,'x_lo'=2,'core'=2,'z_hi'=8,'z_lo'=4,'y_lo'=2] {'c..., dimensions={0}, use_global_device_ids=true | all-gather | bytes 688128 | tf_op jit(solution)/shard_map/all_gather | solution.py:298
  59.8 0.0 all-to-all-done
  59.8 3.5 %collective-permute-start.2 = (bf16[64,896]{1,0:T(8,128)(2,1)}, bf16[64,896]{1,0:T(8,128)(2,1)S(1)}, u32[]{:S(2)}, u32[]{:S(2)}) collective-permute-start(bf16[64,896]{1,0:T(8,128)(2,1)} %bitcast.1.refs_1_), channel_id=1, source_target_pairs={{0,6},{2,0},{4,2},{6,4},{1,7},{3,1},{5,3},{7,5},{8,14},{10,8},{12,... | collective-permute-start | bytes 344072 | tf_op jit(solution)/shard_map/ppermute | solution.py:304
  63.3 4.4 %collective-permute-start.1 = (bf16[64,896]{1,0:T(8,128)(2,1)}, bf16[64,896]{1,0:T(8,128)(2,1)S(1)}, u32[]{:S(2)}, u32[]{:S(2)}) collective-permute-start(bf16[64,896]{1,0:T(8,128)(2,1)} %bitcast.1.refs_1_), channel_id=1, source_target_pairs={{0,4},{2,6},{4,0},{6,2},{1,5},{3,7},{5,1},{7,3},{8,12},{10,14},{12... | collective-permute-start | bytes 344072 | tf_op jit(solution)/shard_map/ppermute | solution.py:304
  67.8 2.9 %collective-permute-start = (bf16[64,896]{1,0:T(8,128)(2,1)}, bf16[64,896]{1,0:T(8,128)(2,1)S(1)}, u32[]{:S(2)}, u32[]{:S(2)}) collective-permute-start(bf16[64,896]{1,0:T(8,128)(2,1)} %bitcast.1.refs_1_), channel_id=1, source_target_pairs={{0,2},{2,4},{4,6},{6,0},{1,3},{3,5},{5,7},{7,1},{8,10},{10,12},{12... | collective-permute-start | bytes 344072 | tf_op jit(solution)/shard_map/ppermute | solution.py:304
  72.0 0.0 collective-permute-done.2.refs_4_
  72.1 0.0 collective-permute-done.1.refs_3_
  72.1 3.5 %collective-permute-done.refs_2_ = bf16[64,896]{1,0:T(8,128)(2,1)S(1)} collective-permute-done((bf16[64,896]{1,0:T(8,128)(2,1)}, bf16[64,896]{1,0:T(8,128)(2,1)S(1)}, u32[]{:S(2)}, u32[]{:S(2)}) %collective-permute-start) | collective-permute-done | bytes 114720 | tf_op jit(solution)/shard_map/ppermute | solution.py:304
  75.6 0.0 copy-start.1
  75.6 1.0 copy-done.1
  76.6 0.0 copy-start.4
  76.6 0.7 copy-done.4
  77.3 0.0 copy-start.2
  77.3 2.5 %tile.1 = bf16[256,896]{1,0:T(8,128)(2,1)S(1)} custom-call(bf16[256,896]{1,0:T(8,128)(2,1)S(1)} %copy-done.1, bf16[64,896]{1,0:T(8,128)(2,1)} %bitcast.1.refs_1_, bf16[64,896]{1,0:T(8,128)(2,1)S(1)} %collective-permute-done.refs_2_, bf16[64,896]{1,0:T(8,128)(2,1)S(1)} %collective-permute-done.1.refs_3_, bf16[64,896]{1,0:T(8,128)(2,1)S(1)} %collective-permute-done.2.refs_4_, ...), custom_call_target="tpu_custom_call" | custom-call | tf_op jit(solution)/shard_map/tile/pallas_call | solution.py:305
  79.8 21.5 %all_to_all.10 = bf16[32,8,896]{2,1,0:T(8,128)(2,1)S(1)} all-to-all(bf16[32,8,896]{2,1,0:T(8,128)(2,1)S(1)} %bitcast.5), channel_id=1, replica_groups=mesh['y_hi'=2,'x_hi'=2,'x_lo'=2,'core'=2,'z_hi'=8,'z_lo'=4,'y_lo'=2] {'c..., dimensions={0} | all-to-all | bytes 917504 | tf_op jit(solution)/shard_map/all_to_all | solution.py:253
  101.3 0.0 copy-done.3
  101.3 0.0 copy-done
  101.4 0.0 copy-done.2
  101.4 1.8 %grads.1 = (f32[3,1536]{1,0:T(4,128)}, f32[3,1152]{1,0:T(4,128)}) custom-call(bf16[256,896]{1,0:T(8,128)(2,1)S(1)} %bitcast.6, f32[8,1152]{1,0:T(8,128)S(1)} %copy-done.2, bf16[1536,1152]{1,0:T(8,128)(2,1)S(1)} %copy-done, bf16[3,1152]{1,0:T(4,128)(2,1)S(1)} %copy-done.3), custom_call_target="tpu_custom_call" | custom-call | tf_op jit(solution)/shard_map/grads/pallas_call | solution.py:320
Async XLA Ops:
  5.4 54.4 %all-to-all-start = ((bf16[8,8,896]{2,1,0:T(8,128)(2,1)}), bf16[8,8,896]{2,1,0:T(8,128)(2,1)}, u32[]{:S(2)}, u32[]{:S(2)}) async-start(bf16[8,8,896]{2,1,0:T(8,128)(2,1)} %bitcast.8), calls=%async_computation | async-start | bytes 229376 | tf_op jit(solution)/shard_map/all_to_all | solution.py:253
  34.3 67.0 %copy-start.3 = (bf16[3,1152]{1,0:T(4,128)(2,1)S(1)}, bf16[3,1152]{1,0:T(4,128)(2,1)}, u32[]{:S(2)}) copy-start(bf16[3,1152]{1,0:T(4,128)(2,1)} %text.1) | copy-start | bytes 20740
  37.8 63.5 %copy-start = (bf16[1536,1152]{1,0:T(8,128)(2,1)S(1)}, bf16[1536,1152]{1,0:T(8,128)(2,1)}, u32[]{:S(2)}) copy-start(bf16[1536,1152]{1,0:T(8,128)(2,1)} %projection.1) | copy-start | bytes 10616836
  59.8 12.3 %collective-permute-start.2 = (bf16[64,896]{1,0:T(8,128)(2,1)}, bf16[64,896]{1,0:T(8,128)(2,1)S(1)}, u32[]{:S(2)}, u32[]{:S(2)}) collective-permute-start(bf16[64,896]{1,0:T(8,128)(2,1)} %bitcast.1.refs_1_), channel_id=1, source_target_pairs={{0,6},{2,0},{4,2},{6,4},{1,7},{3,1},{5,3},{7,5},{8,14},{10,8},{12,... | collective-permute-start | bytes 344072 | tf_op jit(solution)/shard_map/ppermute | solution.py:304
  63.3 8.7 %collective-permute-start.1 = (bf16[64,896]{1,0:T(8,128)(2,1)}, bf16[64,896]{1,0:T(8,128)(2,1)S(1)}, u32[]{:S(2)}, u32[]{:S(2)}) collective-permute-start(bf16[64,896]{1,0:T(8,128)(2,1)} %bitcast.1.refs_1_), channel_id=1, source_target_pairs={{0,4},{2,6},{4,0},{6,2},{1,5},{3,7},{5,1},{7,3},{8,12},{10,14},{12... | collective-permute-start | bytes 344072 | tf_op jit(solution)/shard_map/ppermute | solution.py:304
  67.8 7.8 %collective-permute-start = (bf16[64,896]{1,0:T(8,128)(2,1)}, bf16[64,896]{1,0:T(8,128)(2,1)S(1)}, u32[]{:S(2)}, u32[]{:S(2)}) collective-permute-start(bf16[64,896]{1,0:T(8,128)(2,1)} %bitcast.1.refs_1_), channel_id=1, source_target_pairs={{0,2},{2,4},{4,6},{6,0},{1,3},{3,5},{5,7},{7,1},{8,10},{10,12},{12... | collective-permute-start | bytes 344072 | tf_op jit(solution)/shard_map/ppermute | solution.py:304
  75.6 1.0 copy-start.1
  76.6 0.7 copy-start.4
  77.3 24.1 %copy-start.2 = (f32[8,1152]{1,0:T(8,128)S(1)}, f32[8,1152]{1,0:T(8,128)}, u32[]{:S(2)}) copy-start(f32[8,1152]{1,0:T(8,128)} %get-tuple-element.11.projected) | copy-start | bytes 110596

commit v8 on v7

--- a/solution.py
+++ b/solution.py
@@ -294,9 +294,10 @@
 
     far = exchange(copies, "z_hi")
     plane = block
-    for axis in PLANE[::-1]:
+    for axis in PLANE[:0:-1]:
         plane = lax.all_gather(plane, axis, axis=0, tiled=True)
     far, plane = lax.optimization_barrier((far, plane))
+    plane = lax.all_gather(plane, PLANE[0], axis=0, tiled=True)
     n_near = lax.axis_size("z_lo")
     lines = [far]
     for ahead in range(1, n_near):

time: 104 us -> 102 us (0.981)
  local copies, waits for them, and re-layouts: 1.74 us -> 0.02 us
  blocking collectives: 47 us -> 45.5 us
  starting transfers between devices: 39.8 us -> 41.3 us
    all_gather x5 -> x4, blocking collectives: 25.4 us -> 19.2 us  [shards(): plane = lax.all_gather(plane, axis, axis=0, tiled=True)]
    all_gather x0 -> x1, blocking collectives: none -> 4.82 us  [shards(): plane = lax.all_gather(plane, PLANE[0], axis=0, tiled=True)]
    ppermute x3, waiting for transfers between devices: 3.51 us -> 0.01 us  [shards(): lines.append(lax.ppermute(far, 'z_lo', route))]
    all_to_all x1, waiting for transfers between devices: 0.01 us -> 3.44 us  [exchange(): lax.all_to_all(rows.reshape(shape), axis, 0, 0, tiled=True)]
    unnamed x10 -> x8, local copies, waits for them, and re-layouts: 1.74 us -> 0.02 us
    ppermute x3, starting transfers between devices: 10.9 us -> 12.4 us  [shards(): lines.append(lax.ppermute(far, 'z_lo', route))]
where the time goes in v8:
time: 102 us; the launch traced here: 101 us
  blocking collectives  45.5 us (45%)
  starting transfers between devices  41.3 us (40%)
  Pallas kernels  9.09 us (9%)
  waiting for transfers between devices  3.45 us (3%)
  between operations  2.01 us (2%)
    all_to_all x1, starting transfers between devices, exchange(): lax.all_to_all(rows.reshape(shape), axis, 0, 0, tiled=True)  28.9 us
    all_to_all x1, blocking collectives, exchange(): lax.all_to_all(rows.reshape(shape), axis, 0, 0, tiled=True)  21.5 us
    all_gather x4, blocking collectives, shards(): plane = lax.all_gather(plane, axis, axis=0, tiled=True)  19.2 us
    ppermute x3, starting transfers between devices, shards(): lines.append(lax.ppermute(far, 'z_lo', route))  12.4 us
    all_gather x1, blocking collectives, shards(): plane = lax.all_gather(plane, PLANE[0], axis=0, tiled=True)  4.82 us
    pallas_call x1, Pallas kernels, shards(): pl.pallas_call(units_kernel, out_shape=(jax.ShapeDtypeStruct((BLOCK, narr...  4.79 us
    all_to_all x1, waiting for transfers between devices, exchange(): lax.all_to_all(rows.reshape(shape), axis, 0, 0, tiled=True)  3.44 us
    pallas_call x1, Pallas kernels, shards(): pl.pallas_call(lambda *refs: tile_kernel(count, *refs), out_shape=jax.Sha...  2.53 us
  transfers between devices with their start and end apart: 4, of which 1 were waited for; matrix products, arithmetic and copies ran while one was open for 0% of the time, Pallas kernels for 0%

profile of v8, /device:TPU:1, one launch (start us, length us, event | category | flops | bytes accessed | tf_op | source)
XLA Modules:
  0.0 101.4 jit_solution(12178703089131374995)
XLA Ops:
  0.6 4.8 %units.1 = (bf16[8,896]{1,0:T(8,128)(2,1)}, bf16[64,896]{1,0:T(8,128)(2,1)}, f32[8,1152]{1,0:T(8,128)}) custom-call(s32[1,3]{1,0:T(1,128)} %lengths_at.1, bf16[384,1536]{1,0:T(8,128)(2,1)} %keys_at.1, bf16[384,1536]{1,0:T(8,128)(2,1)} %values_at.1, bf16[1536]{0:T(1024)(128)(2,1)} %probe.1, bf16[1536,1152]{1,0:T(8,128)(2,1)} %projection.1, bf16[3,1152]{1,0:T(4,128)(2,1)} %text.1), custom_call_target="tpu_custom_call" | custom-call | tf_op jit(solution)/shard_map/units/pallas_call | solution.py:272
  5.4 0.0 copy-start.3
  5.4 28.9 %all-to-all-start = ((bf16[8,8,896]{2,1,0:T(8,128)(2,1)}), bf16[8,8,896]{2,1,0:T(8,128)(2,1)}, u32[]{:S(2)}, u32[]{:S(2)}) async-start(bf16[8,8,896]{2,1,0:T(8,128)(2,1)} %bitcast.8), calls=%async_computation | async-start | bytes 229376 | tf_op jit(solution)/shard_map/all_to_all | solution.py:253
  35.6 3.5 %all_gather.15 = bf16[16,896]{1,0:T(8,128)(2,1)S(1)} all-gather(bf16[8,896]{1,0:T(8,128)(2,1)} %get-tuple-element.8), channel_id=1, replica_groups=mesh['y_hi'=2,'x_hi'=2,'x_lo'=2,'core'=2,'z_hi'=8,'z_lo'=4,'y_lo'=2] {'x..., dimensions={0}, use_global_device_ids=true | all-gather | bytes 43008 | tf_op jit(solution)/shard_map/all_gather | solution.py:298
  39.1 0.0 copy-start
  39.1 3.9 %all_gather.16 = bf16[32,896]{1,0:T(8,128)(2,1)S(1)} all-gather(bf16[16,896]{1,0:T(8,128)(2,1)S(1)} %all_gather.15), channel_id=1, replica_groups=mesh['y_hi'=2,'x_hi'=2,'x_lo'=2,'core'=2,'z_hi'=8,'z_lo'=4,'y_lo'=2] {'y..., dimensions={0}, use_global_device_ids=true | all-gather | bytes 86016 | tf_op jit(solution)/shard_map/all_gather | solution.py:298
  43.0 5.6 %all_gather.17 = bf16[64,896]{1,0:T(8,128)(2,1)S(1)} all-gather(bf16[32,896]{1,0:T(8,128)(2,1)S(1)} %all_gather.16), channel_id=1, replica_groups=mesh['y_hi'=2,'x_hi'=2,'x_lo'=2,'core'=2,'z_hi'=8,'z_lo'=4,'y_lo'=2] {'x..., dimensions={0}, use_global_device_ids=true | all-gather | bytes 172032 | tf_op jit(solution)/shard_map/all_gather | solution.py:298
  48.6 6.2 %all_gather.18 = bf16[128,896]{1,0:T(8,128)(2,1)} all-gather(bf16[64,896]{1,0:T(8,128)(2,1)S(1)} %all_gather.17), channel_id=1, replica_groups=mesh['y_hi'=2,'x_hi'=2,'x_lo'=2,'core'=2,'z_hi'=8,'z_lo'=4,'y_lo'=2] {'y..., dimensions={0}, use_global_device_ids=true | all-gather | bytes 344064 | tf_op jit(solution)/shard_map/all_gather | solution.py:298
  54.9 3.4 %all-to-all-done = bf16[8,8,896]{2,1,0:T(8,128)(2,1)} async-done(((bf16[8,8,896]{2,1,0:T(8,128)(2,1)}), bf16[8,8,896]{2,1,0:T(8,128)(2,1)}, u32[]{:S(2)}, u32[]{:S(2)}) %all-to-all-start) | async-done | bytes 114720 | tf_op jit(solution)/shard_map/all_to_all | solution.py:253
  58.3 3.6 %collective-permute-start.2 = (bf16[64,896]{1,0:T(8,128)(2,1)}, bf16[64,896]{1,0:T(8,128)(2,1)S(1)}, u32[]{:S(2)}, u32[]{:S(2)}) collective-permute-start(bf16[64,896]{1,0:T(8,128)(2,1)} %bitcast.1.refs_1_), channel_id=1, source_target_pairs={{0,6},{2,0},{4,2},{6,4},{1,7},{3,1},{5,3},{7,5},{8,14},{10,8},{12,... | collective-permute-start | bytes 344072 | tf_op jit(solution)/shard_map/ppermute | solution.py:305
  61.9 5.9 %collective-permute-start.1 = (bf16[64,896]{1,0:T(8,128)(2,1)}, bf16[64,896]{1,0:T(8,128)(2,1)S(1)}, u32[]{:S(2)}, u32[]{:S(2)}) collective-permute-start(bf16[64,896]{1,0:T(8,128)(2,1)} %bitcast.1.refs_1_), channel_id=1, source_target_pairs={{0,4},{2,6},{4,0},{6,2},{1,5},{3,7},{5,1},{7,3},{8,12},{10,14},{12... | collective-permute-start | bytes 344072 | tf_op jit(solution)/shard_map/ppermute | solution.py:305
  67.8 2.9 %collective-permute-start = (bf16[64,896]{1,0:T(8,128)(2,1)}, bf16[64,896]{1,0:T(8,128)(2,1)S(1)}, u32[]{:S(2)}, u32[]{:S(2)}) collective-permute-start(bf16[64,896]{1,0:T(8,128)(2,1)} %bitcast.1.refs_1_), channel_id=1, source_target_pairs={{0,2},{2,4},{4,6},{6,0},{1,3},{3,5},{5,7},{7,1},{8,10},{10,12},{12... | collective-permute-start | bytes 344072 | tf_op jit(solution)/shard_map/ppermute | solution.py:305
  70.8 4.8 %all_gather.19.refs_0_ = bf16[256,896]{1,0:T(8,128)(2,1)S(1)} all-gather(bf16[128,896]{1,0:T(8,128)(2,1)} %all_gather.18), channel_id=1, replica_groups=mesh['y_hi'=2,'x_hi'=2,'x_lo'=2,'core'=2,'z_hi'=8,'z_lo'=4,'y_lo'=2] {'c..., dimensions={0}, use_global_device_ids=true | all-gather | bytes 688128 | tf_op jit(solution)/shard_map/all_gather | solution.py:300
  75.6 0.0 copy-start.1
  75.6 0.0 copy-start.2
  75.6 0.0 collective-permute-done.2.refs_4_
  75.6 0.0 collective-permute-done.1.refs_3_
  75.6 0.0 collective-permute-done.refs_2_
  75.6 0.0 copy-done.3
  75.6 2.5 %tile.1 = bf16[256,896]{1,0:T(8,128)(2,1)S(1)} custom-call(bf16[256,896]{1,0:T(8,128)(2,1)S(1)} %all_gather.19.refs_0_, bf16[64,896]{1,0:T(8,128)(2,1)} %bitcast.1.refs_1_, bf16[64,896]{1,0:T(8,128)(2,1)S(1)} %collective-permute-done.refs_2_, bf16[64,896]{1,0:T(8,128)(2,1)S(1)} %collective-permute-done.1.refs_3_, ...), custom_call_target="tpu_custom_call" | custom-call | tf_op jit(solution)/shard_map/tile/pallas_call | solution.py:306
  78.2 21.5 %all_to_all.10 = bf16[32,8,896]{2,1,0:T(8,128)(2,1)S(1)} all-to-all(bf16[32,8,896]{2,1,0:T(8,128)(2,1)S(1)} %bitcast.5), channel_id=1, replica_groups=mesh['y_hi'=2,'x_hi'=2,'x_lo'=2,'core'=2,'z_hi'=8,'z_lo'=4,'y_lo'=2] {'c..., dimensions={0} | all-to-all | bytes 917504 | tf_op jit(solution)/shard_map/all_to_all | solution.py:253
  99.6 0.0 copy-done
  99.6 0.0 copy-done.1
  99.6 0.0 copy-done.2
  99.6 1.8 %grads.1 = (f32[3,1536]{1,0:T(4,128)}, f32[3,1152]{1,0:T(4,128)}) custom-call(bf16[256,896]{1,0:T(8,128)(2,1)S(1)} %bitcast.6, f32[8,1152]{1,0:T(8,128)S(1)} %copy-done.1, bf16[1536,1152]{1,0:T(8,128)(2,1)S(1)} %copy-done, bf16[3,1152]{1,0:T(4,128)(2,1)S(1)} %copy-done.2), custom_call_target="tpu_custom_call" | custom-call | tf_op jit(solution)/shard_map/grads/pallas_call | solution.py:321
Async XLA Ops:
  5.4 70.2 %copy-start.3 = (s32[3072]{0:T(1024)S(1)}, s32[3072]{0:T(1024)}, u32[]{:S(2)}) copy-start(s32[3072]{0:T(1024)} %param.15) | copy-start | bytes 36868
  5.4 52.9 %all-to-all-start = ((bf16[8,8,896]{2,1,0:T(8,128)(2,1)}), bf16[8,8,896]{2,1,0:T(8,128)(2,1)}, u32[]{:S(2)}, u32[]{:S(2)}) async-start(bf16[8,8,896]{2,1,0:T(8,128)(2,1)} %bitcast.8), calls=%async_computation | async-start | bytes 229376 | tf_op jit(solution)/shard_map/all_to_all | solution.py:253
  39.1 60.5 %copy-start = (bf16[1536,1152]{1,0:T(8,128)(2,1)S(1)}, bf16[1536,1152]{1,0:T(8,128)(2,1)}, u32[]{:S(2)}) copy-start(bf16[1536,1152]{1,0:T(8,128)(2,1)} %projection.1) | copy-start | bytes 10616836
  58.3 17.3 %collective-permute-start.2 = (bf16[64,896]{1,0:T(8,128)(2,1)}, bf16[64,896]{1,0:T(8,128)(2,1)S(1)}, u32[]{:S(2)}, u32[]{:S(2)}) collective-permute-start(bf16[64,896]{1,0:T(8,128)(2,1)} %bitcast.1.refs_1_), channel_id=1, source_target_pairs={{0,6},{2,0},{4,2},{6,4},{1,7},{3,1},{5,3},{7,5},{8,14},{10,8},{12,... | collective-permute-start | bytes 344072 | tf_op jit(solution)/shard_map/ppermute | solution.py:305
  61.9 13.7 %collective-permute-start.1 = (bf16[64,896]{1,0:T(8,128)(2,1)}, bf16[64,896]{1,0:T(8,128)(2,1)S(1)}, u32[]{:S(2)}, u32[]{:S(2)}) collective-permute-start(bf16[64,896]{1,0:T(8,128)(2,1)} %bitcast.1.refs_1_), channel_id=1, source_target_pairs={{0,4},{2,6},{4,0},{6,2},{1,5},{3,7},{5,1},{7,3},{8,12},{10,14},{12... | collective-permute-start | bytes 344072 | tf_op jit(solution)/shard_map/ppermute | solution.py:305
  67.8 7.8 %collective-permute-start = (bf16[64,896]{1,0:T(8,128)(2,1)}, bf16[64,896]{1,0:T(8,128)(2,1)S(1)}, u32[]{:S(2)}, u32[]{:S(2)}) collective-permute-start(bf16[64,896]{1,0:T(8,128)(2,1)} %bitcast.1.refs_1_), channel_id=1, source_target_pairs={{0,2},{2,4},{4,6},{6,0},{1,3},{3,5},{5,7},{7,1},{8,10},{10,12},{12... | collective-permute-start | bytes 344072 | tf_op jit(solution)/shard_map/ppermute | solution.py:305
  75.6 24.1 %copy-start.1 = (f32[8,1152]{1,0:T(8,128)S(1)}, f32[8,1152]{1,0:T(8,128)}, u32[]{:S(2)}) copy-start(f32[8,1152]{1,0:T(8,128)} %get-tuple-element.11.projected) | copy-start | bytes 110596
  75.6 24.1 %copy-start.2 = (bf16[3,1152]{1,0:T(4,128)(2,1)S(1)}, bf16[3,1152]{1,0:T(4,128)(2,1)}, u32[]{:S(2)}) copy-start(bf16[3,1152]{1,0:T(4,128)(2,1)} %text.1) | copy-start | bytes 20740

commit v9 on v8

--- a/solution.py
+++ b/solution.py
@@ -11,7 +11,7 @@
 HD = 96
 
 AXES = ("y_hi", "x_hi", "x_lo", "core", "z_hi", "z_lo", "y_lo")
-SIZES = (2, 2, 2, 2, 8, 4, 2)
+SIZES = (2, 2, 2, 2, 16, 2, 2)
 PLANE = ("core", "y_hi", "x_hi", "y_lo", "x_lo")
 
 BLOCK = 8

time: 102 us -> 99.5 us (0.975); the launches traced: 101 us -> 97.8 us
  starting transfers between devices: 41.3 us -> 36.6 us
  waiting for transfers between devices: 3.45 us -> 5.61 us
  blocking collectives: 45.5 us -> 44.4 us
    ppermute x3 -> x1, starting transfers between devices: 12.4 us -> 7.5 us  [shards(): lines.append(lax.ppermute(far, 'z_lo', route))]
    all_to_all x1, blocking collectives: 21.5 us -> 18.8 us  [exchange(): lax.all_to_all(rows.reshape(shape), axis, 0, 0, tiled=True)]
    all_to_all x1, waiting for transfers between devices: 3.44 us -> 5.61 us  [exchange(): lax.all_to_all(rows.reshape(shape), axis, 0, 0, tiled=True)]
    all_gather x1, blocking collectives: 4.82 us -> 6.8 us  [shards(): plane = lax.all_gather(plane, PLANE[0], axis=0, tiled=True)]
  transfers between devices with their start and end apart: 4 -> 2, of which waited for: 1 -> 1; matrix products, arithmetic and copies ran while one was open for 0% -> 0% of each run, Pallas kernels for 0% -> 0%
where the time goes in v9:
time: 99.5 us; the launch traced here: 97.8 us
  blocking collectives  44.4 us (45%)
  starting transfers between devices  36.6 us (37%)
  Pallas kernels  9.2 us (9%)
  waiting for transfers between devices  5.61 us (6%)
  between operations  1.99 us (2%)
    all_to_all x1, starting transfers between devices, exchange(): lax.all_to_all(rows.reshape(shape), axis, 0, 0, tiled=True)  29.1 us
    all_gather x4, blocking collectives, shards(): plane = lax.all_gather(plane, axis, axis=0, tiled=True)  18.8 us
    all_to_all x1, blocking collectives, exchange(): lax.all_to_all(rows.reshape(shape), axis, 0, 0, tiled=True)  18.8 us
    ppermute x1, starting transfers between devices, shards(): lines.append(lax.ppermute(far, 'z_lo', route))  7.5 us
    all_gather x1, blocking collectives, shards(): plane = lax.all_gather(plane, PLANE[0], axis=0, tiled=True)  6.8 us
    all_to_all x1, waiting for transfers between devices, exchange(): lax.all_to_all(rows.reshape(shape), axis, 0, 0, tiled=True)  5.61 us
    pallas_call x1, Pallas kernels, shards(): pl.pallas_call(units_kernel, out_shape=(jax.ShapeDtypeStruct((BLOCK, narr...  4.84 us
    pallas_call x1, Pallas kernels, shards(): pl.pallas_call(lambda *refs: tile_kernel(count, *refs), out_shape=jax.Sha...  2.59 us
  transfers between devices with their start and end apart: 2, of which 1 were waited for; matrix products, arithmetic and copies ran while one was open for 0% of the time, Pallas kernels for 0%

profile of v9, /device:TPU:1, one launch (start us, length us, event | category | flops | bytes accessed | tf_op | source)
XLA Modules:
  0.0 97.8 jit_solution(9770817145869415916)
XLA Ops:
  0.6 4.8 %units.1 = (bf16[8,896]{1,0:T(8,128)(2,1)}, bf16[128,896]{1,0:T(8,128)(2,1)}, f32[8,1152]{1,0:T(8,128)}) custom-call(s32[1,3]{1,0:T(1,128)} %lengths_at.1, bf16[384,1536]{1,0:T(8,128)(2,1)} %keys_at.1, bf16[384,1536]{1,0:T(8,128)(2,1)} %values_at.1, bf16[1536]{0:T(1024)(128)(2,1)} %probe.1, bf16[1536,1152]{1,0:T(8,128)(2,1)} %projection.1, bf16[3,1152]{1,0:T(4,128)(2,1)} %text.1), custom_call_target="tpu_custom_call" | custom-call | tf_op jit(solution)/shard_map/units/pallas_call | solution.py:272
  5.5 0.0 copy-start.3
  5.5 29.1 %all-to-all-start = ((bf16[16,8,896]{2,1,0:T(8,128)(2,1)}), bf16[16,8,896]{2,1,0:T(8,128)(2,1)}, u32[]{:S(2)}, u32[]{:S(2)}) async-start(bf16[16,8,896]{2,1,0:T(8,128)(2,1)} %bitcast.8), calls=%async_computation | async-start | bytes 458752 | tf_op jit(solution)/shard_map/all_to_all | solution.py:253
  34.6 0.0 copy-start
  34.6 3.6 %all_gather.15 = bf16[16,896]{1,0:T(8,128)(2,1)S(1)} all-gather(bf16[8,896]{1,0:T(8,128)(2,1)} %get-tuple-element.8), channel_id=1, replica_groups=mesh['y_hi'=2,'x_hi'=2,'x_lo'=2,'core'=2,'z_hi'=16,'z_lo'=2,'y_lo'=2] {'..., dimensions={0}, use_global_device_ids=true | all-gather | bytes 43008 | tf_op jit(solution)/shard_map/all_gather | solution.py:298
  38.2 3.4 %all_gather.16 = bf16[32,896]{1,0:T(8,128)(2,1)S(1)} all-gather(bf16[16,896]{1,0:T(8,128)(2,1)S(1)} %all_gather.15), channel_id=1, replica_groups=mesh['y_hi'=2,'x_hi'=2,'x_lo'=2,'core'=2,'z_hi'=16,'z_lo'=2,'y_lo'=2] {'..., dimensions={0}, use_global_device_ids=true | all-gather | bytes 86016 | tf_op jit(solution)/shard_map/all_gather | solution.py:298
  41.6 5.6 %all_gather.17 = bf16[64,896]{1,0:T(8,128)(2,1)S(1)} all-gather(bf16[32,896]{1,0:T(8,128)(2,1)S(1)} %all_gather.16), channel_id=1, replica_groups=mesh['y_hi'=2,'x_hi'=2,'x_lo'=2,'core'=2,'z_hi'=16,'z_lo'=2,'y_lo'=2] {'..., dimensions={0}, use_global_device_ids=true | all-gather | bytes 172032 | tf_op jit(solution)/shard_map/all_gather | solution.py:298
  47.2 6.2 %all_gather.18 = bf16[128,896]{1,0:T(8,128)(2,1)} all-gather(bf16[64,896]{1,0:T(8,128)(2,1)S(1)} %all_gather.17), channel_id=1, replica_groups=mesh['y_hi'=2,'x_hi'=2,'x_lo'=2,'core'=2,'z_hi'=16,'z_lo'=2,'y_lo'=2] {'..., dimensions={0}, use_global_device_ids=true | all-gather | bytes 344064 | tf_op jit(solution)/shard_map/all_gather | solution.py:298
  53.4 5.6 %all-to-all-done = bf16[16,8,896]{2,1,0:T(8,128)(2,1)} async-done(((bf16[16,8,896]{2,1,0:T(8,128)(2,1)}), bf16[16,8,896]{2,1,0:T(8,128)(2,1)}, u32[]{:S(2)}, u32[]{:S(2)}) %all-to-all-start) | async-done | bytes 229408 | tf_op jit(solution)/shard_map/all_to_all | solution.py:253
  59.0 7.5 %collective-permute-start = (bf16[128,896]{1,0:T(8,128)(2,1)}, bf16[128,896]{1,0:T(8,128)(2,1)S(1)}, u32[]{:S(2)}, u32[]{:S(2)}) collective-permute-start(bf16[128,896]{1,0:T(8,128)(2,1)} %bitcast.1.refs_1_), channel_id=1, source_target_pairs={{0,2},{2,0},{1,3},{3,1},{4,6},{6,4},{5,7},{7,5},{8,10},{10,8},{9,1... | collective-permute-start | bytes 688136 | tf_op jit(solution)/shard_map/ppermute | solution.py:305
  67.8 6.8 %all_gather.19.refs_0_ = bf16[256,896]{1,0:T(8,128)(2,1)S(1)} all-gather(bf16[128,896]{1,0:T(8,128)(2,1)} %all_gather.18), channel_id=1, replica_groups=mesh['y_hi'=2,'x_hi'=2,'x_lo'=2,'core'=2,'z_hi'=16,'z_lo'=2,'y_lo'=2] {'..., dimensions={0}, use_global_device_ids=true | all-gather | bytes 688128 | tf_op jit(solution)/shard_map/all_gather | solution.py:300
  74.6 0.0 copy-start.1
  74.6 0.0 copy-start.2
  74.6 0.0 collective-permute-done.refs_2_
  74.6 0.0 copy-done.3
  74.6 2.6 %tile.1 = bf16[256,896]{1,0:T(8,128)(2,1)S(1)} custom-call(bf16[256,896]{1,0:T(8,128)(2,1)S(1)} %all_gather.19.refs_0_, bf16[128,896]{1,0:T(8,128)(2,1)} %bitcast.1.refs_1_, bf16[128,896]{1,0:T(8,128)(2,1)S(1)} %collective-permute-done.refs_2_, s32[24,128]{1,0:T(8,128)S(1)} %bitcast.7, f32[1]{0:T(128)S(6)} %copy.11.refs_4_, f32[1]{0:T(128)S(6)} %copy.12.refs_5_), custom_call_target="tpu_custom_call" | custom-call | tf_op jit(solution)/shard_map/tile/pallas_call | solution.py:306
  77.2 18.8 %all_to_all.10 = bf16[32,8,896]{2,1,0:T(8,128)(2,1)S(1)} all-to-all(bf16[32,8,896]{2,1,0:T(8,128)(2,1)S(1)} %bitcast.5), channel_id=1, replica_groups=mesh['y_hi'=2,'x_hi'=2,'x_lo'=2,'core'=2,'z_hi'=16,'z_lo'=2,'y_lo'=2] {'..., dimensions={0} | all-to-all | bytes 917504 | tf_op jit(solution)/shard_map/all_to_all | solution.py:253
  96.0 0.0 copy-done
  96.0 0.0 copy-done.1
  96.0 0.0 copy-done.2
  96.0 1.8 %grads.1 = (f32[3,1536]{1,0:T(4,128)}, f32[3,1152]{1,0:T(4,128)}) custom-call(bf16[256,896]{1,0:T(8,128)(2,1)S(1)} %bitcast.6, f32[8,1152]{1,0:T(8,128)S(1)} %copy-done.1, bf16[1536,1152]{1,0:T(8,128)(2,1)S(1)} %copy-done, bf16[3,1152]{1,0:T(4,128)(2,1)S(1)} %copy-done.2), custom_call_target="tpu_custom_call" | custom-call | tf_op jit(solution)/shard_map/grads/pallas_call | solution.py:321
Async XLA Ops:
  5.5 69.1 %copy-start.3 = (s32[3072]{0:T(1024)S(1)}, s32[3072]{0:T(1024)}, u32[]{:S(2)}) copy-start(s32[3072]{0:T(1024)} %param.15) | copy-start | bytes 36868
  5.5 53.5 %all-to-all-start = ((bf16[16,8,896]{2,1,0:T(8,128)(2,1)}), bf16[16,8,896]{2,1,0:T(8,128)(2,1)}, u32[]{:S(2)}, u32[]{:S(2)}) async-start(bf16[16,8,896]{2,1,0:T(8,128)(2,1)} %bitcast.8), calls=%async_computation | async-start | bytes 458752 | tf_op jit(solution)/shard_map/all_to_all | solution.py:253
  34.6 61.4 %copy-start = (bf16[1536,1152]{1,0:T(8,128)(2,1)S(1)}, bf16[1536,1152]{1,0:T(8,128)(2,1)}, u32[]{:S(2)}) copy-start(bf16[1536,1152]{1,0:T(8,128)(2,1)} %projection.1) | copy-start | bytes 10616836
  59.0 15.6 %collective-permute-start = (bf16[128,896]{1,0:T(8,128)(2,1)}, bf16[128,896]{1,0:T(8,128)(2,1)S(1)}, u32[]{:S(2)}, u32[]{:S(2)}) collective-permute-start(bf16[128,896]{1,0:T(8,128)(2,1)} %bitcast.1.refs_1_), channel_id=1, source_target_pairs={{0,2},{2,0},{1,3},{3,1},{4,6},{6,4},{5,7},{7,5},{8,10},{10,8},{9,1... | collective-permute-start | bytes 688136 | tf_op jit(solution)/shard_map/ppermute | solution.py:305
  74.6 21.4 %copy-start.1 = (f32[8,1152]{1,0:T(8,128)S(1)}, f32[8,1152]{1,0:T(8,128)}, u32[]{:S(2)}) copy-start(f32[8,1152]{1,0:T(8,128)} %get-tuple-element.11.projected) | copy-start | bytes 110596
  74.6 21.4 %copy-start.2 = (bf16[3,1152]{1,0:T(4,128)(2,1)S(1)}, bf16[3,1152]{1,0:T(4,128)(2,1)}, u32[]{:S(2)}) copy-start(bf16[3,1152]{1,0:T(4,128)(2,1)} %text.1) | copy-start | bytes 20740

commit v10 on v9

--- a/solution.py
+++ b/solution.py
@@ -77,7 +77,7 @@
     values_at,
     probe,
     projection_at,
-    text_at,
+    text,
     block,
     copies,
     projected,
@@ -85,7 +85,6 @@
     keys,
     values,
     projection,
-    text,
     pooled,
     units,
     arrived,
@@ -98,7 +97,6 @@
                 (lengths_at, lengths),
                 (keys_at, keys),
                 (values_at, values),
-                (text_at, text),
             ]
             + [
                 (projection_at.at[pl.ds(part * deep, deep)], projection.at[pl.ds(part * deep, deep)])
@@ -137,7 +135,7 @@
         pooled[image : image + 1, :] = jnp.sum(jnp.where(own, part, 0.0), axis=0, keepdims=True)
     proj = jnp.zeros((2 * BLOCK, projected.shape[1]), jnp.float32)
     for part in range(PARTS):
-        fetches[4 + part].wait()
+        fetches[3 + part].wait()
         here = slice(part * deep, (part + 1) * deep)
         proj += jnp.dot(
             pooled[:, here].astype(jnp.bfloat16),
@@ -145,7 +143,6 @@
             preferred_element_type=jnp.float32,
         )
     proj = proj[:BLOCK]
-    fetches[3].wait()
     projected[...] = proj
     units[...] = proj / row_norm(proj)
     text_wide = text[...].astype(jnp.float32)
@@ -276,17 +273,16 @@
             jax.ShapeDtypeStruct((n_far * BLOCK, narrow), jnp.bfloat16),
             jax.ShapeDtypeStruct((BLOCK, width), jnp.float32),
         ),
-        in_specs=[HBM] * 3 + [VMEM] + [HBM] * 2,
+        in_specs=[HBM] * 3 + [VMEM, HBM, VMEM],
         out_specs=(VMEM, VMEM, VMEM),
         scratch_shapes=[
             pltpu.SMEM(lengths.shape, lengths.dtype),
             pltpu.VMEM(patch_keys.shape, patch_keys.dtype),
             pltpu.VMEM(patch_values.shape, patch_values.dtype),
             pltpu.VMEM(projection.shape, projection.dtype),
-            pltpu.VMEM(text_embeds.shape, text_embeds.dtype),
             pltpu.VMEM((2 * BLOCK, depth), jnp.float32),
             pltpu.VMEM((BLOCK, width), jnp.float32),
-            pltpu.SemaphoreType.DMA((4 + PARTS,)),
+            pltpu.SemaphoreType.DMA((3 + PARTS,)),
         ],
         compiler_params=pltpu.CompilerParams(vmem_limit_bytes=60 << 20),
         name="units",

time: 99.5 us -> 99.5 us (level)
  no operation moved by 1% of the time
where the time goes in v10:
time: 99.5 us; the launch traced here: 97.8 us
  blocking collectives  44.4 us (45%)
  starting transfers between devices  36.5 us (37%)
  Pallas kernels  9.21 us (9%)
  waiting for transfers between devices  5.62 us (6%)
  between operations  1.99 us (2%)
    all_to_all x1, starting transfers between devices, exchange(): lax.all_to_all(rows.reshape(shape), axis, 0, 0, tiled=True)  29.1 us
    all_gather x4, blocking collectives, shards(): plane = lax.all_gather(plane, axis, axis=0, tiled=True)  18.8 us
    all_to_all x1, blocking collectives, exchange(): lax.all_to_all(rows.reshape(shape), axis, 0, 0, tiled=True)  18.8 us
    ppermute x1, starting transfers between devices, shards(): lines.append(lax.ppermute(far, 'z_lo', route))  7.49 us
    all_gather x1, blocking collectives, shards(): plane = lax.all_gather(plane, PLANE[0], axis=0, tiled=True)  6.81 us
    all_to_all x1, waiting for transfers between devices, exchange(): lax.all_to_all(rows.reshape(shape), axis, 0, 0, tiled=True)  5.61 us
    pallas_call x1, Pallas kernels, shards(): pl.pallas_call(units_kernel, out_shape=(jax.ShapeDtypeStruct((BLOCK, narr...  4.85 us
    pallas_call x1, Pallas kernels, shards(): pl.pallas_call(lambda *refs: tile_kernel(count, *refs), out_shape=jax.Sha...  2.59 us
  transfers between devices with their start and end apart: 2, of which 1 were waited for; matrix products, arithmetic and copies ran while one was open for 0% of the time, Pallas kernels for 0%

profile of v10, /device:TPU:1, one launch (start us, length us, event | category | flops | bytes accessed | tf_op | source)
XLA Modules:
  0.0 97.8 jit_solution(13340245302879458348)
XLA Ops:
  0.6 4.9 %units.1 = (bf16[8,896]{1,0:T(8,128)(2,1)}, bf16[128,896]{1,0:T(8,128)(2,1)}, f32[8,1152]{1,0:T(8,128)}) custom-call(s32[1,3]{1,0:T(1,128)} %lengths_at.1, bf16[384,1536]{1,0:T(8,128)(2,1)} %keys_at.1, bf16[384,1536]{1,0:T(8,128)(2,1)} %values_at.1, bf16[1536]{0:T(1024)(128)(2,1)} %probe.1, bf16[1536,1152]{1,0:T(8,128)(2,1)} %projection.1, bf16[3,1152]{1,0:T(4,128)(2,1)} %text.3), custom_call_target="tpu_custom_call" | custom-call | tf_op jit(solution)/shard_map/units/pallas_call | solution.py:269
  5.5 0.0 copy-start.3
  5.5 29.1 %all-to-all-start = ((bf16[16,8,896]{2,1,0:T(8,128)(2,1)}), bf16[16,8,896]{2,1,0:T(8,128)(2,1)}, u32[]{:S(2)}, u32[]{:S(2)}) async-start(bf16[16,8,896]{2,1,0:T(8,128)(2,1)} %bitcast.8), calls=%async_computation | async-start | bytes 458752 | tf_op jit(solution)/shard_map/all_to_all | solution.py:250
  34.6 0.0 copy-start
  34.6 3.6 %all_gather.15 = bf16[16,896]{1,0:T(8,128)(2,1)S(1)} all-gather(bf16[8,896]{1,0:T(8,128)(2,1)} %get-tuple-element.8), channel_id=1, replica_groups=mesh['y_hi'=2,'x_hi'=2,'x_lo'=2,'core'=2,'z_hi'=16,'z_lo'=2,'y_lo'=2] {'..., dimensions={0}, use_global_device_ids=true | all-gather | bytes 43008 | tf_op jit(solution)/shard_map/all_gather | solution.py:294
  38.2 3.4 %all_gather.16 = bf16[32,896]{1,0:T(8,128)(2,1)S(1)} all-gather(bf16[16,896]{1,0:T(8,128)(2,1)S(1)} %all_gather.15), channel_id=1, replica_groups=mesh['y_hi'=2,'x_hi'=2,'x_lo'=2,'core'=2,'z_hi'=16,'z_lo'=2,'y_lo'=2] {'..., dimensions={0}, use_global_device_ids=true | all-gather | bytes 86016 | tf_op jit(solution)/shard_map/all_gather | solution.py:294
  41.6 5.6 %all_gather.17 = bf16[64,896]{1,0:T(8,128)(2,1)S(1)} all-gather(bf16[32,896]{1,0:T(8,128)(2,1)S(1)} %all_gather.16), channel_id=1, replica_groups=mesh['y_hi'=2,'x_hi'=2,'x_lo'=2,'core'=2,'z_hi'=16,'z_lo'=2,'y_lo'=2] {'..., dimensions={0}, use_global_device_ids=true | all-gather | bytes 172032 | tf_op jit(solution)/shard_map/all_gather | solution.py:294
  47.2 6.2 %all_gather.18 = bf16[128,896]{1,0:T(8,128)(2,1)} all-gather(bf16[64,896]{1,0:T(8,128)(2,1)S(1)} %all_gather.17), channel_id=1, replica_groups=mesh['y_hi'=2,'x_hi'=2,'x_lo'=2,'core'=2,'z_hi'=16,'z_lo'=2,'y_lo'=2] {'..., dimensions={0}, use_global_device_ids=true | all-gather | bytes 344064 | tf_op jit(solution)/shard_map/all_gather | solution.py:294
  53.4 5.6 %all-to-all-done = bf16[16,8,896]{2,1,0:T(8,128)(2,1)} async-done(((bf16[16,8,896]{2,1,0:T(8,128)(2,1)}), bf16[16,8,896]{2,1,0:T(8,128)(2,1)}, u32[]{:S(2)}, u32[]{:S(2)}) %all-to-all-start) | async-done | bytes 229408 | tf_op jit(solution)/shard_map/all_to_all | solution.py:250
  59.0 7.5 %collective-permute-start = (bf16[128,896]{1,0:T(8,128)(2,1)}, bf16[128,896]{1,0:T(8,128)(2,1)S(1)}, u32[]{:S(2)}, u32[]{:S(2)}) collective-permute-start(bf16[128,896]{1,0:T(8,128)(2,1)} %bitcast.1.refs_1_), channel_id=1, source_target_pairs={{0,2},{2,0},{1,3},{3,1},{4,6},{6,4},{5,7},{7,5},{8,10},{10,8},{9,1... | collective-permute-start | bytes 688136 | tf_op jit(solution)/shard_map/ppermute | solution.py:301
  67.8 6.8 %all_gather.19.refs_0_ = bf16[256,896]{1,0:T(8,128)(2,1)S(1)} all-gather(bf16[128,896]{1,0:T(8,128)(2,1)} %all_gather.18), channel_id=1, replica_groups=mesh['y_hi'=2,'x_hi'=2,'x_lo'=2,'core'=2,'z_hi'=16,'z_lo'=2,'y_lo'=2] {'..., dimensions={0}, use_global_device_ids=true | all-gather | bytes 688128 | tf_op jit(solution)/shard_map/all_gather | solution.py:296
  74.6 0.0 copy-start.1
  74.6 0.0 copy-start.2
  74.6 0.0 collective-permute-done.refs_2_
  74.6 0.0 copy-done.3
  74.6 2.6 %tile.1 = bf16[256,896]{1,0:T(8,128)(2,1)S(1)} custom-call(bf16[256,896]{1,0:T(8,128)(2,1)S(1)} %all_gather.19.refs_0_, bf16[128,896]{1,0:T(8,128)(2,1)} %bitcast.1.refs_1_, bf16[128,896]{1,0:T(8,128)(2,1)S(1)} %collective-permute-done.refs_2_, s32[24,128]{1,0:T(8,128)S(1)} %bitcast.7, f32[1]{0:T(128)S(6)} %copy.11.refs_4_, f32[1]{0:T(128)S(6)} %copy.12.refs_5_), custom_call_target="tpu_custom_call" | custom-call | tf_op jit(solution)/shard_map/tile/pallas_call | solution.py:302
  77.2 18.8 %all_to_all.10 = bf16[32,8,896]{2,1,0:T(8,128)(2,1)S(1)} all-to-all(bf16[32,8,896]{2,1,0:T(8,128)(2,1)S(1)} %bitcast.5), channel_id=1, replica_groups=mesh['y_hi'=2,'x_hi'=2,'x_lo'=2,'core'=2,'z_hi'=16,'z_lo'=2,'y_lo'=2] {'..., dimensions={0} | all-to-all | bytes 917504 | tf_op jit(solution)/shard_map/all_to_all | solution.py:250
  96.0 0.0 copy-done
  96.0 0.0 copy-done.1
  96.0 0.0 copy-done.2
  96.0 1.8 %grads.1 = (f32[3,1536]{1,0:T(4,128)}, f32[3,1152]{1,0:T(4,128)}) custom-call(bf16[256,896]{1,0:T(8,128)(2,1)S(1)} %bitcast.6, f32[8,1152]{1,0:T(8,128)S(1)} %copy-done.1, bf16[1536,1152]{1,0:T(8,128)(2,1)S(1)} %copy-done, bf16[3,1152]{1,0:T(4,128)(2,1)S(1)} %copy-done.2), custom_call_target="tpu_custom_call" | custom-call | tf_op jit(solution)/shard_map/grads/pallas_call | solution.py:317
Async XLA Ops:
  5.5 69.1 %copy-start.3 = (s32[3072]{0:T(1024)S(1)}, s32[3072]{0:T(1024)}, u32[]{:S(2)}) copy-start(s32[3072]{0:T(1024)} %param.15) | copy-start | bytes 36868
  5.5 53.5 %all-to-all-start = ((bf16[16,8,896]{2,1,0:T(8,128)(2,1)}), bf16[16,8,896]{2,1,0:T(8,128)(2,1)}, u32[]{:S(2)}, u32[]{:S(2)}) async-start(bf16[16,8,896]{2,1,0:T(8,128)(2,1)} %bitcast.8), calls=%async_computation | async-start | bytes 458752 | tf_op jit(solution)/shard_map/all_to_all | solution.py:250
  34.6 61.4 %copy-start = (bf16[1536,1152]{1,0:T(8,128)(2,1)S(1)}, bf16[1536,1152]{1,0:T(8,128)(2,1)}, u32[]{:S(2)}) copy-start(bf16[1536,1152]{1,0:T(8,128)(2,1)} %projection.1) | copy-start | bytes 10616836
  59.0 15.6 %collective-permute-start = (bf16[128,896]{1,0:T(8,128)(2,1)}, bf16[128,896]{1,0:T(8,128)(2,1)S(1)}, u32[]{:S(2)}, u32[]{:S(2)}) collective-permute-start(bf16[128,896]{1,0:T(8,128)(2,1)} %bitcast.1.refs_1_), channel_id=1, source_target_pairs={{0,2},{2,0},{1,3},{3,1},{4,6},{6,4},{5,7},{7,5},{8,10},{10,8},{9,1... | collective-permute-start | bytes 688136 | tf_op jit(solution)/shard_map/ppermute | solution.py:301
  74.6 21.4 %copy-start.1 = (f32[8,1152]{1,0:T(8,128)S(1)}, f32[8,1152]{1,0:T(8,128)}, u32[]{:S(2)}) copy-start(f32[8,1152]{1,0:T(8,128)} %get-tuple-element.11.projected) | copy-start | bytes 110596
  74.6 21.4 %copy-start.2 = (bf16[3,1152]{1,0:T(4,128)(2,1)S(1)}, bf16[3,1152]{1,0:T(4,128)(2,1)}, u32[]{:S(2)}) copy-start(bf16[3,1152]{1,0:T(4,128)(2,1)} %text.3) | copy-start | bytes 20740

commit v11 on v10

--- a/solution.py
+++ b/solution.py
@@ -290,10 +290,9 @@
 
     far = exchange(copies, "z_hi")
     plane = block
-    for axis in PLANE[:0:-1]:
+    for axis in PLANE[::-1]:
         plane = lax.all_gather(plane, axis, axis=0, tiled=True)
     far, plane = lax.optimization_barrier((far, plane))
-    plane = lax.all_gather(plane, PLANE[0], axis=0, tiled=True)
     n_near = lax.axis_size("z_lo")
     lines = [far]
     for ahead in range(1, n_near):

time: 99.5 us -> 101 us (1.015)
  blocking collectives: 44.4 us -> 48.7 us
  waiting for transfers between devices: 5.62 us -> 2.31 us
  local copies, waits for them, and re-layouts: 0.02 us -> 1.74 us
    all_gather x1 -> x0, blocking collectives: 6.81 us -> none  [shards(): plane = lax.all_gather(plane, PLANE[0], axis=0, tiled=True)]
    all_gather x4 -> x5, blocking collectives: 18.8 us -> 25.4 us  [shards(): plane = lax.all_gather(plane, axis, axis=0, tiled=True)]
    all_to_all x1, waiting for transfers between devices: 5.61 us -> 0.01 us  [exchange(): lax.all_to_all(rows.reshape(shape), axis, 0, 0, tiled=True)]
    all_to_all x1, blocking collectives: 18.8 us -> 23.3 us  [exchange(): lax.all_to_all(rows.reshape(shape), axis, 0, 0, tiled=True)]
    ppermute x1, waiting for transfers between devices: 0.01 us -> 2.31 us  [shards(): lines.append(lax.ppermute(far, 'z_lo', route))]
    unnamed x8 -> x10, local copies, waits for them, and re-layouts: 0.02 us -> 1.74 us
    ppermute x1, starting transfers between devices: 7.49 us -> 6.46 us  [shards(): lines.append(lax.ppermute(far, 'z_lo', route))]
where the time goes in v11:
time: 101 us; the launch traced here: 99.5 us
  blocking collectives  48.7 us (48%)
  starting transfers between devices  35.5 us (35%)
  Pallas kernels  9.2 us (9%)
  waiting for transfers between devices  2.31 us (2%)
  between operations  1.97 us (2%)
  local copies, waits for them, and re-layouts  1.74 us (2%)
    all_to_all x1, starting transfers between devices, exchange(): lax.all_to_all(rows.reshape(shape), axis, 0, 0, tiled=True)  29.1 us
    all_gather x5, blocking collectives, shards(): plane = lax.all_gather(plane, axis, axis=0, tiled=True)  25.4 us
    all_to_all x1, blocking collectives, exchange(): lax.all_to_all(rows.reshape(shape), axis, 0, 0, tiled=True)  23.3 us
    ppermute x1, starting transfers between devices, shards(): lines.append(lax.ppermute(far, 'z_lo', route))  6.46 us
    pallas_call x1, Pallas kernels, shards(): pl.pallas_call(units_kernel, out_shape=(jax.ShapeDtypeStruct((BLOCK, narr...  4.86 us
    pallas_call x1, Pallas kernels, shards(): pl.pallas_call(lambda *refs: tile_kernel(count, *refs), out_shape=jax.Sha...  2.57 us
    ppermute x1, waiting for transfers between devices, shards(): lines.append(lax.ppermute(far, 'z_lo', route))  2.31 us
  transfers between devices with their start and end apart: 2, of which 1 were waited for; matrix products, arithmetic and copies ran while one was open for 0% of the time, Pallas kernels for 0%

profile of v11, /device:TPU:1, one launch (start us, length us, event | category | flops | bytes accessed | tf_op | source)
XLA Modules:
  0.0 99.5 jit_solution(802974268643114234)
XLA Ops:
  0.6 4.9 %units.1 = (bf16[8,896]{1,0:T(8,128)(2,1)}, bf16[128,896]{1,0:T(8,128)(2,1)}, f32[8,1152]{1,0:T(8,128)}) custom-call(s32[1,3]{1,0:T(1,128)} %lengths_at.1, bf16[384,1536]{1,0:T(8,128)(2,1)} %keys_at.1, bf16[384,1536]{1,0:T(8,128)(2,1)} %values_at.1, bf16[1536]{0:T(1024)(128)(2,1)} %probe.1, bf16[1536,1152]{1,0:T(8,128)(2,1)} %projection.1, bf16[3,1152]{1,0:T(4,128)(2,1)} %text.3), custom_call_target="tpu_custom_call" | custom-call | tf_op jit(solution)/shard_map/units/pallas_call | solution.py:269
  5.5 29.1 %all-to-all-start = ((bf16[16,8,896]{2,1,0:T(8,128)(2,1)}), bf16[16,8,896]{2,1,0:T(8,128)(2,1)}, u32[]{:S(2)}, u32[]{:S(2)}) async-start(bf16[16,8,896]{2,1,0:T(8,128)(2,1)} %bitcast.8), calls=%async_computation | async-start | bytes 458752 | tf_op jit(solution)/shard_map/all_to_all | solution.py:250
  34.6 0.0 copy-start.3
  34.6 3.5 %all_gather.15 = bf16[16,896]{1,0:T(8,128)(2,1)S(1)} all-gather(bf16[8,896]{1,0:T(8,128)(2,1)} %get-tuple-element.8), channel_id=1, replica_groups=mesh['y_hi'=2,'x_hi'=2,'x_lo'=2,'core'=2,'z_hi'=16,'z_lo'=2,'y_lo'=2] {'..., dimensions={0}, use_global_device_ids=true | all-gather | bytes 43008 | tf_op jit(solution)/shard_map/all_gather | solution.py:294
  38.1 0.0 copy-start
  38.1 3.5 %all_gather.16 = bf16[32,896]{1,0:T(8,128)(2,1)S(1)} all-gather(bf16[16,896]{1,0:T(8,128)(2,1)S(1)} %all_gather.15), channel_id=1, replica_groups=mesh['y_hi'=2,'x_hi'=2,'x_lo'=2,'core'=2,'z_hi'=16,'z_lo'=2,'y_lo'=2] {'..., dimensions={0}, use_global_device_ids=true | all-gather | bytes 86016 | tf_op jit(solution)/shard_map/all_gather | solution.py:294
  41.6 5.6 %all_gather.17 = bf16[64,896]{1,0:T(8,128)(2,1)S(1)} all-gather(bf16[32,896]{1,0:T(8,128)(2,1)S(1)} %all_gather.16), channel_id=1, replica_groups=mesh['y_hi'=2,'x_hi'=2,'x_lo'=2,'core'=2,'z_hi'=16,'z_lo'=2,'y_lo'=2] {'..., dimensions={0}, use_global_device_ids=true | all-gather | bytes 172032 | tf_op jit(solution)/shard_map/all_gather | solution.py:294
  47.2 6.2 %all_gather.18 = bf16[128,896]{1,0:T(8,128)(2,1)S(1)} all-gather(bf16[64,896]{1,0:T(8,128)(2,1)S(1)} %all_gather.17), channel_id=1, replica_groups=mesh['y_hi'=2,'x_hi'=2,'x_lo'=2,'core'=2,'z_hi'=16,'z_lo'=2,'y_lo'=2] {'..., dimensions={0}, use_global_device_ids=true | all-gather | bytes 344064 | tf_op jit(solution)/shard_map/all_gather | solution.py:294
  53.4 6.6 %all_gather.19.refs_0_ = bf16[256,896]{1,0:T(8,128)(2,1)} all-gather(bf16[128,896]{1,0:T(8,128)(2,1)S(1)} %all_gather.18), channel_id=1, replica_groups=mesh['y_hi'=2,'x_hi'=2,'x_lo'=2,'core'=2,'z_hi'=16,'z_lo'=2,'y_lo'=2] {'..., dimensions={0}, use_global_device_ids=true | all-gather | bytes 688128 | tf_op jit(solution)/shard_map/all_gather | solution.py:294
  60.0 0.0 all-to-all-done
  60.0 6.5 %collective-permute-start = (bf16[128,896]{1,0:T(8,128)(2,1)}, bf16[128,896]{1,0:T(8,128)(2,1)S(1)}, u32[]{:S(2)}, u32[]{:S(2)}) collective-permute-start(bf16[128,896]{1,0:T(8,128)(2,1)} %bitcast.1.refs_1_), channel_id=1, source_target_pairs={{0,2},{2,0},{1,3},{3,1},{4,6},{6,4},{5,7},{7,5},{8,10},{10,8},{9,1... | collective-permute-start | bytes 688136 | tf_op jit(solution)/shard_map/ppermute | solution.py:300
  67.8 2.3 %collective-permute-done.refs_2_ = bf16[128,896]{1,0:T(8,128)(2,1)S(1)} collective-permute-done((bf16[128,896]{1,0:T(8,128)(2,1)}, bf16[128,896]{1,0:T(8,128)(2,1)S(1)}, u32[]{:S(2)}, u32[]{:S(2)}) %collective-permute-start) | collective-permute-done | bytes 229408 | tf_op jit(solution)/shard_map/ppermute | solution.py:300
  70.1 0.0 copy-start.1
  70.1 1.0 %copy-done.1 = bf16[256,896]{1,0:T(8,128)(2,1)S(1)} copy-done((bf16[256,896]{1,0:T(8,128)(2,1)S(1)}, bf16[256,896]{1,0:T(8,128)(2,1)}, u32[]{:S(2)}) %copy-start.1) | copy-done | bytes 458776
  71.1 0.0 copy-start.4
  71.1 0.7 copy-done.4
  71.8 0.0 copy-start.2
  71.8 2.6 %tile.1 = bf16[256,896]{1,0:T(8,128)(2,1)S(1)} custom-call(bf16[256,896]{1,0:T(8,128)(2,1)S(1)} %copy-done.1, bf16[128,896]{1,0:T(8,128)(2,1)} %bitcast.1.refs_1_, bf16[128,896]{1,0:T(8,128)(2,1)S(1)} %collective-permute-done.refs_2_, s32[24,128]{1,0:T(8,128)S(1)} %bitcast.7, f32[1]{0:T(128)S(6)} %copy.11.refs_4_, f32[1]{0:T(128)S(6)} %copy.12.refs_5_), custom_call_target="tpu_custom_call" | custom-call | tf_op jit(solution)/shard_map/tile/pallas_call | solution.py:301
  74.4 23.3 %all_to_all.10 = bf16[32,8,896]{2,1,0:T(8,128)(2,1)S(1)} all-to-all(bf16[32,8,896]{2,1,0:T(8,128)(2,1)S(1)} %bitcast.5), channel_id=1, replica_groups=mesh['y_hi'=2,'x_hi'=2,'x_lo'=2,'core'=2,'z_hi'=16,'z_lo'=2,'y_lo'=2] {'..., dimensions={0} | all-to-all | bytes 917504 | tf_op jit(solution)/shard_map/all_to_all | solution.py:250
  97.7 0.0 copy-done.3
  97.7 0.0 copy-done
  97.7 0.0 copy-done.2
  97.7 1.8 %grads.1 = (f32[3,1536]{1,0:T(4,128)}, f32[3,1152]{1,0:T(4,128)}) custom-call(bf16[256,896]{1,0:T(8,128)(2,1)S(1)} %bitcast.6, f32[8,1152]{1,0:T(8,128)S(1)} %copy-done.2, bf16[1536,1152]{1,0:T(8,128)(2,1)S(1)} %copy-done, bf16[3,1152]{1,0:T(4,128)(2,1)S(1)} %copy-done.3), custom_call_target="tpu_custom_call" | custom-call | tf_op jit(solution)/shard_map/grads/pallas_call | solution.py:316
Async XLA Ops:
  5.5 54.5 %all-to-all-start = ((bf16[16,8,896]{2,1,0:T(8,128)(2,1)}), bf16[16,8,896]{2,1,0:T(8,128)(2,1)}, u32[]{:S(2)}, u32[]{:S(2)}) async-start(bf16[16,8,896]{2,1,0:T(8,128)(2,1)} %bitcast.8), calls=%async_computation | async-start | bytes 458752 | tf_op jit(solution)/shard_map/all_to_all | solution.py:250
  34.6 63.1 %copy-start.3 = (bf16[3,1152]{1,0:T(4,128)(2,1)S(1)}, bf16[3,1152]{1,0:T(4,128)(2,1)}, u32[]{:S(2)}) copy-start(bf16[3,1152]{1,0:T(4,128)(2,1)} %text.3) | copy-start | bytes 20740
  38.1 59.7 %copy-start = (bf16[1536,1152]{1,0:T(8,128)(2,1)S(1)}, bf16[1536,1152]{1,0:T(8,128)(2,1)}, u32[]{:S(2)}) copy-start(bf16[1536,1152]{1,0:T(8,128)(2,1)} %projection.1) | copy-start | bytes 10616836
  60.0 10.1 %collective-permute-start = (bf16[128,896]{1,0:T(8,128)(2,1)}, bf16[128,896]{1,0:T(8,128)(2,1)S(1)}, u32[]{:S(2)}, u32[]{:S(2)}) collective-permute-start(bf16[128,896]{1,0:T(8,128)(2,1)} %bitcast.1.refs_1_), channel_id=1, source_target_pairs={{0,2},{2,0},{1,3},{3,1},{4,6},{6,4},{5,7},{7,5},{8,10},{10,8},{9,1... | collective-permute-start | bytes 688136 | tf_op jit(solution)/shard_map/ppermute | solution.py:300
  70.1 1.0 %copy-start.1 = (bf16[256,896]{1,0:T(8,128)(2,1)S(1)}, bf16[256,896]{1,0:T(8,128)(2,1)}, u32[]{:S(2)}) copy-start(bf16[256,896]{1,0:T(8,128)(2,1)} %all_gather.19.refs_0_) | copy-start | bytes 1376260
  71.1 0.7 copy-start.4
  71.8 25.9 %copy-start.2 = (f32[8,1152]{1,0:T(8,128)S(1)}, f32[8,1152]{1,0:T(8,128)}, u32[]{:S(2)}) copy-start(f32[8,1152]{1,0:T(8,128)} %get-tuple-element.11.projected) | copy-start | bytes 110596
